TPU v7x, 32 devices: a whole 2x2x4 slice. The times are simulated.
32 devices in a mesh: dp: 4 (over z), expert: 8 (over y, x, core).
Axes of the slice: x: 2, y: 2, z: 4, core: 2. Of those that a mesh axis runs over, the one named last changes fastest.
Arguments:
- inputs: bfloat16 [4096, 2048], P(('dp', 'expert')), may hold values from -6 to 6
- out_grad: bfloat16 [4096, 2048], P(('dp', 'expert')), may hold values from -6 to 6
- combine: float32 [4096, 8], P(('dp', 'expert')), may hold values from 0 to 1, as said below
- routes: int32 [4096, 8], P(('dp', 'expert')), may hold values from 0 to 31, all different within a row; in each aligned block of 128 rows (0 to 127, 128 to 255, ...) at most 48 rows name the same one
- saved_hidden: bfloat16 [4, 32, 8, 48, 768], P('dp', 'expert'), may hold values from -6 to 6
- down_weight: bfloat16 [32, 2048, 768], P('expert'), may hold values from -0.21875 to 0.21875
- router_weight: bfloat16 [32, 2048], replicated, may hold values from -0.125 to 0.125
Outputs:
- hidden_grad: bfloat16 [4, 32, 8, 48, 768], P('dp', 'expert')
- down_grad: bfloat16 [32, 2048, 768], P('expert', 'dp')
- input_grad: bfloat16 [4096, 2048], P(('dp', 'expert'))
- router_grad: float32 [32, 2048], replicated
Inputs may be any that keep to these rules, and one draw needn't show every extreme that they name: `routes`: each token names 8 different experts; among the 128 tokens of one device no expert is named by more than 48 tokens, a bound that some block reaches. `combine`: each token's 8 weights are positive and sum to one.
All inputs are finite; a program needn't handle non-finite values.
Results may differ from a plain program's by a relative error of at most 0.017.
Values may be sent and summed in bfloat16 or wider, within the bound.
No kernel may reach another device: no remote copies, remote signals or barrier semaphores. Data moves between devices by JAX's collectives and lax.ppermute only.
A program may use at most 128 MiB of HBM per device.

v0:
```python
import jax
import jax.numpy as jnp
from jax import lax
from jax.sharding import PartitionSpec as P


def make_marks(block_routes, total_experts):
    return block_routes[:, :, None] == jnp.arange(total_experts, dtype=jnp.int32)[None, None, :]


def slot_positions(route_marks):
    counts = jnp.sum(route_marks.astype(jnp.bfloat16), axis=1)
    token_order = jnp.arange(route_marks.shape[0], dtype=jnp.int32)
    earlier = (token_order[None, :] < token_order[:, None]).astype(jnp.bfloat16)
    before = jnp.dot(earlier, counts, preferred_element_type=jnp.float32)
    picked = jnp.sum(jnp.where(route_marks, before[:, None, :], 0.0), axis=2)
    return picked.astype(jnp.int32)


def pack_rows(scaled, lane_index, owner_slot, positions, local_experts, groups, capacity):
    width = scaled.shape[-1]
    flat_index = (owner_slot * groups + lane_index) * capacity + positions
    zero_rows = jnp.zeros((local_experts * groups * capacity, width), jnp.bfloat16)
    filled = zero_rows.at[flat_index.reshape(-1)].set(scaled.reshape(-1, width))
    return filled.reshape(local_experts, groups, capacity, width)


def local(inputs, out_grad, combine, routes, saved_hidden, down_weight, router_weight):
    token_count, width = out_grad.shape
    local_experts = down_weight.shape[0]
    total_experts = router_weight.shape[0]
    groups = lax.axis_size("expert")
    capacity = saved_hidden.shape[3]
    hidden_width = saved_hidden.shape[4]
    route_marks = make_marks(routes, total_experts)
    positions = slot_positions(route_marks)
    owner_dev = routes // local_experts
    owner_slot = routes % local_experts
    scaled = (combine[:, :, None] * out_grad[:, None, :].astype(jnp.float32)).astype(jnp.bfloat16)
    packed = pack_rows(scaled, owner_dev, owner_slot, positions, local_experts, groups, capacity)
    received = lax.all_to_all(packed, "expert", split_axis=1, concat_axis=1, tiled=True)
    hidden_local = saved_hidden[0]
    products_list = []
    hidden_list = []
    weight_terms = []
    for expert in range(local_experts):
        slot_rows = received[expert].reshape(groups * capacity, width)
        slot_acts = hidden_local[expert].reshape(groups * capacity, hidden_width)
        weight = down_weight[expert]
        recomputed = lax.dot_general(
            slot_acts, weight, (((1,), (1,)), ((), ())), preferred_element_type=jnp.float32
        )
        products_list.append(jnp.sum(recomputed * slot_rows.astype(jnp.float32), axis=1))
        hidden_list.append(
            jnp.dot(slot_rows, weight, preferred_element_type=jnp.float32).astype(jnp.bfloat16)
        )
        weight_terms.append(
            lax.dot_general(
                slot_rows, slot_acts, (((0,), (0,)), ((), ())), preferred_element_type=jnp.float32
            )
        )
    down_grad = lax.psum_scatter(
        jnp.stack(weight_terms).astype(jnp.bfloat16), "dp", scatter_dimension=1, tiled=True
    )
    hidden_grad = jnp.stack(hidden_list).reshape(1, local_experts, groups, capacity, hidden_width)
    slot_products = jnp.stack(products_list).reshape(local_experts, groups, capacity)
    returned = lax.all_to_all(slot_products, "expert", split_axis=1, concat_axis=1, tiled=True)
    pair_index = (owner_slot * groups + owner_dev) * capacity + positions
    pair_sums = returned.reshape(-1)[pair_index]
    logit_grad = pair_sums - combine * jnp.sum(pair_sums, axis=1, keepdims=True)
    dense_grad = jnp.sum(jnp.where(route_marks, logit_grad[:, :, None], 0.0), axis=1).astype(
        jnp.bfloat16
    )
    input_grad = jnp.dot(dense_grad, router_weight, preferred_element_type=jnp.float32).astype(
        jnp.bfloat16
    )
    router_part = lax.dot_general(
        dense_grad, inputs, (((0,), (0,)), ((), ())), preferred_element_type=jnp.float32
    )
    router_grad = lax.psum(router_part, ("dp", "expert"))
    return (hidden_grad, down_grad, input_grad, router_grad)


def solution(mesh):
    placed = (
        P(("dp", "expert"), None),
        P(("dp", "expert"), None),
        P(("dp", "expert"), None),
        P(("dp", "expert"), None),
        P("dp", "expert", None, None, None),
        P("expert", None, None),
        P(),
    )
    return jax.shard_map(
        local,
        mesh=mesh,
        in_specs=placed,
        out_specs=(
            P("dp", "expert", None, None, None),
            P("expert", "dp", None),
            P(("dp", "expert"), None),
            P(),
        ),
        check_vma=False,
    )
```

profile of v0, /device:TPU:0, one launch (start us, length us, event | category | flops | bytes accessed | tf_op | source)
XLA Modules:
  0.0 465.3 jit_solution(12077046493116865724)
XLA Ops:
  12.6 10.6 %scatter_custom_fusion = bf16[1536,2048]{1,0:T(8,128)(2,1)} fusion(s32[1024]{0:T(1024)S(1)} %bitcast.114, f32[128,2048]{1,0:T(8,128)S(1)} %convert_element_type.50, f32[1024]{0:T(1024)S(1)} %mul.48, bf16[]{:T(256)} %constant.31.clone.1), kind=kCustom, calls=%fused_computation.5 | custom fusion | flops 4194304 | bytes 7344130 | tf_op jit(solution)/shard_map/scatter | solution.py:24
  23.2 6.6 %copy.47 = bf16[4,8,48,2048]{3,2,0,1:T(8,128)(2,1)} copy(bf16[4,8,48,2048]{3,2,1,0:T(8,128)(2,1)} %bitcast.88) | data formatting | bytes 12582912 | tf_op jit(solution)/shard_map/reshape | solution.py:25
  29.8 5.3 %all-to-all-start = ((bf16[4,8,48,2048]{3,2,0,1:T(8,128)(2,1)}), bf16[4,8,48,2048]{3,2,0,1:T(8,128)(2,1)}, u32[]{:S(2)}, u32[]{:S(2)}) async-start(bf16[4,8,48,2048]{3,2,0,1:T(8,128)(2,1)} %copy.47), calls=%async_computation | async-start | bytes 12582912 | tf_op jit(solution)/shard_map/all_to_all | solution.py:41
  35.3 1.2 fusion.70
  36.5 70.6 %all-to-all-done = bf16[4,8,48,2048]{3,2,0,1:T(8,128)(2,1)} async-done(((bf16[4,8,48,2048]{3,2,0,1:T(8,128)(2,1)}), bf16[4,8,48,2048]{3,2,0,1:T(8,128)(2,1)}, u32[]{:S(2)}, u32[]{:S(2)}) %all-to-all-start) | async-done | bytes 6291488 | tf_op jit(solution)/shard_map/all_to_all | solution.py:41
  107.1 3.6 fusion.69
  110.7 3.5 fusion.23
  114.3 3.6 multiply_reduce_fusion.2
  117.9 1.5 multiply_reduce_fusion.1
  119.4 3.5 fusion.24
  122.9 1.5 multiply_reduce_fusion.3
  124.4 3.5 fusion.22
  128.0 1.5 multiply_reduce_fusion
  130.6 3.3 all-to-all-start.1
  134.2 4.9 %fusion.25 = bf16[1,2048,768]{2,1,0:T(8,128)(2,1)} fusion(bf16[384,2048]{1,0:T(8,128)(2,1)} %bitcast.99, bf16[384,768]{1,0:T(8,128)(2,1)S(1)} %bitcast.102), kind=kOutput, calls=%fused_computation.36 | convolution fusion | flops 1209532416 | bytes 5308416 | tf_op jit(solution)/shard_map/dot_general | solution.py:58
  140.5 6.2 %gather_fusion = f32[1024]{0:T(1024)S(1)} fusion(f32[1536]{0:T(1024)S(1)} %reshape.84, s32[1024]{0:T(1024)S(1)} %broadcast_clamp_fusion), kind=kCustom, calls=%fused_computation | custom fusion | bytes 12288 | tf_op jit(solution)/shard_map/gather | solution.py:69
  147.9 10.7 %pad_maximum_fusion = bf16[4,2048,768]{2,1,0:T(8,128)(2,1)} fusion(bf16[1,2048,768]{2,1,0:T(8,128)(2,1)} %fusion.25, bf16[1,2048,768]{2,1,0:T(8,128)(2,1)} %fusion.24, bf16[1,2048,768]{2,1,0:T(8,128)(2,1)} %fusion.23, bf16[1,2048,768]{2,1,0:T(8,128)(2,1)} %fusion.22), kind=kLoop, calls=%fused_computation.2 | loop fusion | flops 18874368 | bytes 25165824 | tf_op jit(solution)/shard_map/stack | solution.py:63
  158.7 3.9 fusion.51
  162.6 3.4 fusion.42
  166.1 4.2 fusion.48
  170.3 3.3 fusion.45
  173.6 1.7 pad_maximum_fusion.1
  176.4 279.8 %all-reduce.2.cloned.1.call-done = f32[32,2048]{1,0:T(8,128)} async-done(((f32[32,2048]{1,0:T(8,128)}), f32[32,2048]{1,0:T(8,128)}) %all-reduce.2.cloned.1.call-update) | async-done | bytes 262160 | tf_op jit(solution)/shard_map/psum | solution.py:80
  456.2 1.7 copy.52
  (70 shorter events, 9.9 us)
Async XLA Ops:
  8.0 139.0 %copy-start = (bf16[128,2048]{1,0:T(8,128)(2,1)S(1)}, bf16[128,2048]{1,0:T(8,128)(2,1)}, u32[]{:S(2)}) copy-start(bf16[128,2048]{1,0:T(8,128)(2,1)} %param.7) | copy-start | bytes 1572868
  29.8 5.5 %copy-start.1 = (bf16[1,4,8,48,768]{4,3,2,1,0:T(8,128)(2,1)S(1)}, bf16[1,4,8,48,768]{4,3,2,1,0:T(8,128)(2,1)}, u32[]{:S(2)}) copy-start(bf16[1,4,8,48,768]{4,3,2,1,0:T(8,128)(2,1)} %param.11) | copy-start | bytes 7077892
  29.8 77.3 %all-to-all-start = ((bf16[4,8,48,2048]{3,2,0,1:T(8,128)(2,1)}), bf16[4,8,48,2048]{3,2,0,1:T(8,128)(2,1)}, u32[]{:S(2)}, u32[]{:S(2)}) async-start(bf16[4,8,48,2048]{3,2,0,1:T(8,128)(2,1)} %copy.47), calls=%async_computation | async-start | bytes 12582912 | tf_op jit(solution)/shard_map/all_to_all | solution.py:41
  36.5 74.2 %copy-start.9 = (bf16[1,1,8,48,768]{4,3,2,1,0:T(8,128)(2,1)S(1)}, bf16[1,1,8,48,768]{4,3,2,1,0:T(8,128)(2,1)}, u32[]{:S(2)}) copy-start(bf16[1,1,8,48,768]{4,3,2,1,0:T(8,128)(2,1)} %get-tuple-element.11) | copy-start | bytes 1769476
  107.1 10.7 %slice-start = ((s8[12582912]{0:T(1024)(128)(4,1)}), s8[4194304]{0:T(1024)(128)(4,1)S(1)}, s32[]{:S(2)}) async-start(s8[12582912]{0:T(1024)(128)(4,1)} %bitcast.115), calls=%async_computation.5 | async-start | bytes 8388608
  107.1 10.7 %slice-start.1 = ((s8[12582912]{0:T(1024)(128)(4,1)}), s8[4194304]{0:T(1024)(128)(4,1)S(1)}, s32[]{:S(2)}) async-start(s8[12582912]{0:T(1024)(128)(4,1)} %bitcast.115), calls=%async_computation.6 | async-start | bytes 8388608
  110.7 8.7 %copy-start.2 = (bf16[1,8,48,2048]{3,2,0,1:T(8,128)(2,1)}, bf16[1,8,48,2048]{3,2,0,1:T(8,128)(2,1)S(1)}, u32[]{:S(2)}) copy-start(bf16[1,8,48,2048]{3,2,0,1:T(8,128)(2,1)S(1)} %get-tuple-element.8) | copy-start | bytes 4718596
  110.7 13.7 %copy-start.4 = (bf16[1,8,48,2048]{3,2,0,1:T(8,128)(2,1)}, bf16[1,8,48,2048]{3,2,0,1:T(8,128)(2,1)S(1)}, u32[]{:S(2)}) copy-start(bf16[1,8,48,2048]{3,2,0,1:T(8,128)(2,1)S(1)} %get-tuple-element.6) | copy-start | bytes 4718596
  110.7 17.3 %copy-start.6 = (bf16[1,8,48,2048]{3,2,0,1:T(8,128)(2,1)}, bf16[1,8,48,2048]{3,2,0,1:T(8,128)(2,1)S(1)}, u32[]{:S(2)}) copy-start(bf16[1,8,48,2048]{3,2,0,1:T(8,128)(2,1)S(1)} %get-tuple-element.7) | copy-start | bytes 4718596
  114.2 3.6 copy-start.8
  114.3 3.6 slice-start.2
  119.4 3.5 copy-start.7
  130.6 8.5 %all-to-all-start.1 = ((f32[8,1,192]{2,1,0:T(1,128)}), f32[8,1,192]{2,1,0:T(1,128)S(1)}, u32[]{:S(2)}, u32[]{:S(2)}) async-start(f32[8,1,192]{2,1,0:T(1,128)} %reshape.105), calls=%async_computation.2 | async-start | bytes 16384 | tf_op jit(solution)/shard_map/all_to_all | solution.py:67
  133.9 322.3 %all-reduce.2.cloned.1.call-start = ((), (), s32[]{:S(2)}) async-start(), calls=%async_computation.4 | async-start | bytes 524288 | tf_op jit(solution)/shard_map/psum | solution.py:80
  140.4 6.4 %copy-start.12 = (f32[128,8]{0,1:T(8,128)S(1)}, f32[128,8]{0,1:T(8,128)}, u32[]{:S(2)}) copy-start(f32[128,8]{0,1:T(8,128)} %param.9) | copy-start | bytes 12292
  140.4 6.5 %copy-start.11 = (s32[128,8]{0,1:T(8,128)S(1)}, s32[128,8]{0,1:T(8,128)}, u32[]{:S(2)}) copy-start(s32[128,8]{0,1:T(8,128)} %param.10) | copy-start | bytes 12292
  147.9 308.3 %reduce-scatter.2.cloned.1.call-start = ((), (), s32[]{:S(2)}) async-start(), calls=%async_computation.3 | async-start | bytes 15728640 | tf_op jit(solution)/shard_map/reduce_scatter | solution.py:62
  158.7 3.9 copy-start.5
  162.6 3.5 copy-start.3
  173.6 1.7 copy-start.10
Sparse Core Ops, SparseCore 0:
  148.0 308.1 all-reduce.1
Sparse Core Ops, SparseCore 1:
  158.8 214.6 reduce-scatter.1
where the time goes:
time: 466 us; the launch traced here: 465 us
  waiting for transfers between devices  350 us (75%)
  matrix products  40.6 us (9%)
  other arithmetic  27.2 us (6%)
  local copies, waits for them, and re-layouts  22.4 us (5%)
  between operations  15.8 us (3%)
  starting transfers between devices  8.94 us (2%)
    psum x1, waiting for transfers between devices, local(): router_grad = lax.psum(router_part, ('dp', 'expert'))  280 us
    all_to_all x1, waiting for transfers between devices, local(): lax.all_to_all(packed, 'expert', split_axis=1, concat_axis=1, tiled=True)  70.6 us
    dot_general x4, matrix products, local(): lax.dot_general(slot_rows, slot_acts, (((0,), (0,)), ((), ())), preferred...  15.5 us
    dot_general x4, matrix products, local(): jnp.dot(slot_rows, weight, preferred_element_type=jnp.float32)  14.9 us
    another operation x1, other arithmetic, local(): jnp.stack(weight_terms).astype(jnp.bfloat16)  10.7 us
    scatter x1, other arithmetic, pack_rows(): filled = zero_rows.at[flat_index.reshape(-1)].set(scaled.reshape(-1, width))  10.6 us
  transfers between devices with their start and end apart: 4, of which 2 were waited for; matrix products, arithmetic and copies ran while one was open for 7% of the time, Pallas kernels for 0%

commit v1 on v0

v1 whole, which is shorter than its diff:
```python
import functools

import jax
import jax.numpy as jnp
from jax import lax
from jax.experimental import pallas as pl
from jax.experimental.pallas import tpu as pltpu
from jax.sharding import PartitionSpec as P

F32 = jnp.float32
BF16 = jnp.bfloat16
LANES = 128
KINDS = 4
VMEM_LIMIT = 56 * 1024 * 1024


def make_marks(block_routes, total_experts):
    return block_routes[:, :, None] == jnp.arange(total_experts, dtype=jnp.int32)[None, None, :]


def slot_positions(route_marks):
    counts = jnp.sum(route_marks.astype(BF16), axis=1)
    token_order = jnp.arange(route_marks.shape[0], dtype=jnp.int32)
    earlier = (token_order[None, :] < token_order[:, None]).astype(BF16)
    before = jnp.dot(earlier, counts, preferred_element_type=F32)
    picked = jnp.sum(jnp.where(route_marks, before[:, None, :], 0.0), axis=2)
    return picked.astype(jnp.int32)


def pack_rows(scaled, lane_index, owner_slot, positions, local_experts, groups, capacity):
    width = scaled.shape[-1]
    flat_index = (owner_slot * groups + lane_index) * capacity + positions
    zero_rows = jnp.zeros((local_experts * groups * capacity, width), BF16)
    filled = zero_rows.at[flat_index.reshape(-1)].set(scaled.reshape(-1, width))
    return filled.reshape(local_experts, groups, capacity, width)


def local_any(inputs, out_grad, combine, routes, saved_hidden, down_weight, router_weight):
    token_count, width = out_grad.shape
    local_experts = down_weight.shape[0]
    total_experts = router_weight.shape[0]
    groups = lax.axis_size("expert")
    capacity = saved_hidden.shape[3]
    hidden_width = saved_hidden.shape[4]
    route_marks = make_marks(routes, total_experts)
    positions = slot_positions(route_marks)
    owner_dev = routes // local_experts
    owner_slot = routes % local_experts
    scaled = (combine[:, :, None] * out_grad[:, None, :].astype(F32)).astype(BF16)
    packed = pack_rows(scaled, owner_dev, owner_slot, positions, local_experts, groups, capacity)
    received = lax.all_to_all(packed, "expert", split_axis=1, concat_axis=1, tiled=True)
    hidden_local = saved_hidden[0]
    products_list = []
    hidden_list = []
    weight_terms = []
    for expert in range(local_experts):
        slot_rows = received[expert].reshape(groups * capacity, width)
        slot_acts = hidden_local[expert].reshape(groups * capacity, hidden_width)
        weight = down_weight[expert]
        hidden = jnp.dot(slot_rows, weight, preferred_element_type=F32)
        products_list.append(jnp.sum(hidden * slot_acts.astype(F32), axis=1))
        hidden_list.append(hidden.astype(BF16))
        weight_terms.append(
            lax.dot_general(
                slot_rows, slot_acts, (((0,), (0,)), ((), ())), preferred_element_type=F32
            )
        )
    down_grad = lax.psum_scatter(
        jnp.stack(weight_terms).astype(BF16), "dp", scatter_dimension=1, tiled=True
    )
    hidden_grad = jnp.stack(hidden_list).reshape(1, local_experts, groups, capacity, hidden_width)
    slot_products = jnp.stack(products_list).reshape(local_experts, groups, capacity)
    returned = lax.all_to_all(slot_products, "expert", split_axis=1, concat_axis=1, tiled=True)
    pair_index = (owner_slot * groups + owner_dev) * capacity + positions
    pair_sums = returned.reshape(-1)[pair_index]
    logit_grad = pair_sums - combine * jnp.sum(pair_sums, axis=1, keepdims=True)
    dense_grad = jnp.sum(jnp.where(route_marks, logit_grad[:, :, None], 0.0), axis=1).astype(BF16)
    input_grad = jnp.dot(dense_grad, router_weight, preferred_element_type=F32).astype(BF16)
    router_part = lax.dot_general(
        dense_grad, inputs, (((0,), (0,)), ((), ())), preferred_element_type=F32
    )
    router_grad = lax.psum(router_part, ("dp", "expert"))
    return (hidden_grad, down_grad, input_grad, router_grad)


INNER = [(1, 2), (2, 1)]
FAR = [(0, 2), (3, 1)]
OUTER = [(0, 1), (3, 2)]
OUTWARD = [(1, 0), (2, 3)]


def plane_swap(x, bits):
    return lax.ppermute(x, "expert", [(i, i ^ bits) for i in range(8)])


def plane_gather(x):
    half = x.shape[0] // 2
    across = plane_swap(x, 2)
    along = plane_swap(x, 4)
    diagonal = jnp.concatenate([plane_swap(across[:half], 4), plane_swap(along[half:], 2)])
    same_core = {0: x, 2: across, 4: along, 6: diagonal}
    blocks = dict(same_core)
    for k, block in same_core.items():
        blocks[k + 1] = plane_swap(block, 1)
    return [blocks[k] for k in range(8)]


def dense_routes(routes, combine, total_experts):
    marks = make_marks(routes, total_experts)
    counts = jnp.sum(marks.astype(F32), axis=1)
    token_order = jnp.arange(routes.shape[0], dtype=jnp.int32)
    earlier = (token_order[None, :] < token_order[:, None]).astype(BF16)
    before = jnp.dot(earlier, counts.astype(BF16), preferred_element_type=F32)
    routed = counts > 0.0
    weights = jnp.sum(jnp.where(marks, combine[:, :, None], 0.0), axis=1)
    return routed, jnp.where(routed, before, -1.0), weights


def describe(positions, weights):
    high = lax.reduce_precision(weights, 8, 7)
    middle = lax.reduce_precision(weights - high, 8, 7)
    low = weights - high - middle
    stacked = jnp.concatenate([positions, high, middle, low], axis=1)
    return stacked.T.astype(BF16)


def pick_rows(owner, local_experts, total_experts):
    row = lax.broadcasted_iota(jnp.int32, (KINDS * local_experts, LANES), 0)
    column = lax.broadcasted_iota(jnp.int32, (KINDS * local_experts, LANES), 1)
    wanted = (row // local_experts) * total_experts + owner * local_experts + row % local_experts
    return (column == wanted).astype(BF16)


def place_rows(ref, start, width, picker, local_experts, capacity, step, store):
    notes = jnp.dot(
        picker, ref[:, start + width : start + width + LANES], preferred_element_type=F32
    )
    slots = lax.broadcasted_iota(jnp.int32, (capacity, LANES), 0).astype(F32)
    marks = []
    scales = []
    for expert in range(local_experts):
        weight = (
            notes[local_experts + expert : local_experts + expert + 1]
            + notes[2 * local_experts + expert : 2 * local_experts + expert + 1]
            + notes[3 * local_experts + expert : 3 * local_experts + expert + 1]
        )
        hit = slots == notes[expert : expert + 1]
        marks.append(jnp.where(hit, 1.0, 0.0).astype(BF16))
        scales.append(jnp.sum(jnp.where(hit, weight, 0.0), axis=1, keepdims=True))
    mark = jnp.concatenate(marks, axis=0)
    scale = jnp.concatenate(scales, axis=0)
    for column in range(0, width, step):
        rows = jnp.dot(
            mark,
            ref[:, start + column : start + column + step],
            preferred_element_type=F32,
        )
        rows = (rows * scale).astype(BF16)
        for expert in range(local_experts):
            store(expert, column, step, rows[expert * capacity : (expert + 1) * capacity])


def hidden_kernel(local_experts, total_experts, capacity, width, part, place, *refs):
    blocks = refs[:8]
    weight_ref, acts_ref, hidden_ref, products_ref, near_ref, rows = refs[8:]
    expert = pl.program_id(0)
    me = place[0]

    @pl.when(expert == 0)
    def _():
        picker = pick_rows(me, local_experts, total_experts)
        for k in range(8):
            base = pl.multiple_of((me ^ k) * capacity, 16)

            def store(e, column, step, value, base=base):
                rows[e, pl.ds(base, capacity), column : column + step] = value

            place_rows(blocks[k], 0, width, picker, local_experts, capacity, 512, store)

    hidden = jnp.dot(rows[expert], weight_ref[0], preferred_element_type=F32)
    hidden_ref[0] = hidden.astype(BF16)
    product = hidden * acts_ref[0].astype(F32)
    products_ref[0] = jnp.sum(product.reshape(8, capacity, product.shape[1]), axis=2)
    own = pl.multiple_of(place[1] * part, LANES)
    other = pl.multiple_of(place[2] * part, LANES)
    near_ref[0, :, :part] = rows[expert, :, pl.ds(own, part)]
    near_ref[0, :, part:] = rows[expert, :, pl.ds(other, part)]


def hidden_call(place, blocks, weight, acts, total_experts, capacity, part):
    local_experts, width, hidden_width = weight.shape
    slots = acts.shape[1]
    kernel = functools.partial(
        hidden_kernel, local_experts, total_experts, capacity, width, part
    )
    whole = pl.BlockSpec(blocks[0].shape, lambda e, p: (0, 0))
    return pl.pallas_call(
        kernel,
        grid_spec=pltpu.PrefetchScalarGridSpec(
            num_scalar_prefetch=1,
            grid=(local_experts,),
            in_specs=[whole] * 8
            + [
                pl.BlockSpec((1, width, hidden_width), lambda e, p: (e, 0, 0)),
                pl.BlockSpec((1, slots, hidden_width), lambda e, p: (e, 0, 0)),
            ],
            out_specs=[
                pl.BlockSpec((1, slots, hidden_width), lambda e, p: (e, 0, 0)),
                pl.BlockSpec((1, 8, capacity), lambda e, p: (e, 0, 0)),
                pl.BlockSpec((1, slots, 2 * part), lambda e, p: (e, 0, 0)),
            ],
            scratch_shapes=[pltpu.VMEM((local_experts, slots, width), BF16)],
        ),
        out_shape=[
            jax.ShapeDtypeStruct((local_experts, slots, hidden_width), BF16),
            jax.ShapeDtypeStruct((local_experts, 8, capacity), F32),
            jax.ShapeDtypeStruct((local_experts, slots, 2 * part), BF16),
        ],
        compiler_params=pltpu.CompilerParams(vmem_limit_bytes=VMEM_LIMIT),
        cost_estimate=pl.CostEstimate(
            flops=2 * local_experts * slots * width * (hidden_width + 256),
            bytes_accessed=2 * (weight.size + 2 * acts.size + 10 * blocks[0].size),
            transcendentals=0,
        ),
        name="hidden_and_products",
    )(place, *blocks, weight, acts)


def rows_kernel(local_experts, total_experts, capacity, widths, place, *refs):
    blocks = refs[:8]
    outs = refs[8:]
    me = place[0]
    picker = pick_rows(me, local_experts, total_experts)
    for k in range(8):
        base = pl.multiple_of((me ^ k) * capacity, 16)
        start = 0
        for out, width in zip(outs, widths):

            def store(e, column, step, value, base=base, out=out):
                out[e, pl.ds(base, capacity), column : column + step] = value

            place_rows(blocks[k], start, width, picker, local_experts, capacity, 512, store)
            start += width + LANES


def rows_call(place, blocks, widths, local_experts, total_experts, capacity):
    kernel = functools.partial(rows_kernel, local_experts, total_experts, capacity, widths)
    slots = 8 * capacity
    vmem = pl.BlockSpec(memory_space=pltpu.VMEM)
    return pl.pallas_call(
        kernel,
        in_specs=[pl.BlockSpec(memory_space=pltpu.SMEM)] + [vmem] * 8,
        out_specs=[vmem] * len(widths),
        out_shape=[jax.ShapeDtypeStruct((local_experts, slots, w), BF16) for w in widths],
        compiler_params=pltpu.CompilerParams(vmem_limit_bytes=VMEM_LIMIT),
        cost_estimate=pl.CostEstimate(
            flops=2 * local_experts * slots * 256 * sum(widths),
            bytes_accessed=2 * (8 * blocks[0].size + local_experts * slots * sum(widths)),
            transcendentals=0,
        ),
        name="far_rows",
    )(place, *blocks)


def outer_product(rows, acts):
    return lax.dot_general(rows, acts, (((0,), (0,)), ((), ())), preferred_element_type=F32)


def down_kernel(near, inner, far, outer, near_a, inner_a, far_a, outer_a, own_ref, other_ref):
    total = outer_product(near[0], near_a[...])
    total += outer_product(inner[0], inner_a[...])
    total += outer_product(far[0], far_a[...])

    @pl.when(pl.program_id(0) == 0)
    def _():
        other_ref[...] = total.astype(BF16)

    @pl.when(pl.program_id(0) == 1)
    def _():
        own_ref[...] = total + outer_product(outer[0], outer_a[...])


def down_call(expert, near, inner, far, outer, near_a, inner_a, far_a, outer_a):
    slots, hidden_width = near_a.shape
    part = outer.shape[2]
    half = pl.BlockSpec((1, slots, part), lambda i: (expert, 0, 1 - i))
    acts = pl.BlockSpec((slots, hidden_width), lambda i: (0, 0))
    result = pl.BlockSpec((part, hidden_width), lambda i: (0, 0))
    return pl.pallas_call(
        down_kernel,
        grid=(2,),
        in_specs=[half, half, half, pl.BlockSpec((1, slots, part), lambda i: (expert, 0, 0))]
        + [acts] * 4,
        out_specs=[result, result],
        out_shape=[
            jax.ShapeDtypeStruct((part, hidden_width), F32),
            jax.ShapeDtypeStruct((part, hidden_width), BF16),
        ],
        compiler_params=pltpu.CompilerParams(vmem_limit_bytes=VMEM_LIMIT),
        cost_estimate=pl.CostEstimate(
            flops=2 * slots * hidden_width * 7 * part,
            bytes_accessed=2 * (7 * slots * part + 4 * slots * hidden_width + 3 * part * hidden_width),
            transcendentals=0,
        ),
        name="down_terms",
    )(near, inner, far, outer, near_a, inner_a, far_a, outer_a)


def sum_everywhere(x, member):
    kept = []
    for bits in (1, 2, 4):
        half = x.shape[1] // 2
        low, high = x[:, :half], x[:, half:]
        upper = (member & bits) != 0
        kept.append(upper)
        x = jnp.where(upper, high, low) + plane_swap(jnp.where(upper, low, high), bits)
    others = [lax.ppermute(x, "dp", [(i, i ^ k) for i in range(4)]) for k in (1, 2, 3)]
    x = (x + others[0]) + (others[1] + others[2])
    for bits, upper in zip((4, 2, 1), reversed(kept)):
        other = plane_swap(x, bits)
        x = jnp.concatenate([jnp.where(upper, other, x), jnp.where(upper, x, other)], axis=1)
    return x


def local_line(inputs, out_grad, combine, routes, saved_hidden, down_weight, router_weight):
    width = out_grad.shape[1]
    local_experts = down_weight.shape[0]
    total_experts = router_weight.shape[0]
    capacity = saved_hidden.shape[3]
    hidden_width = saved_hidden.shape[4]
    slots = 8 * capacity
    part = width // 4
    plane = lax.axis_index("dp")
    member = lax.axis_index("expert")
    lower = plane < 2
    acts = saved_hidden.reshape(local_experts, slots, hidden_width)

    routed, positions, weights = dense_routes(routes, combine, total_experts)
    notes = describe(positions, weights)
    parts = [out_grad[:, i * part : (i + 1) * part] for i in range(4)]

    pair = jnp.concatenate(
        [jnp.where(lower, parts[2], parts[1]), jnp.where(lower, parts[3], parts[0]), notes], axis=1
    )
    single = jnp.concatenate([jnp.where(lower, parts[1], parts[2]), notes], axis=1)
    from_inner = lax.ppermute(pair, "dp", INNER)
    from_far = lax.ppermute(pair, "dp", FAR)
    from_outer = lax.ppermute(single, "dp", OUTER)

    own_blocks = plane_gather(jnp.concatenate([out_grad, notes], axis=1))

    inner_acts = []
    outer_acts = []
    far_acts = []
    for expert in range(local_experts):
        outer_acts.append(lax.ppermute(acts[expert], "dp", OUTER))
        inner_acts.append(lax.ppermute(acts[expert], "dp", INNER))
        far_acts.append(lax.ppermute(acts[expert], "dp", FAR))

    other_blocks = plane_gather(jnp.concatenate([from_inner, from_far, from_outer], axis=1))

    other_part = jnp.where(lower, 0, 3)
    place = jnp.stack([member, plane, other_part]).astype(jnp.int32)
    hidden, products, near = hidden_call(
        place, own_blocks, down_weight, acts, total_experts, capacity, part
    )

    returned = lax.all_to_all(products, "expert", split_axis=1, concat_axis=1, tiled=True)
    by_expert = returned.transpose(1, 0, 2).reshape(total_experts, capacity)
    slot_order = jnp.arange(capacity, dtype=jnp.int32).astype(F32)
    hit = positions[:, :, None] == slot_order[None, None, :]
    pair_sums = jnp.sum(jnp.where(hit, by_expert[None], 0.0), axis=2)
    logit_grad = pair_sums - weights * jnp.sum(pair_sums, axis=1, keepdims=True)
    dense_grad = jnp.where(routed, logit_grad, 0.0).astype(BF16)
    input_grad = jnp.dot(dense_grad, router_weight, preferred_element_type=F32).astype(BF16)
    router_part = lax.dot_general(
        dense_grad, inputs, (((0,), (0,)), ((), ())), preferred_element_type=F32
    )
    router_grad = sum_everywhere(router_part, member)

    inner, far, outer = rows_call(
        place, other_blocks, (2 * part, 2 * part, part), local_experts, total_experts, capacity
    )
    down = []
    for expert in range(local_experts):
        own, other = down_call(
            expert, near, inner, far, outer,
            acts[expert], inner_acts[expert], far_acts[expert], outer_acts[expert],
        )
        arrived = lax.ppermute(other, "dp", OUTWARD)
        down.append((own + arrived.astype(F32)).astype(BF16))
    down_grad = jnp.stack(down)

    hidden_grad = hidden.reshape(saved_hidden.shape)
    return (hidden_grad, down_grad, input_grad, router_grad)


def solution(mesh):
    in_line = mesh.shape["dp"] == 4 and mesh.shape["expert"] == 8

    def local(inputs, out_grad, combine, routes, saved_hidden, down_weight, router_weight):
        tokens, width = out_grad.shape
        fits = (
            in_line
            and tokens == LANES
            and KINDS * router_weight.shape[0] == LANES
            and width % 2048 == 0
            and saved_hidden.shape[3] % 16 == 0
            and saved_hidden.shape[4] % LANES == 0
        )
        body = local_line if fits else local_any
        return body(
            inputs, out_grad, combine, routes, saved_hidden, down_weight, router_weight
        )

    placed = (
        P(("dp", "expert"), None),
        P(("dp", "expert"), None),
        P(("dp", "expert"), None),
        P(("dp", "expert"), None),
        P("dp", "expert", None, None, None),
        P("expert", None, None),
        P(),
    )
    return jax.shard_map(
        local,
        mesh=mesh,
        in_specs=placed,
        out_specs=(
            P("dp", "expert", None, None, None),
            P("expert", "dp", None),
            P(("dp", "expert"), None),
            P(),
        ),
        check_vma=False,
    )
```

time: 466 us -> 258 us (0.55)
  waiting for transfers between devices: 350 us -> 112 us
  starting transfers between devices: 8.94 us -> 69.5 us
  Pallas kernels: 0 us -> 54.8 us
  matrix products: 40.6 us -> 1.45 us
  other arithmetic: 27.2 us -> 7.11 us
  between operations: 15.8 us -> 1.47 us
  local copies, waits for them, and re-layouts: 22.4 us -> 10.1 us
    psum x1 -> x0, waiting for transfers between devices: 280 us -> none  [local(): router_grad = lax.psum(router_part, ('dp', 'expert'))]
    ppermute x0 -> x44, waiting for transfers between devices: none -> 109 us  [the longest x22 45.1 us: plane_swap(): return lax.ppermute(x, 'expert', [(i, i ^ bits) for i in range(8)])]
    all_to_all x2 -> x1, waiting for transfers between devices: 70.6 us -> 3.88 us  [local_line(): lax.all_to_all(products, 'expert', split_axis=1, concat_axis=1, tiled=True)]
    ppermute x0 -> x44, starting transfers between devices: none -> 66.2 us  [the longest x4 24.1 us: local_line(): far_acts.append(lax.ppermute(acts[expert], 'dp', FAR))]
    pallas_call x0 -> x6, Pallas kernels: none -> 54.8 us  [the longest x4 29 us: down_call(): pl.pallas_call(down_kernel, grid=(2,), in_specs=[half, half, half, pl.Blo...]
    dot_general x15 -> x3, matrix products: 40.6 us -> 1.45 us  [the longest x1 1.11 us: local_line(): jnp.dot(dense_grad, router_weight, preferred_element_type=F32).astype(BF16)]
    scatter x1 -> x0, other arithmetic: 10.6 us -> none  [pack_rows(): filled = zero_rows.at[flat_index.reshape(-1)].set(scaled.reshape(-1, width))]
    another operation x2 -> x7, other arithmetic: 12.4 us -> 3.25 us  [the longest x5 2.62 us: local_line(): down_grad = jnp.stack(down)]
  transfers between devices with their start and end apart: 4 -> 45, of which waited for: 2 -> 17; matrix products, arithmetic and copies ran while one was open for 7% -> 5% of each run, Pallas kernels for 0% -> 21%
where the time goes in v1:
time: 258 us; the launch traced here: 257 us
  waiting for transfers between devices  112 us (43%)
  starting transfers between devices  69.5 us (27%)
  Pallas kernels  54.8 us (21%)
  local copies, waits for them, and re-layouts  10.1 us (4%)
  other arithmetic  7.11 us (3%)
    ppermute x22, waiting for transfers between devices, plane_swap(): return lax.ppermute(x, 'expert', [(i, i ^ bits) for i in range(8)])  45.1 us
    pallas_call x4, Pallas kernels, down_call(): pl.pallas_call(down_kernel, grid=(2,), in_specs=[half, half, half, pl.Blo...  29 us
    ppermute x4, waiting for transfers between devices, local_line(): outer_acts.append(lax.ppermute(acts[expert], 'dp', OUTER))  25.4 us
    ppermute x4, waiting for transfers between devices, local_line(): arrived = lax.ppermute(other, 'dp', OUTWARD)  24.4 us
    ppermute x4, starting transfers between devices, local_line(): far_acts.append(lax.ppermute(acts[expert], 'dp', FAR))  24.1 us
    ppermute x22, starting transfers between devices, plane_swap(): return lax.ppermute(x, 'expert', [(i, i ^ bits) for i in range(8)])  15.8 us
    pallas_call x1, Pallas kernels, hidden_call(): pl.pallas_call(kernel, grid_spec=pltpu.PrefetchScalarGridSpec(num_scalar_...  15 us
    ppermute x4, waiting for transfers between devices, local_line(): far_acts.append(lax.ppermute(acts[expert], 'dp', FAR))  13.4 us
  transfers between devices with their start and end apart: 45, of which 17 were waited for; matrix products, arithmetic and copies ran while one was open for 5% of the time, Pallas kernels for 21%

profile of v1, /device:TPU:0, one launch (start us, length us, event | category | flops | bytes accessed | tf_op | source)
XLA Modules:
  0.0 256.7 jit_solution(9423943149763738539)
XLA Ops:
  7.3 11.2 %collective-permute-done.1.refs_2_ = bf16[128,2176]{1,0:T(8,128)(2,1)} collective-permute-done((bf16[128,2176]{1,0:T(8,128)(2,1)S(1)}, bf16[128,2176]{1,0:T(8,128)(2,1)}, u32[]{:S(2)}, u32[]{:S(2)}) %collective-permute-start.1) | collective-permute-done | bytes 557088 | tf_op jit(solution)/shard_map/ppermute | solution.py:93
  28.1 3.4 %collective-permute-done.6 = bf16[64,2176]{1,0:T(8,128)(2,1)S(1)} collective-permute-done((bf16[64,2176]{1,0:T(8,128)(2,1)S(1)}, bf16[64,2176]{1,0:T(8,128)(2,1)S(1)}, u32[]{:S(2)}, u32[]{:S(2)}) %collective-permute-start.6) | collective-permute-done | bytes 278560 | tf_op jit(solution)/shard_map/ppermute | solution.py:93
  33.6 6.2 %collective-permute-start.9 = (bf16[128,1152]{1,0:T(8,128)(2,1)S(1)}, bf16[128,1152]{1,0:T(8,128)(2,1)S(1)}, u32[]{:S(2)}, u32[]{:S(2)}) collective-permute-start(bf16[128,1152]{1,0:T(8,128)(2,1)S(1)} %pad_maximum_fusion.2), channel_id=1, source_target_pairs={{0,16},{24,8},{1,17},{25,9},{2,18},{26,10},{3,19},{27,11},{4,20},{... | collective-permute-start | bytes 884744 | tf_op jit(solution)/shard_map/ppermute | solution.py:347
  42.1 15.0 %hidden_and_products.1 = (bf16[4,384,768]{2,1,0:T(8,128)(2,1)}, f32[4,8,48]{2,1,0:T(8,128)}, bf16[4,384,1024]{2,1,0:T(8,128)(2,1)}) custom-call(s32[3]{0:T(128)} %pad_add_fusion.place, bf16[128,2176]{1,0:T(8,128)(2,1)} %copy-done.22, bf16[128,2176]{1,0:T(8,128)(2,1)} %collective-permute-done.refs_1_, bf16[128,2176]{1,0:T(8,128)(2,1)} %collective-permute-done.1.refs_2_, ...), custom_call_target="tpu_custom_call" | custom-call | flops 6442450944 | bytes 22872064 | tf_op jit(solution)/shard_map/hidden_and_products/pallas_call | solution.py:197
  58.5 3.3 %all-to-all-start = ((f32[8,1,192]{2,1,0:T(1,128)}), f32[8,1,192]{2,1,0:T(1,128)S(1)}, u32[]{:S(2)}, u32[]{:S(2)}) async-start(f32[8,1,192]{2,1,0:T(1,128)} %reshape.33), calls=%async_computation | async-start | bytes 16384 | tf_op jit(solution)/shard_map/all_to_all | solution.py:368
  62.6 3.9 %all-to-all-done = f32[8,1,192]{2,1,0:T(1,128)S(1)} async-done(((f32[8,1,192]{2,1,0:T(1,128)}), f32[8,1,192]{2,1,0:T(1,128)S(1)}, u32[]{:S(2)}, u32[]{:S(2)}) %all-to-all-start) | async-done | bytes 6176 | tf_op jit(solution)/shard_map/all_to_all | solution.py:368
  72.6 18.1 %collective-permute-done.36 = f32[32,512]{1,0:T(8,128)S(1)} collective-permute-done((f32[32,512]{1,0:T(8,128)S(1)}, f32[32,512]{1,0:T(8,128)S(1)}, u32[]{:S(2)}, u32[]{:S(2)}) %collective-permute-start.36) | collective-permute-done | bytes 65568 | tf_op jit(solution)/shard_map/ppermute | solution.py:93
  100.0 5.5 %collective-permute-start.32 = (bf16[384,768]{1,0:T(8,128)(2,1)S(1)}, bf16[384,768]{1,0:T(8,128)(2,1)S(1)}, u32[]{:S(2)}, u32[]{:S(2)}) collective-permute-start(bf16[384,768]{1,0:T(8,128)(2,1)S(1)} %bitcast.43), channel_id=1, source_target_pairs={{0,16},{24,8},{1,17},{25,9},{2,18},{26,10},{3,19},{27,11},{4,20},{... | collective-permute-start | bytes 1769480 | tf_op jit(solution)/shard_map/ppermute | solution.py:358
  112.3 6.9 %collective-permute-done.32.far_a = bf16[384,768]{1,0:T(8,128)(2,1)S(1)} collective-permute-done((bf16[384,768]{1,0:T(8,128)(2,1)S(1)}, bf16[384,768]{1,0:T(8,128)(2,1)S(1)}, u32[]{:S(2)}, u32[]{:S(2)}) %collective-permute-start.32) | collective-permute-done | bytes 589856 | tf_op jit(solution)/shard_map/ppermute | solution.py:358
  119.3 9.0 %collective-permute-done.33.outer_a = bf16[384,768]{1,0:T(8,128)(2,1)S(1)} collective-permute-done((bf16[384,768]{1,0:T(8,128)(2,1)S(1)}, bf16[384,768]{1,0:T(8,128)(2,1)S(1)}, u32[]{:S(2)}, u32[]{:S(2)}) %collective-permute-start.33) | collective-permute-done | bytes 589856 | tf_op jit(solution)/shard_map/ppermute | solution.py:356
  128.9 3.9 %collective-permute-done.42 = f32[32,512]{1,0:T(8,128)S(1)} collective-permute-done((f32[32,512]{1,0:T(8,128)S(1)}, f32[32,512]{1,0:T(8,128)S(1)}, u32[]{:S(2)}, u32[]{:S(2)}) %collective-permute-start.42) | collective-permute-done | bytes 65568 | tf_op jit(solution)/shard_map/ppermute | solution.py:93
  134.6 8.9 %collective-permute-start.28 = (bf16[384,768]{1,0:T(8,128)(2,1)S(1)}, bf16[384,768]{1,0:T(8,128)(2,1)S(1)}, u32[]{:S(2)}, u32[]{:S(2)}) collective-permute-start(bf16[384,768]{1,0:T(8,128)(2,1)S(1)} %bitcast.39), channel_id=1, source_target_pairs={{0,16},{24,8},{1,17},{25,9},{2,18},{26,10},{3,19},{27,11},{4,20},{... | collective-permute-start | bytes 1769480 | tf_op jit(solution)/shard_map/ppermute | solution.py:358
  145.5 3.8 %collective-permute-start.24 = (bf16[384,768]{1,0:T(8,128)(2,1)S(1)}, bf16[384,768]{1,0:T(8,128)(2,1)S(1)}, u32[]{:S(2)}, u32[]{:S(2)}) collective-permute-start(bf16[384,768]{1,0:T(8,128)(2,1)S(1)} %bitcast.35), channel_id=1, source_target_pairs={{0,16},{24,8},{1,17},{25,9},{2,18},{26,10},{3,19},{27,11},{4,20},{... | collective-permute-start | bytes 1769480 | tf_op jit(solution)/shard_map/ppermute | solution.py:358
  150.9 10.8 %far_rows.1 = (bf16[4,384,1024]{2,1,0:T(8,128)(2,1)}, bf16[4,384,1024]{2,1,0:T(8,128)(2,1)}, bf16[4,384,512]{2,1,0:T(8,128)(2,1)}) custom-call(s32[3]{0:T(128)} %pad_add_fusion.place, bf16[128,2944]{1,0:T(8,128)(2,1)} %constant_dynamic-update-slice_fusion.2.refs_0_, bf16[128,2944]{1,0:T(8,128)(2,1)} %collective-permute-done.11.refs_1_, ...), custom_call_target="tpu_custom_call" | custom-call | flops 2013265920 | bytes 13893632 | tf_op jit(solution)/shard_map/far_rows/pallas_call | solution.py:250
  161.7 7.3 %down_terms.7 = (f32[512,768]{1,0:T(8,128)}, bf16[512,768]{1,0:T(8,128)(2,1)}) custom-call(bf16[4,384,1024]{2,1,0:T(8,128)(2,1)} %get-tuple-element.19.near, bf16[4,384,1024]{2,1,0:T(8,128)(2,1)} %get-tuple-element.20.inner, bf16[4,384,1024]{2,1,0:T(8,128)(2,1)} %get-tuple-element.21.far, bf16[4,384,512]{2,1,0:T(8,128)(2,1)} %get-tuple-element.22.outer, ...), custom_call_target="tpu_custom_call" | custom-call | flops 2113929216 | bytes 7471104 | tf_op jit(solution)/shard_map/down_terms/pallas_call | solution.py:289
  169.8 5.9 %collective-permute-start.20 = (bf16[384,768]{1,0:T(8,128)(2,1)S(1)}, bf16[384,768]{1,0:T(8,128)(2,1)}, u32[]{:S(2)}, u32[]{:S(2)}) collective-permute-start(bf16[384,768]{1,0:T(8,128)(2,1)S(1)} %bitcast.31), channel_id=1, source_target_pairs={{0,16},{24,8},{1,17},{25,9},{2,18},{26,10},{3,19},{27,11},{4,20},{... | collective-permute-start | bytes 1769480 | tf_op jit(solution)/shard_map/ppermute | solution.py:358
  177.8 4.6 %collective-permute-done.24.far_a = bf16[384,768]{1,0:T(8,128)(2,1)S(1)} collective-permute-done((bf16[384,768]{1,0:T(8,128)(2,1)S(1)}, bf16[384,768]{1,0:T(8,128)(2,1)S(1)}, u32[]{:S(2)}, u32[]{:S(2)}) %collective-permute-start.24) | collective-permute-done | bytes 589856 | tf_op jit(solution)/shard_map/ppermute | solution.py:358
  183.7 7.2 %down_terms.6 = (f32[512,768]{1,0:T(8,128)}, bf16[512,768]{1,0:T(8,128)(2,1)}) custom-call(bf16[4,384,1024]{2,1,0:T(8,128)(2,1)} %get-tuple-element.19.near, bf16[4,384,1024]{2,1,0:T(8,128)(2,1)} %get-tuple-element.20.inner, bf16[4,384,1024]{2,1,0:T(8,128)(2,1)} %get-tuple-element.21.far, bf16[4,384,512]{2,1,0:T(8,128)(2,1)} %get-tuple-element.22.outer, ...), custom_call_target="tpu_custom_call" | custom-call | flops 2113929216 | bytes 7471104 | tf_op jit(solution)/shard_map/down_terms/pallas_call | solution.py:289
  190.9 4.1 %collective-permute-done.25.outer_a = bf16[384,768]{1,0:T(8,128)(2,1)S(1)} collective-permute-done((bf16[384,768]{1,0:T(8,128)(2,1)S(1)}, bf16[384,768]{1,0:T(8,128)(2,1)S(1)}, u32[]{:S(2)}, u32[]{:S(2)}) %collective-permute-start.25) | collective-permute-done | bytes 589856 | tf_op jit(solution)/shard_map/ppermute | solution.py:356
  197.0 7.3 %down_terms.5 = (f32[512,768]{1,0:T(8,128)}, bf16[512,768]{1,0:T(8,128)(2,1)}) custom-call(bf16[4,384,1024]{2,1,0:T(8,128)(2,1)} %get-tuple-element.19.near, bf16[4,384,1024]{2,1,0:T(8,128)(2,1)} %get-tuple-element.20.inner, bf16[4,384,1024]{2,1,0:T(8,128)(2,1)} %get-tuple-element.21.far, bf16[4,384,512]{2,1,0:T(8,128)(2,1)} %get-tuple-element.22.outer, ...), custom_call_target="tpu_custom_call" | custom-call | flops 2113929216 | bytes 7471104 | tf_op jit(solution)/shard_map/down_terms/pallas_call | solution.py:289
  207.7 12.2 %collective-permute-done.21.outer_a = bf16[384,768]{1,0:T(8,128)(2,1)} collective-permute-done((bf16[384,768]{1,0:T(8,128)(2,1)S(1)}, bf16[384,768]{1,0:T(8,128)(2,1)}, u32[]{:S(2)}, u32[]{:S(2)}) %collective-permute-start.21) | collective-permute-done | bytes 589856 | tf_op jit(solution)/shard_map/ppermute | solution.py:356
  219.9 7.2 %down_terms.4 = (f32[512,768]{1,0:T(8,128)}, bf16[512,768]{1,0:T(8,128)(2,1)}) custom-call(bf16[4,384,1024]{2,1,0:T(8,128)(2,1)} %get-tuple-element.19.near, bf16[4,384,1024]{2,1,0:T(8,128)(2,1)} %get-tuple-element.20.inner, bf16[4,384,1024]{2,1,0:T(8,128)(2,1)} %get-tuple-element.21.far, bf16[4,384,512]{2,1,0:T(8,128)(2,1)} %get-tuple-element.22.outer, ...), custom_call_target="tpu_custom_call" | custom-call | flops 2113929216 | bytes 7471104 | tf_op jit(solution)/shard_map/down_terms/pallas_call | solution.py:289
  230.0 9.2 %collective-permute-done.26 = bf16[512,768]{1,0:T(8,128)(2,1)S(1)} collective-permute-done((bf16[512,768]{1,0:T(8,128)(2,1)}, bf16[512,768]{1,0:T(8,128)(2,1)S(1)}, u32[]{:S(2)}, u32[]{:S(2)}) %collective-permute-start.26) | collective-permute-done | bytes 786464 | tf_op jit(solution)/shard_map/ppermute | solution.py:390
  239.4 15.2 %collective-permute-done.22 = bf16[512,768]{1,0:T(8,128)(2,1)S(1)} collective-permute-done((bf16[512,768]{1,0:T(8,128)(2,1)}, bf16[512,768]{1,0:T(8,128)(2,1)S(1)}, u32[]{:S(2)}, u32[]{:S(2)}) %collective-permute-start.22) | collective-permute-done | bytes 786464 | tf_op jit(solution)/shard_map/ppermute | solution.py:390
  (183 shorter events, 65.1 us)
Async XLA Ops:
  32.3 29.6 %collective-permute-start.8 = (bf16[128,1152]{1,0:T(8,128)(2,1)S(1)}, bf16[128,1152]{1,0:T(8,128)(2,1)S(1)}, u32[]{:S(2)}, u32[]{:S(2)}) collective-permute-start(bf16[128,1152]{1,0:T(8,128)(2,1)S(1)} %pad_maximum_fusion.2), channel_id=1, source_target_pairs={{8,16},{16,8},{9,17},{17,9},{10,18},{18,10},{11,19},{19,11},{12,20... | collective-permute-start | bytes 884744 | tf_op jit(solution)/shard_map/ppermute | solution.py:346
  33.6 34.8 %collective-permute-start.9 = (bf16[128,1152]{1,0:T(8,128)(2,1)S(1)}, bf16[128,1152]{1,0:T(8,128)(2,1)S(1)}, u32[]{:S(2)}, u32[]{:S(2)}) collective-permute-start(bf16[128,1152]{1,0:T(8,128)(2,1)S(1)} %pad_maximum_fusion.2), channel_id=1, source_target_pairs={{0,16},{24,8},{1,17},{25,9},{2,18},{26,10},{3,19},{27,11},{4,20},{... | collective-permute-start | bytes 884744 | tf_op jit(solution)/shard_map/ppermute | solution.py:347
  39.8 29.4 %collective-permute-start.10 = (bf16[128,640]{1,0:T(8,128)(2,1)S(1)}, bf16[128,640]{1,0:T(8,128)(2,1)S(1)}, u32[]{:S(2)}, u32[]{:S(2)}) collective-permute-start(bf16[128,640]{1,0:T(8,128)(2,1)S(1)} %pad_maximum_fusion.4), channel_id=1, source_target_pairs={{0,8},{24,16},{1,9},{25,17},{2,10},{26,18},{3,11},{27,19},{4,12},{... | collective-permute-start | bytes 491528 | tf_op jit(solution)/shard_map/ppermute | solution.py:348
  69.9 21.5 %collective-permute-start.12 = (bf16[128,2944]{1,0:T(8,128)(2,1)}, bf16[128,2944]{1,0:T(8,128)(2,1)S(1)}, u32[]{:S(2)}, u32[]{:S(2)}) collective-permute-start(bf16[128,2944]{1,0:T(8,128)(2,1)} %constant_dynamic-update-slice_fusion.2.refs_0_), channel_id=1, source_target_pairs={{0,2},{1,3},{2,0},{3,1},{4,6},{5,7},{6,4},{7,5},{8,10},{9,11},{10,... | collective-permute-start | bytes 2261000 | tf_op jit(solution)/shard_map/ppermute | solution.py:93
  70.5 20.2 %collective-permute-start.36 = (f32[32,512]{1,0:T(8,128)S(1)}, f32[32,512]{1,0:T(8,128)S(1)}, u32[]{:S(2)}, u32[]{:S(2)}) collective-permute-start(f32[32,512]{1,0:T(8,128)S(1)} %slice_select_fusion.2), channel_id=1, source_target_pairs={{0,2},{1,3},{2,0},{3,1},{4,6},{5,7},{6,4},{7,5},{8,10},{9,11},{10,... | collective-permute-start | bytes 196616 | tf_op jit(solution)/shard_map/ppermute | solution.py:93
  72.0 26.9 %collective-permute-start.14 = (bf16[128,2944]{1,0:T(8,128)(2,1)}, bf16[128,2944]{1,0:T(8,128)(2,1)S(1)}, u32[]{:S(2)}, u32[]{:S(2)}) collective-permute-start(bf16[128,2944]{1,0:T(8,128)(2,1)} %constant_dynamic-update-slice_fusion.2.refs_0_), channel_id=1, source_target_pairs={{0,4},{1,5},{2,6},{3,7},{4,0},{5,1},{6,2},{7,3},{8,12},{9,13},{10,... | collective-permute-start | bytes 2261000 | tf_op jit(solution)/shard_map/ppermute | solution.py:93
  100.0 19.3 %collective-permute-start.32 = (bf16[384,768]{1,0:T(8,128)(2,1)S(1)}, bf16[384,768]{1,0:T(8,128)(2,1)S(1)}, u32[]{:S(2)}, u32[]{:S(2)}) collective-permute-start(bf16[384,768]{1,0:T(8,128)(2,1)S(1)} %bitcast.43), channel_id=1, source_target_pairs={{0,16},{24,8},{1,17},{25,9},{2,18},{26,10},{3,19},{27,11},{4,20},{... | collective-permute-start | bytes 1769480 | tf_op jit(solution)/shard_map/ppermute | solution.py:358
  105.6 22.7 %collective-permute-start.33 = (bf16[384,768]{1,0:T(8,128)(2,1)S(1)}, bf16[384,768]{1,0:T(8,128)(2,1)S(1)}, u32[]{:S(2)}, u32[]{:S(2)}) collective-permute-start(bf16[384,768]{1,0:T(8,128)(2,1)S(1)} %bitcast.44), channel_id=1, source_target_pairs={{0,8},{24,16},{1,9},{25,17},{2,10},{26,18},{3,11},{27,19},{4,12},{... | collective-permute-start | bytes 1769480 | tf_op jit(solution)/shard_map/ppermute | solution.py:356
  106.9 21.4 %collective-permute-start.17 = (bf16[64,2944]{1,0:T(8,128)(2,1)S(1)}, bf16[64,2944]{1,0:T(8,128)(2,1)S(1)}, u32[]{:S(2)}, u32[]{:S(2)}) collective-permute-start(bf16[64,2944]{1,0:T(8,128)(2,1)S(1)} %slice.91), channel_id=1, source_target_pairs={{0,2},{1,3},{2,0},{3,1},{4,6},{5,7},{6,4},{7,5},{8,10},{9,11},{10,... | collective-permute-start | bytes 1130504 | tf_op jit(solution)/shard_map/ppermute | solution.py:93
  111.5 21.3 %collective-permute-start.27 = (bf16[384,768]{1,0:T(8,128)(2,1)S(1)}, bf16[384,768]{1,0:T(8,128)(2,1)S(1)}, u32[]{:S(2)}, u32[]{:S(2)}) collective-permute-start(bf16[384,768]{1,0:T(8,128)(2,1)S(1)} %bitcast.38), channel_id=1, source_target_pairs={{8,16},{16,8},{9,17},{17,9},{10,18},{18,10},{11,19},{19,11},{12,20... | collective-permute-start | bytes 1769480 | tf_op jit(solution)/shard_map/ppermute | solution.py:357
  112.3 22.3 %collective-permute-start.11 = (bf16[128,2944]{1,0:T(8,128)(2,1)S(1)}, bf16[128,2944]{1,0:T(8,128)(2,1)}, u32[]{:S(2)}, u32[]{:S(2)}) collective-permute-start(bf16[128,2944]{1,0:T(8,128)(2,1)S(1)} %copy-done.27), channel_id=1, source_target_pairs={{0,1},{1,0},{2,3},{3,2},{4,5},{5,4},{6,7},{7,6},{8,9},{9,8},{10,11... | collective-permute-start | bytes 2261000 | tf_op jit(solution)/shard_map/ppermute | solution.py:93
  119.3 24.1 %collective-permute-start.13 = (bf16[128,2944]{1,0:T(8,128)(2,1)S(1)}, bf16[128,2944]{1,0:T(8,128)(2,1)}, u32[]{:S(2)}, u32[]{:S(2)}) collective-permute-start(bf16[128,2944]{1,0:T(8,128)(2,1)S(1)} %collective-permute-done.12.refs_2_), channel_id=1, source_target_pairs={{0,1},{1,0},{2,3},{3,2},{4,5},{5,4},{6,7},{7,6},{8,9},{9,8},{10,11... | collective-permute-start | bytes 2261000 | tf_op jit(solution)/shard_map/ppermute | solution.py:93
  134.6 34.5 %collective-permute-start.28 = (bf16[384,768]{1,0:T(8,128)(2,1)S(1)}, bf16[384,768]{1,0:T(8,128)(2,1)S(1)}, u32[]{:S(2)}, u32[]{:S(2)}) collective-permute-start(bf16[384,768]{1,0:T(8,128)(2,1)S(1)} %bitcast.39), channel_id=1, source_target_pairs={{0,16},{24,8},{1,17},{25,9},{2,18},{26,10},{3,19},{27,11},{4,20},{... | collective-permute-start | bytes 1769480 | tf_op jit(solution)/shard_map/ppermute | solution.py:358
  143.4 26.3 %collective-permute-start.29 = (bf16[384,768]{1,0:T(8,128)(2,1)S(1)}, bf16[384,768]{1,0:T(8,128)(2,1)S(1)}, u32[]{:S(2)}, u32[]{:S(2)}) collective-permute-start(bf16[384,768]{1,0:T(8,128)(2,1)S(1)} %bitcast.40), channel_id=1, source_target_pairs={{0,8},{24,16},{1,9},{25,17},{2,10},{26,18},{3,11},{27,19},{4,12},{... | collective-permute-start | bytes 1769480 | tf_op jit(solution)/shard_map/ppermute | solution.py:356
  144.8 30.8 %collective-permute-start.23 = (bf16[384,768]{1,0:T(8,128)(2,1)S(1)}, bf16[384,768]{1,0:T(8,128)(2,1)S(1)}, u32[]{:S(2)}, u32[]{:S(2)}) collective-permute-start(bf16[384,768]{1,0:T(8,128)(2,1)S(1)} %bitcast.34), channel_id=1, source_target_pairs={{8,16},{16,8},{9,17},{17,9},{10,18},{18,10},{11,19},{19,11},{12,20... | collective-permute-start | bytes 1769480 | tf_op jit(solution)/shard_map/ppermute | solution.py:357
  145.5 36.9 %collective-permute-start.24 = (bf16[384,768]{1,0:T(8,128)(2,1)S(1)}, bf16[384,768]{1,0:T(8,128)(2,1)S(1)}, u32[]{:S(2)}, u32[]{:S(2)}) collective-permute-start(bf16[384,768]{1,0:T(8,128)(2,1)S(1)} %bitcast.35), channel_id=1, source_target_pairs={{0,16},{24,8},{1,17},{25,9},{2,18},{26,10},{3,19},{27,11},{4,20},{... | collective-permute-start | bytes 1769480 | tf_op jit(solution)/shard_map/ppermute | solution.py:358
  149.3 45.7 %collective-permute-start.25 = (bf16[384,768]{1,0:T(8,128)(2,1)S(1)}, bf16[384,768]{1,0:T(8,128)(2,1)S(1)}, u32[]{:S(2)}, u32[]{:S(2)}) collective-permute-start(bf16[384,768]{1,0:T(8,128)(2,1)S(1)} %bitcast.36), channel_id=1, source_target_pairs={{0,8},{24,16},{1,9},{25,17},{2,10},{26,18},{3,11},{27,19},{4,12},{... | collective-permute-start | bytes 1769480 | tf_op jit(solution)/shard_map/ppermute | solution.py:356
  169.0 35.3 %collective-permute-start.19 = (bf16[384,768]{1,0:T(8,128)(2,1)S(1)}, bf16[384,768]{1,0:T(8,128)(2,1)S(1)}, u32[]{:S(2)}, u32[]{:S(2)}) collective-permute-start(bf16[384,768]{1,0:T(8,128)(2,1)S(1)} %bitcast.30), channel_id=1, source_target_pairs={{8,16},{16,8},{9,17},{17,9},{10,18},{18,10},{11,19},{19,11},{12,20... | collective-permute-start | bytes 1769480 | tf_op jit(solution)/shard_map/ppermute | solution.py:357
  169.8 37.9 %collective-permute-start.20 = (bf16[384,768]{1,0:T(8,128)(2,1)S(1)}, bf16[384,768]{1,0:T(8,128)(2,1)}, u32[]{:S(2)}, u32[]{:S(2)}) collective-permute-start(bf16[384,768]{1,0:T(8,128)(2,1)S(1)} %bitcast.31), channel_id=1, source_target_pairs={{0,16},{24,8},{1,17},{25,9},{2,18},{26,10},{3,19},{27,11},{4,20},{... | collective-permute-start | bytes 1769480 | tf_op jit(solution)/shard_map/ppermute | solution.py:358
  175.6 44.3 %collective-permute-start.21 = (bf16[384,768]{1,0:T(8,128)(2,1)S(1)}, bf16[384,768]{1,0:T(8,128)(2,1)}, u32[]{:S(2)}, u32[]{:S(2)}) collective-permute-start(bf16[384,768]{1,0:T(8,128)(2,1)S(1)} %bitcast.32), channel_id=1, source_target_pairs={{0,8},{24,16},{1,9},{25,17},{2,10},{26,18},{3,11},{27,19},{4,12},{... | collective-permute-start | bytes 1769480 | tf_op jit(solution)/shard_map/ppermute | solution.py:356
  182.4 46.0 %collective-permute-start.34 = (bf16[512,768]{1,0:T(8,128)(2,1)}, bf16[512,768]{1,0:T(8,128)(2,1)S(1)}, u32[]{:S(2)}, u32[]{:S(2)}) collective-permute-start(bf16[512,768]{1,0:T(8,128)(2,1)} %get-tuple-element.30), channel_id=1, source_target_pairs={{8,0},{16,24},{9,1},{17,25},{10,2},{18,26},{11,3},{19,27},{12,4},{... | collective-permute-start | bytes 2359304 | tf_op jit(solution)/shard_map/ppermute | solution.py:390
  195.0 33.6 %collective-permute-start.30 = (bf16[512,768]{1,0:T(8,128)(2,1)}, bf16[512,768]{1,0:T(8,128)(2,1)S(1)}, u32[]{:S(2)}, u32[]{:S(2)}) collective-permute-start(bf16[512,768]{1,0:T(8,128)(2,1)} %get-tuple-element.28), channel_id=1, source_target_pairs={{8,0},{16,24},{9,1},{17,25},{10,2},{18,26},{11,3},{19,27},{12,4},{... | collective-permute-start | bytes 2359304 | tf_op jit(solution)/shard_map/ppermute | solution.py:390
  204.4 34.9 %collective-permute-start.26 = (bf16[512,768]{1,0:T(8,128)(2,1)}, bf16[512,768]{1,0:T(8,128)(2,1)S(1)}, u32[]{:S(2)}, u32[]{:S(2)}) collective-permute-start(bf16[512,768]{1,0:T(8,128)(2,1)} %get-tuple-element.26), channel_id=1, source_target_pairs={{8,0},{16,24},{9,1},{17,25},{10,2},{18,26},{11,3},{19,27},{12,4},{... | collective-permute-start | bytes 2359304 | tf_op jit(solution)/shard_map/ppermute | solution.py:390
  227.1 27.6 %collective-permute-start.22 = (bf16[512,768]{1,0:T(8,128)(2,1)}, bf16[512,768]{1,0:T(8,128)(2,1)S(1)}, u32[]{:S(2)}, u32[]{:S(2)}) collective-permute-start(bf16[512,768]{1,0:T(8,128)(2,1)} %get-tuple-element.24), channel_id=1, source_target_pairs={{8,0},{16,24},{9,1},{17,25},{10,2},{18,26},{11,3},{19,27},{12,4},{... | collective-permute-start | bytes 2359304 | tf_op jit(solution)/shard_map/ppermute | solution.py:390
  (52 other events, 995.7 us)

commit v2 on v1

--- a/solution.py
+++ b/solution.py
@@ -11,7 +11,9 @@
 BF16 = jnp.bfloat16
 LANES = 128
 KINDS = 4
-VMEM_LIMIT = 56 * 1024 * 1024
+VMEM_LIMIT = 48 * 1024 * 1024
+ANYWHERE = pl.BlockSpec(memory_space=pl.ANY)
+SMALL = pl.CostEstimate(flops=1000, bytes_accessed=1000, transcendentals=0)
 
 
 def make_marks(block_routes, total_experts):
@@ -93,16 +95,21 @@
     return lax.ppermute(x, "expert", [(i, i ^ bits) for i in range(8)])
 
 
-def plane_gather(x):
-    half = x.shape[0] // 2
-    across = plane_swap(x, 2)
-    along = plane_swap(x, 4)
-    diagonal = jnp.concatenate([plane_swap(across[:half], 4), plane_swap(along[half:], 2)])
-    same_core = {0: x, 2: across, 4: along, 6: diagonal}
-    blocks = dict(same_core)
-    for k, block in same_core.items():
-        blocks[k + 1] = plane_swap(block, 1)
-    return [blocks[k] for k in range(8)]
+def plane_blocks(x, across, along, diagonal):
+    return [
+        x,
+        plane_swap(x, 1),
+        across,
+        plane_swap(across, 1),
+        along,
+        plane_swap(along, 1),
+        diagonal,
+        tuple(plane_swap(piece, 1) for piece in diagonal),
+    ]
+
+
+def plane_diagonal(halves):
+    return plane_swap(halves[0], 4), plane_swap(halves[1], 2)
 
 
 def dense_routes(routes, combine, total_experts):
@@ -133,7 +140,7 @@
 
 def place_rows(ref, start, width, picker, local_experts, capacity, step, store):
     notes = jnp.dot(
-        picker, ref[:, start + width : start + width + LANES], preferred_element_type=F32
+        picker, read_block(ref, start + width, start + width + LANES), preferred_element_type=F32
     )
     slots = lax.broadcasted_iota(jnp.int32, (capacity, LANES), 0).astype(F32)
     marks = []
@@ -152,7 +159,7 @@
     for column in range(0, width, step):
         rows = jnp.dot(
             mark,
-            ref[:, start + column : start + column + step],
+            read_block(ref, start + column, start + column + step),
             preferred_element_type=F32,
         )
         rows = (rows * scale).astype(BF16)
@@ -160,9 +167,39 @@
             store(expert, column, step, rows[expert * capacity : (expert + 1) * capacity])
 
 
-def hidden_kernel(local_experts, total_experts, capacity, width, part, place, *refs):
-    blocks = refs[:8]
-    weight_ref, acts_ref, hidden_ref, products_ref, near_ref, rows = refs[8:]
+def read_block(block, start, stop):
+    if isinstance(block, tuple):
+        return jnp.concatenate([half[:, start:stop] for half in block], axis=0)
+    return block[:, start:stop]
+
+
+def split_blocks(blocks):
+    flat = []
+    for block in blocks:
+        flat.extend(block if isinstance(block, tuple) else (block,))
+    return flat
+
+
+def join_blocks(refs, shapes):
+    refs = list(refs)
+    blocks = []
+    for count in shapes:
+        blocks.append(refs.pop(0) if count == 1 else (refs.pop(0), refs.pop(0)))
+    return blocks
+
+
+def counts_of(blocks):
+    return tuple(2 if isinstance(block, tuple) else 1 for block in blocks)
+
+
+def hidden_kernel(
+    local_experts, total_experts, capacity, width, part, counts, n_after, place, *refs
+):
+    n_blocks = sum(counts)
+    blocks = join_blocks(refs[:n_blocks], counts)
+    weight_ref, acts_ref = refs[n_blocks : n_blocks + 2]
+    hidden_ref, products_ref, near_ref = refs[n_blocks + 2 + n_after :][:3]
+    rows = refs[-1]
     expert = pl.program_id(0)
     me = place[0]
 
@@ -180,61 +217,80 @@
     hidden = jnp.dot(rows[expert], weight_ref[0], preferred_element_type=F32)
     hidden_ref[0] = hidden.astype(BF16)
     product = hidden * acts_ref[0].astype(F32)
-    products_ref[0] = jnp.sum(product.reshape(8, capacity, product.shape[1]), axis=2)
+    sums = jnp.sum(product.reshape(8, capacity, product.shape[1]), axis=2)
+    empty = jnp.zeros((8, LANES - capacity), F32)
+    products_ref[0] = jnp.concatenate([sums, empty], axis=1)
     own = pl.multiple_of(place[1] * part, LANES)
     other = pl.multiple_of(place[2] * part, LANES)
     near_ref[0, :, :part] = rows[expert, :, pl.ds(own, part)]
     near_ref[0, :, part:] = rows[expert, :, pl.ds(other, part)]
 
 
-def hidden_call(place, blocks, weight, acts, total_experts, capacity, part):
+def hidden_call(place, blocks, weight, acts, total_experts, capacity, part, after, through):
     local_experts, width, hidden_width = weight.shape
     slots = acts.shape[1]
     kernel = functools.partial(
-        hidden_kernel, local_experts, total_experts, capacity, width, part
-    )
-    whole = pl.BlockSpec(blocks[0].shape, lambda e, p: (0, 0))
+        hidden_kernel,
+        local_experts,
+        total_experts,
+        capacity,
+        width,
+        part,
+        counts_of(blocks),
+        len(after) + len(through),
+    )
+    flat = split_blocks(blocks)
+    tokens = flat[0]
+    n_before = 1 + len(flat) + 2 + len(after)
     return pl.pallas_call(
         kernel,
         grid_spec=pltpu.PrefetchScalarGridSpec(
             num_scalar_prefetch=1,
             grid=(local_experts,),
-            in_specs=[whole] * 8
+            in_specs=[pl.BlockSpec(b.shape, lambda e, p: (0, 0)) for b in flat]
             + [
                 pl.BlockSpec((1, width, hidden_width), lambda e, p: (e, 0, 0)),
                 pl.BlockSpec((1, slots, hidden_width), lambda e, p: (e, 0, 0)),
-            ],
+            ]
+            + [ANYWHERE] * (len(after) + len(through)),
             out_specs=[
                 pl.BlockSpec((1, slots, hidden_width), lambda e, p: (e, 0, 0)),
-                pl.BlockSpec((1, 8, capacity), lambda e, p: (e, 0, 0)),
+                pl.BlockSpec((1, 8, LANES), lambda e, p: (e, 0, 0)),
                 pl.BlockSpec((1, slots, 2 * part), lambda e, p: (e, 0, 0)),
-            ],
+            ]
+            + [ANYWHERE] * len(through),
             scratch_shapes=[pltpu.VMEM((local_experts, slots, width), BF16)],
         ),
         out_shape=[
             jax.ShapeDtypeStruct((local_experts, slots, hidden_width), BF16),
-            jax.ShapeDtypeStruct((local_experts, 8, capacity), F32),
-            jax.ShapeDtypeStruct((local_experts, slots, 2 * part), BF16),
-        ],
+            jax.ShapeDtypeStruct((local_experts, 8, LANES), F32),
+            pltpu.VMEM((local_experts, slots, 2 * part), BF16),
+        ]
+        + [jax.ShapeDtypeStruct(array.shape, array.dtype) for array in through],
+        input_output_aliases={n_before + i: 3 + i for i in range(len(through))},
         compiler_params=pltpu.CompilerParams(vmem_limit_bytes=VMEM_LIMIT),
         cost_estimate=pl.CostEstimate(
             flops=2 * local_experts * slots * width * (hidden_width + 256),
-            bytes_accessed=2 * (weight.size + 2 * acts.size + 10 * blocks[0].size),
+            bytes_accessed=2 * (weight.size + 2 * acts.size + 10 * tokens.size),
             transcendentals=0,
         ),
         name="hidden_and_products",
-    )(place, *blocks, weight, acts)
-
-
-def rows_kernel(local_experts, total_experts, capacity, widths, place, *refs):
-    blocks = refs[:8]
-    outs = refs[8:]
+    )(place, *flat, weight, acts, *after, *through)
+
+
+def rows_kernel(
+    local_experts, total_experts, capacity, widths, counts, n_after, place, *refs
+):
+    n_blocks = sum(counts)
+    blocks = join_blocks(refs[:n_blocks], counts)
+    beyond, outer = refs[n_blocks + n_after :]
+    targets = ((beyond, 0), (beyond, 8 * capacity), (outer, 0))
     me = place[0]
     picker = pick_rows(me, local_experts, total_experts)
     for k in range(8):
-        base = pl.multiple_of((me ^ k) * capacity, 16)
         start = 0
-        for out, width in zip(outs, widths):
+        for (out, first), width in zip(targets, widths):
+            base = pl.multiple_of(first + (me ^ k) * capacity, 16)
 
             def store(e, column, step, value, base=base, out=out):
                 out[e, pl.ds(base, capacity), column : column + step] = value
@@ -243,33 +299,96 @@
             start += width + LANES
 
 
-def rows_call(place, blocks, widths, local_experts, total_experts, capacity):
-    kernel = functools.partial(rows_kernel, local_experts, total_experts, capacity, widths)
+def rows_call(place, blocks, widths, local_experts, total_experts, capacity, after):
+    kernel = functools.partial(
+        rows_kernel,
+        local_experts,
+        total_experts,
+        capacity,
+        widths,
+        counts_of(blocks),
+        len(after),
+    )
+    flat = split_blocks(blocks)
     slots = 8 * capacity
     vmem = pl.BlockSpec(memory_space=pltpu.VMEM)
     return pl.pallas_call(
         kernel,
-        in_specs=[pl.BlockSpec(memory_space=pltpu.SMEM)] + [vmem] * 8,
-        out_specs=[vmem] * len(widths),
-        out_shape=[jax.ShapeDtypeStruct((local_experts, slots, w), BF16) for w in widths],
+        in_specs=[pl.BlockSpec(memory_space=pltpu.SMEM)]
+        + [vmem] * len(flat)
+        + [ANYWHERE] * len(after),
+        out_specs=[vmem] * 2,
+        out_shape=[
+            pltpu.VMEM((local_experts, 2 * slots, widths[0]), BF16),
+            pltpu.VMEM((local_experts, slots, widths[2]), BF16),
+        ],
         compiler_params=pltpu.CompilerParams(vmem_limit_bytes=VMEM_LIMIT),
-        cost_estimate=pl.CostEstimate(
-            flops=2 * local_experts * slots * 256 * sum(widths),
-            bytes_accessed=2 * (8 * blocks[0].size + local_experts * slots * sum(widths)),
-            transcendentals=0,
-        ),
+        cost_estimate=SMALL,
         name="far_rows",
-    )(place, *blocks)
+    )(place, *flat, *after)
+
+
+def copy_kernel(moves, first_target, *refs):
+    targets = refs[first_target : first_target + len(moves)]
+    for target, pieces in zip(targets, moves):
+        for source, source_index, target_index in pieces:
+            target[target_index] = refs[source][source_index]
+
+
+def copies(name, sources, results, moves, after, through=()):
+    vmem = pl.BlockSpec(memory_space=pltpu.VMEM)
+    n_before = len(sources) + len(after)
+    return pl.pallas_call(
+        functools.partial(copy_kernel, moves, n_before + len(through)),
+        in_specs=[vmem] * len(sources) + [ANYWHERE] * (len(after) + len(through)),
+        out_specs=[vmem] * len(results) + [ANYWHERE] * len(through),
+        out_shape=[jax.ShapeDtypeStruct(shape, BF16) for shape in results]
+        + [jax.ShapeDtypeStruct(array.shape, array.dtype) for array in through],
+        input_output_aliases={n_before + i: len(results) + i for i in range(len(through))},
+        compiler_params=pltpu.CompilerParams(vmem_limit_bytes=VMEM_LIMIT),
+        cost_estimate=SMALL,
+        name=name,
+    )(*sources, *after, *through)
+
+
+def rows_of(start, stop):
+    return (slice(start, stop), slice(None))
+
+
+def columns_of(start, stop):
+    return (slice(None), slice(start, stop))
+
+
+def halves_of(across, along, after, through):
+    tokens, width = across.shape
+    half = tokens // 2
+    return copies(
+        "token_halves",
+        [across, along],
+        [(half, width)] * 2,
+        [
+            [(0, rows_of(0, half), Ellipsis)],
+            [(1, rows_of(half, tokens), Ellipsis)],
+        ],
+        after,
+        through,
+    )
 
 
 def outer_product(rows, acts):
     return lax.dot_general(rows, acts, (((0,), (0,)), ((), ())), preferred_element_type=F32)
 
 
-def down_kernel(near, inner, far, outer, near_a, inner_a, far_a, outer_a, own_ref, other_ref):
-    total = outer_product(near[0], near_a[...])
-    total += outer_product(inner[0], inner_a[...])
-    total += outer_product(far[0], far_a[...])
+def down_kernel(near, outer, beyond, near_a, outer_a, inner_a, far_a, *refs):
+    own_ref, other_ref = refs[-2:]
+    slots = near.shape[1]
+
+    def acts_of(ref):
+        return ref[0] if len(ref.shape) == 3 else ref[...]
+
+    total = outer_product(near[0], acts_of(near_a))
+    total += outer_product(beyond[0, :slots], acts_of(inner_a))
+    total += outer_product(beyond[0, slots:], acts_of(far_a))
 
     @pl.when(pl.program_id(0) == 0)
     def _():
@@ -277,49 +396,93 @@
 
     @pl.when(pl.program_id(0) == 1)
     def _():
-        own_ref[...] = total + outer_product(outer[0], outer_a[...])
-
-
-def down_call(expert, near, inner, far, outer, near_a, inner_a, far_a, outer_a):
-    slots, hidden_width = near_a.shape
+        own_ref[...] = (total + outer_product(outer[0], acts_of(outer_a))).astype(BF16)
+
+
+def down_call(expert, near, outer, beyond, acts, after):
+    slots = near.shape[1]
+    hidden_width = acts[0][0].shape[-1]
     part = outer.shape[2]
-    half = pl.BlockSpec((1, slots, part), lambda i: (expert, 0, 1 - i))
-    acts = pl.BlockSpec((slots, hidden_width), lambda i: (0, 0))
     result = pl.BlockSpec((part, hidden_width), lambda i: (0, 0))
+
+    def block_of(array, index):
+        if array.ndim == 3:
+            return pl.BlockSpec((1, slots, hidden_width), lambda i: (index, 0, 0))
+        return pl.BlockSpec((slots, hidden_width), lambda i: (index, 0))
+
     return pl.pallas_call(
         down_kernel,
         grid=(2,),
-        in_specs=[half, half, half, pl.BlockSpec((1, slots, part), lambda i: (expert, 0, 0))]
-        + [acts] * 4,
+        in_specs=[
+            pl.BlockSpec((1, slots, part), lambda i: (expert, 0, 1 - i)),
+            pl.BlockSpec((1, slots, part), lambda i: (expert, 0, 0)),
+            pl.BlockSpec((1, 2 * slots, part), lambda i: (expert, 0, 1 - i)),
+        ]
+        + [block_of(array, index) for array, index in acts]
+        + [ANYWHERE] * len(after),
         out_specs=[result, result],
+        out_shape=[jax.ShapeDtypeStruct((part, hidden_width), BF16)] * 2,
+        compiler_params=pltpu.CompilerParams(vmem_limit_bytes=VMEM_LIMIT),
+        cost_estimate=SMALL,
+        name="down_terms",
+    )(near, outer, beyond, *[array for array, _ in acts], *after)
+
+
+def router_kernel(total_experts, n_after, products, places, weights, gate, inputs, *refs):
+    input_ref, part_ref = refs[n_after:]
+    by_slot = products[...]
+    capacity = by_slot.shape[1]
+    slots = lax.broadcasted_iota(jnp.int32, (capacity, places.shape[1]), 0).astype(F32)
+    sums = []
+    for expert in range(total_experts):
+        hit = slots == places[expert : expert + 1, :]
+        sums.append(
+            jnp.sum(jnp.where(hit, by_slot[expert][:, None], 0.0), axis=0, keepdims=True)
+        )
+    pair_sums = jnp.concatenate(sums, axis=0)
+    logits = pair_sums - weights[...] * jnp.sum(pair_sums, axis=0, keepdims=True)
+    dense = jnp.where(places[...] >= 0.0, logits, 0.0).astype(BF16)
+    step = part_ref.shape[2]
+    for index in range(part_ref.shape[0]):
+        columns = inputs[:, index * step : (index + 1) * step]
+        part_ref[index] = jnp.dot(dense, columns, preferred_element_type=F32)
+    input_ref[...] = lax.dot_general(
+        dense, gate[...], (((0,), (0,)), ((), ())), preferred_element_type=F32
+    ).astype(BF16)
+
+
+def router_call(products, places, weights, gate, inputs, after):
+    vmem = pl.BlockSpec(memory_space=pltpu.VMEM)
+    return pl.pallas_call(
+        functools.partial(router_kernel, gate.shape[0], len(after)),
+        in_specs=[vmem] * 5 + [ANYWHERE] * len(after),
+        out_specs=[vmem] * 2,
         out_shape=[
-            jax.ShapeDtypeStruct((part, hidden_width), F32),
-            jax.ShapeDtypeStruct((part, hidden_width), BF16),
+            jax.ShapeDtypeStruct(inputs.shape, BF16),
+            jax.ShapeDtypeStruct((8, gate.shape[0], gate.shape[1] // 8), F32),
         ],
         compiler_params=pltpu.CompilerParams(vmem_limit_bytes=VMEM_LIMIT),
-        cost_estimate=pl.CostEstimate(
-            flops=2 * slots * hidden_width * 7 * part,
-            bytes_accessed=2 * (7 * slots * part + 4 * slots * hidden_width + 3 * part * hidden_width),
-            transcendentals=0,
-        ),
-        name="down_terms",
-    )(near, inner, far, outer, near_a, inner_a, far_a, outer_a)
-
-
-def sum_everywhere(x, member):
-    kept = []
-    for bits in (1, 2, 4):
-        half = x.shape[1] // 2
-        low, high = x[:, :half], x[:, half:]
-        upper = (member & bits) != 0
-        kept.append(upper)
-        x = jnp.where(upper, high, low) + plane_swap(jnp.where(upper, low, high), bits)
+        cost_estimate=SMALL,
+        name="router_terms",
+    )(products, places, weights, gate, inputs, *after)
+
+
+def sum_kernel(*refs):
+    own, first, second, third = refs[:4]
+    refs[-1][...] = (own[...] + first[...]) + (second[...] + third[...])
+
+
+def sum_planes(x, after):
     others = [lax.ppermute(x, "dp", [(i, i ^ k) for i in range(4)]) for k in (1, 2, 3)]
-    x = (x + others[0]) + (others[1] + others[2])
-    for bits, upper in zip((4, 2, 1), reversed(kept)):
-        other = plane_swap(x, bits)
-        x = jnp.concatenate([jnp.where(upper, other, x), jnp.where(upper, x, other)], axis=1)
-    return x
+    vmem = pl.BlockSpec(memory_space=pltpu.VMEM)
+    return pl.pallas_call(
+        sum_kernel,
+        in_specs=[vmem] * 4 + [ANYWHERE] * len(after),
+        out_specs=vmem,
+        out_shape=jax.ShapeDtypeStruct(x.shape, x.dtype),
+        cost_estimate=SMALL,
+        name="sum_planes",
+    )(x, *others, *after)
 
 
 def local_line(inputs, out_grad, combine, routes, saved_hidden, down_weight, router_weight):
@@ -347,49 +510,107 @@
     from_far = lax.ppermute(pair, "dp", FAR)
     from_outer = lax.ppermute(single, "dp", OUTER)
 
-    own_blocks = plane_gather(jnp.concatenate([out_grad, notes], axis=1))
-
-    inner_acts = []
-    outer_acts = []
-    far_acts = []
-    for expert in range(local_experts):
-        outer_acts.append(lax.ppermute(acts[expert], "dp", OUTER))
-        inner_acts.append(lax.ppermute(acts[expert], "dp", INNER))
-        far_acts.append(lax.ppermute(acts[expert], "dp", FAR))
-
-    other_blocks = plane_gather(jnp.concatenate([from_inner, from_far, from_outer], axis=1))
-
     other_part = jnp.where(lower, 0, 3)
     place = jnp.stack([member, plane, other_part]).astype(jnp.int32)
-    hidden, products, near = hidden_call(
-        place, own_blocks, down_weight, acts, total_experts, capacity, part
-    )
-
-    returned = lax.all_to_all(products, "expert", split_axis=1, concat_axis=1, tiled=True)
-    by_expert = returned.transpose(1, 0, 2).reshape(total_experts, capacity)
-    slot_order = jnp.arange(capacity, dtype=jnp.int32).astype(F32)
-    hit = positions[:, :, None] == slot_order[None, None, :]
-    pair_sums = jnp.sum(jnp.where(hit, by_expert[None], 0.0), axis=2)
-    logit_grad = pair_sums - weights * jnp.sum(pair_sums, axis=1, keepdims=True)
-    dense_grad = jnp.where(routed, logit_grad, 0.0).astype(BF16)
-    input_grad = jnp.dot(dense_grad, router_weight, preferred_element_type=F32).astype(BF16)
-    router_part = lax.dot_general(
-        dense_grad, inputs, (((0,), (0,)), ((), ())), preferred_element_type=F32
-    )
-    router_grad = sum_everywhere(router_part, member)
-
-    inner, far, outer = rows_call(
-        place, other_blocks, (2 * part, 2 * part, part), local_experts, total_experts, capacity
-    )
-    down = []
-    for expert in range(local_experts):
-        own, other = down_call(
-            expert, near, inner, far, outer,
-            acts[expert], inner_acts[expert], far_acts[expert], outer_acts[expert],
-        )
-        arrived = lax.ppermute(other, "dp", OUTWARD)
-        down.append((own + arrived.astype(F32)).astype(BF16))
-    down_grad = jnp.stack(down)
+
+    tokens = jnp.concatenate([out_grad, notes], axis=1)
+    across = plane_swap(tokens, 2)
+    along = plane_swap(tokens, 4)
+    n_tokens, wide = tokens.shape
+    half = n_tokens // 2
+    early = local_experts // 2
+    *halves, acts_early, acts_late = copies(
+        "first_pieces",
+        [across, along, acts],
+        [(half, wide)] * 2
+        + [(early, slots, hidden_width), (local_experts - early, slots, hidden_width)],
+        [
+            [(0, rows_of(0, half), Ellipsis)],
+            [(1, rows_of(half, n_tokens), Ellipsis)],
+            [(2, slice(0, early), Ellipsis)],
+            [(2, slice(early, local_experts), Ellipsis)],
+        ],
+        [from_inner, from_far, from_outer],
+    )
+    diagonal = plane_diagonal(halves)
+    own_blocks = plane_blocks(tokens, across, along, diagonal)
+    inner_early = lax.ppermute(acts_early, "dp", INNER)
+    outer_early = lax.ppermute(acts_early, "dp", OUTER)
+
+    widths = [block.shape[1] for block in (from_inner, from_far, from_outer)]
+    starts = [sum(widths[:i]) for i in range(3)]
+    (columns,) = copies(
+        "side_by_side",
+        [from_inner, from_far, from_outer],
+        [(n_tokens, sum(widths))],
+        [[(i, Ellipsis, columns_of(starts[i], starts[i] + widths[i])) for i in range(3)]],
+        diagonal,
+    )
+    columns_across = plane_swap(columns, 2)
+    columns_along = plane_swap(columns, 4)
+
+    hidden, products, near, acts_late = hidden_call(
+        place, own_blocks, down_weight, acts, total_experts, capacity, part, [columns],
+        [acts_late],
+    )
+    outer_late = lax.ppermute(acts_late, "dp", OUTER)
+
+    *column_halves, outer_early = halves_of(
+        columns_across, columns_along, [hidden, inner_early], [outer_early]
+    )
+    far_early = lax.ppermute(outer_early, "dp", INNER)
+    other_blocks = plane_blocks(
+        columns, columns_across, columns_along, plane_diagonal(column_halves)
+    )
+    returned = lax.all_to_all(
+        products.transpose(1, 0, 2), "expert", split_axis=0, concat_axis=0
+    ).reshape(total_experts, LANES)
+    beyond, outer = rows_call(
+        place, other_blocks, (2 * part, 2 * part, part), local_experts, total_experts, capacity,
+        [returned],
+    )
+
+    cut = hidden_width // 2
+    chunks = [(2, 0, hidden_width), (3, 0, cut), (3, cut, hidden_width)]
+    homes = copies(
+        "home_acts",
+        [acts_late, outer_late],
+        [(2 * slots, stop - start) for _, start, stop in chunks],
+        [
+            [
+                (source, (expert - early, slice(None), slice(start, stop)), rows_of(source * slots, (source + 1) * slots))
+                for source in range(2)
+            ]
+            for expert, start, stop in chunks
+        ],
+        [outer, far_early],
+    )
+    beyonds = [lax.ppermute(home, "dp", INNER) for home in homes]
+
+    def down(expert, pieces, after):
+        own, other = down_call(expert, near, outer, beyond, pieces, after)
+        return own, lax.ppermute(other, "dp", OUTWARD)
+
+    downs = []
+    for expert in range(early):
+        pieces = [(a, expert) for a in (acts_early, outer_early, inner_early, far_early)]
+        downs.append(down(expert, pieces, list(homes) + [own for own, _ in downs]))
+    input_grad, router_part = router_call(
+        returned, positions.T, weights.T, router_weight, inputs, [downs[-1][0]]
+    )
+    reduced = jnp.sum(
+        lax.all_to_all(router_part, "expert", split_axis=0, concat_axis=0), axis=0
+    )
+    for index, (expert, start, stop) in enumerate(chunks):
+        pieces = [(homes[index], 0), (homes[index], 1), (beyonds[index], 0), (beyonds[index], 1)]
+        downs.append(down(expert, pieces, [downs[-1][0], downs[-2][1], reduced]))
+    summed = sum_planes(reduced, [downs[-1][0]])
+    router_grad = (
+        lax.all_gather(summed, "expert").transpose(1, 0, 2).reshape(total_experts, width)
+    )
+
+    finished = [(own.astype(F32) + came.astype(F32)).astype(BF16) for own, came in downs]
+    down_grad = jnp.stack(finished[:3] + [jnp.concatenate(finished[3:], axis=1)])
 
     hidden_grad = hidden.reshape(saved_hidden.shape)
     return (hidden_grad, down_grad, input_grad, router_grad)

time: 258 us -> 201 us (0.78)
  waiting for transfers between devices: 112 us -> 30.8 us
  blocking collectives: 0 us -> 25.8 us
  starting transfers between devices: 69.5 us -> 53.8 us
  local copies, waits for them, and re-layouts: 10.1 us -> 20.8 us
  Pallas kernels: 54.8 us -> 57.5 us
    ppermute x19 -> x15, waiting for transfers between devices: 63.4 us -> 10 us  [the longest x5 10 us: down(): return (own, lax.ppermute(other, 'dp', OUTWARD))]
    ppermute x22 -> x18, waiting for transfers between devices: 45.1 us -> 15.4 us  [plane_swap(): return lax.ppermute(x, 'expert', [(i, i ^ bits) for i in range(8)])]
    all_to_all x0 -> x2, blocking collectives: none -> 17.1 us  [the longest x1 9.33 us: local_line(): lax.all_to_all(router_part, 'expert', split_axis=0, concat_axis=0)]
    unnamed x68 -> x96, local copies, waits for them, and re-layouts: 5.21 us -> 20.1 us
    all_gather x0 -> x1, blocking collectives: none -> 8.66 us  [local_line(): lax.all_gather(summed, 'expert').transpose(1, 0, 2)]
    ppermute x19 -> x15, starting transfers between devices: 42.1 us -> 34.1 us  [the longest x1 10.6 us: local_line(): outer_early = lax.ppermute(acts_early, 'dp', OUTER)]
    pallas_call x4 -> x11, Pallas kernels: 29 us -> 35.6 us  [the longest x5 26 us: down_call(): pl.pallas_call(down_kernel, grid=(2,), in_specs=[pl.BlockSpec((1, slots,...]
    ppermute x1, waiting for transfers between devices: 0.01 us -> 5.34 us  [local_line(): from_far = lax.ppermute(pair, 'dp', FAR)]
  transfers between devices with their start and end apart: 45 -> 36, of which waited for: 17 -> 8; matrix products, arithmetic and copies ran while one was open for 5% -> 3% of each run, Pallas kernels for 21% -> 28%
where the time goes in v2:
time: 201 us; the launch traced here: 200 us
  Pallas kernels  57.5 us (29%)
  starting transfers between devices  53.8 us (27%)
  waiting for transfers between devices  30.8 us (15%)
  blocking collectives  25.8 us (13%)
  local copies, waits for them, and re-layouts  20.8 us (10%)
  other arithmetic  8.87 us (4%)
    pallas_call x5, Pallas kernels, down_call(): pl.pallas_call(down_kernel, grid=(2,), in_specs=[pl.BlockSpec((1, slots,...  26 us
    unnamed x96, local copies, waits for them, and re-layouts  20.1 us
    ppermute x18, waiting for transfers between devices, plane_swap(): return lax.ppermute(x, 'expert', [(i, i ^ bits) for i in range(8)])  15.4 us
    pallas_call x1, Pallas kernels, hidden_call(): pl.pallas_call(kernel, grid_spec=pltpu.PrefetchScalarGridSpec(num_scalar_...  13.7 us
    ppermute x18, starting transfers between devices, plane_swap(): return lax.ppermute(x, 'expert', [(i, i ^ bits) for i in range(8)])  11.6 us
    ppermute x1, starting transfers between devices, local_line(): outer_early = lax.ppermute(acts_early, 'dp', OUTER)  10.6 us
    ppermute x3, starting transfers between devices, sum_planes(): lax.ppermute(x, 'dp', [(i, i ^ k) for i in range(4)])  10.2 us
    ppermute x5, waiting for transfers between devices, down(): return (own, lax.ppermute(other, 'dp', OUTWARD))  10 us
  transfers between devices with their start and end apart: 36, of which 8 were waited for; matrix products, arithmetic and copies ran while one was open for 3% of the time, Pallas kernels for 28%

profile of v2, /device:TPU:0, one launch (start us, length us, event | category | flops | bytes accessed | tf_op | source)
XLA Modules:
  0.0 199.5 jit_solution(6470312538855215932)
XLA Ops:
  3.3 3.0 %collective-permute-start.1 = (bf16[128,2176]{1,0:T(8,128)(2,1)S(1)}, bf16[128,2176]{1,0:T(8,128)(2,1)}, u32[]{:S(2)}, u32[]{:S(2)}) collective-permute-start(bf16[128,2176]{1,0:T(8,128)(2,1)S(1)} %pad_maximum_fusion.1.refs_0_), channel_id=1, source_target_pairs={{0,2},{1,3},{2,0},{3,1},{4,6},{5,7},{6,4},{7,5},{8,10},{9,11},{10,... | collective-permute-start | bytes 1671176 | tf_op jit(solution)/shard_map/ppermute | solution.py:95
  7.9 3.5 %collective-permute-start.7 = (bf16[128,640]{1,0:T(8,128)(2,1)S(1)}, bf16[128,640]{1,0:T(8,128)(2,1)S(1)}, u32[]{:S(2)}, u32[]{:S(2)}) collective-permute-start(bf16[128,640]{1,0:T(8,128)(2,1)S(1)} %pad_maximum_fusion.3), channel_id=1, source_target_pairs={{0,8},{24,16},{1,9},{25,17},{2,10},{26,18},{3,11},{27,19},{4,12},{... | collective-permute-start | bytes 491528 | tf_op jit(solution)/shard_map/ppermute | solution.py:511
  12.1 4.0 %collective-permute-start.6 = (bf16[128,1152]{1,0:T(8,128)(2,1)S(1)}, bf16[128,1152]{1,0:T(8,128)(2,1)S(1)}, u32[]{:S(2)}, u32[]{:S(2)}) collective-permute-start(bf16[128,1152]{1,0:T(8,128)(2,1)S(1)} %pad_maximum_fusion.2), channel_id=1, source_target_pairs={{0,16},{24,8},{1,17},{25,9},{2,18},{26,10},{3,19},{27,11},{4,20},{... | collective-permute-start | bytes 884744 | tf_op jit(solution)/shard_map/ppermute | solution.py:510
  16.2 5.3 %collective-permute-done.6.refs_4_.refs_1_ = bf16[128,1152]{1,0:T(8,128)(2,1)S(1)} collective-permute-done((bf16[128,1152]{1,0:T(8,128)(2,1)S(1)}, bf16[128,1152]{1,0:T(8,128)(2,1)S(1)}, u32[]{:S(2)}, u32[]{:S(2)}) %collective-permute-start.6) | collective-permute-done | bytes 294944 | tf_op jit(solution)/shard_map/ppermute | solution.py:510
  21.6 2.2 %first_pieces.1 = (bf16[64,2176]{1,0:T(8,128)(2,1)S(1)}, bf16[64,2176]{1,0:T(8,128)(2,1)S(1)}, bf16[2,384,768]{2,1,0:T(8,128)(2,1)S(1)}, bf16[2,384,768]{2,1,0:T(8,128)(2,1)S(1)}) custom-call(bf16[128,2176]{1,0:T(8,128)(2,1)} %collective-permute-done.1.refs_0_.refs_2_, bf16[128,2176]{1,0:T(8,128)(2,1)S(1)} %collective-permute-done.3.refs_1_.refs_4_, ...), custom_call_target="tpu_custom_call" | custom-call | flops 1000 | bytes 1000 | tf_op jit(solution)/shard_map/first_pieces/pallas_call | solution.py:341
  25.9 5.6 %collective-permute-done.8.refs_3_.refs_6_ = bf16[64,2176]{1,0:T(8,128)(2,1)S(1)} collective-permute-done((bf16[64,2176]{1,0:T(8,128)(2,1)S(1)}, bf16[64,2176]{1,0:T(8,128)(2,1)S(1)}, u32[]{:S(2)}, u32[]{:S(2)}) %collective-permute-start.8) | collective-permute-done | bytes 278560 | tf_op jit(solution)/shard_map/ppermute | solution.py:95
  33.6 10.6 %collective-permute-start.18 = (bf16[2,384,768]{2,1,0:T(8,128)(2,1)S(1)}, bf16[2,384,768]{2,1,0:T(8,128)(2,1)S(1)}, u32[]{:S(2)}, u32[]{:S(2)}) collective-permute-start(bf16[2,384,768]{2,1,0:T(8,128)(2,1)S(1)} %get-tuple-element.37.near_a), channel_id=1, source_target_pairs={{0,8},{24,16},{1,9},{25,17},{2,10},{26,18},{3,11},{27,19},{4,12},{... | collective-permute-start | bytes 3538952 | tf_op jit(solution)/shard_map/ppermute | solution.py:538
  54.6 13.7 %hidden_and_products.1 = (bf16[4,384,768]{2,1,0:T(8,128)(2,1)}, f32[4,8,128]{2,1,0:T(8,128)S(1)}, bf16[4,384,1024]{2,1,0:T(8,128)(2,1)S(1)}, bf16[2,384,768]{2,1,0:T(8,128)(2,1)}) custom-call(s32[3]{0:T(128)S(1)} %pad_add_fusion.place, bf16[128,2176]{1,0:T(8,128)(2,1)S(1)} %copy-done.18, ...), custom_call_target="tpu_custom_call", output_to_operand_aliasing={{3}: (14, {})} | custom-call | flops 6442450944 | bytes 22872064 | tf_op jit(solution)/shard_map/hidden_and_products/pallas_call | solution.py:245
  77.3 7.9 %collective-permute-done.19.refs_6_ = bf16[64,2944]{1,0:T(8,128)(2,1)S(1)} collective-permute-done((bf16[64,2944]{1,0:T(8,128)(2,1)S(1)}, bf16[64,2944]{1,0:T(8,128)(2,1)S(1)}, u32[]{:S(2)}, u32[]{:S(2)}) %collective-permute-start.19) | collective-permute-done | bytes 376864 | tf_op jit(solution)/shard_map/ppermute | solution.py:95
  87.2 7.8 %all_to_all.10 = f32[8,4,128]{2,1,0:T(4,128)} all-to-all(f32[8,4,128]{2,1,0:T(4,128)S(1)} %copy.21), channel_id=1, replica_groups=mesh['dp'=4,'expert'=8] {'expert'}, dimensions={0} | all-to-all | bytes 32768 | tf_op jit(solution)/shard_map/all_to_all | solution.py:565
  96.6 8.2 %far_rows.1 = (bf16[4,768,1024]{2,1,0:T(8,128)(2,1)S(1)}, bf16[4,384,512]{2,1,0:T(8,128)(2,1)S(1)}) custom-call(s32[3]{0:T(128)} %copy-done.28, bf16[128,2944]{1,0:T(8,128)(2,1)} %side_by_side.1.refs_12_.refs_0_, bf16[128,2944]{1,0:T(8,128)(2,1)} %copy-done.38, bf16[128,2944]{1,0:T(8,128)(2,1)} %collective-permute-done.13.refs_0_.refs_2_, ...), custom_call_target="tpu_custom_call" | custom-call | flops 1000 | bytes 1000 | tf_op jit(solution)/shard_map/far_rows/pallas_call | solution.py:315
  104.8 2.6 %copy-done = bf16[4,768,1024]{2,1,0:T(8,128)(2,1)} copy-done((bf16[4,768,1024]{2,1,0:T(8,128)(2,1)}, bf16[4,768,1024]{2,1,0:T(8,128)(2,1)S(1)}, u32[]{:S(2)}) %copy-start) | copy-done | bytes 6291480
  111.8 6.2 %down_terms.5 = (bf16[512,768]{1,0:T(8,128)(2,1)S(1)}, bf16[512,768]{1,0:T(8,128)(2,1)}) custom-call(bf16[4,384,1024]{2,1,0:T(8,128)(2,1)} %copy-done.1, bf16[4,384,512]{2,1,0:T(8,128)(2,1)} %copy-done.2, bf16[4,768,1024]{2,1,0:T(8,128)(2,1)} %copy-done, bf16[2,384,768]{2,1,0:T(8,128)(2,1)S(1)} %get-tuple-element.37.near_a, ...), custom_call_target="tpu_custom_call" | custom-call | flops 1000 | bytes 1000 | tf_op jit(solution)/shard_map/down_terms/pallas_call | solution.py:413
  120.5 6.2 %down_terms.6 = (bf16[512,768]{1,0:T(8,128)(2,1)S(1)}, bf16[512,768]{1,0:T(8,128)(2,1)}) custom-call(bf16[4,384,1024]{2,1,0:T(8,128)(2,1)} %copy-done.1, bf16[4,384,512]{2,1,0:T(8,128)(2,1)} %copy-done.2, bf16[4,768,1024]{2,1,0:T(8,128)(2,1)} %copy-done, bf16[2,384,768]{2,1,0:T(8,128)(2,1)S(1)} %copy-done.7, ...), custom_call_target="tpu_custom_call" | custom-call | flops 1000 | bytes 1000 | tf_op jit(solution)/shard_map/down_terms/pallas_call | solution.py:413
  131.4 9.3 %all_to_all.11 = f32[8,32,256]{2,1,0:T(8,128)S(1)} all-to-all(f32[8,32,256]{2,1,0:T(8,128)S(1)} %get-tuple-element.52), channel_id=1, replica_groups=mesh['dp'=4,'expert'=8] {'expert'}, dimensions={0} | all-to-all | bytes 524288 | tf_op jit(solution)/shard_map/all_to_all | solution.py:602
  140.8 5.8 %down_terms.7 = (bf16[512,768]{1,0:T(8,128)(2,1)S(1)}, bf16[512,768]{1,0:T(8,128)(2,1)S(1)}) custom-call(bf16[4,384,1024]{2,1,0:T(8,128)(2,1)} %copy-done.1, bf16[4,384,512]{2,1,0:T(8,128)(2,1)} %copy-done.2, bf16[4,768,1024]{2,1,0:T(8,128)(2,1)} %copy-done, bf16[768,768]{1,0:T(8,128)(2,1)} %get-tuple-element.45.refs_0_.near_a.outer_a, ...), custom_call_target="tpu_custom_call" | custom-call | flops 1000 | bytes 1000 | tf_op jit(solution)/shard_map/down_terms/pallas_call | solution.py:413
  148.6 8.4 %collective-permute-start.33 = (f32[32,256]{1,0:T(8,128)S(1)}, f32[32,256]{1,0:T(8,128)S(1)}, u32[]{:S(2)}, u32[]{:S(2)}) collective-permute-start(f32[32,256]{1,0:T(8,128)S(1)} %reduce_sum.29.refs_2_.refs_0_), channel_id=1, source_target_pairs={{0,8},{8,0},{16,24},{24,16},{1,9},{9,1},{17,25},{25,17},{2,10},{10... | collective-permute-start | bytes 98312 | tf_op jit(solution)/shard_map/ppermute | solution.py:476
  157.6 3.9 %down_terms.8 = (bf16[512,384]{1,0:T(8,128)(2,1)S(1)}, bf16[512,384]{1,0:T(8,128)(2,1)S(1)}) custom-call(bf16[4,384,1024]{2,1,0:T(8,128)(2,1)} %copy-done.1, bf16[4,384,512]{2,1,0:T(8,128)(2,1)S(1)} %copy-done.3, bf16[4,768,1024]{2,1,0:T(8,128)(2,1)} %copy-done, bf16[768,384]{1,0:T(8,128)(2,1)S(1)} %get-tuple-element.46.refs_1_.near_a.outer_a, ...), custom_call_target="tpu_custom_call" | custom-call | flops 1000 | bytes 1000 | tf_op jit(solution)/shard_map/down_terms/pallas_call | solution.py:413
  162.8 2.3 %fusion = bf16[1,512,768]{2,1,0:T(8,128)(2,1)} fusion(bf16[512,768]{1,0:T(8,128)(2,1)} %collective-permute-done.25.refs_1_, bf16[512,768]{1,0:T(8,128)(2,1)S(1)} %copy-done.11), kind=kLoop, calls=%fused_computation.5 | loop fusion | flops 1572864 | bytes 2359296 | tf_op jit(solution)/shard_map/stack | solution.py:613
  165.1 2.3 %fusion.1 = bf16[1,512,768]{2,1,0:T(8,128)(2,1)} fusion(bf16[512,768]{1,0:T(8,128)(2,1)} %collective-permute-done.26.refs_1_, bf16[512,768]{1,0:T(8,128)(2,1)S(1)} %get-tuple-element.50.refs_0_), kind=kLoop, calls=%fused_computation.6 | loop fusion | flops 1572864 | bytes 2359296 | tf_op jit(solution)/shard_map/stack | solution.py:613
  169.1 6.7 %collective-permute-done.28.refs_1_ = bf16[512,768]{1,0:T(8,128)(2,1)S(1)} collective-permute-done((bf16[512,768]{1,0:T(8,128)(2,1)S(1)}, bf16[512,768]{1,0:T(8,128)(2,1)S(1)}, u32[]{:S(2)}, u32[]{:S(2)}) %collective-permute-start.28) | collective-permute-done | bytes 786464 | tf_op jit(solution)/shard_map/ppermute | solution.py:592
  175.8 3.9 %down_terms.9 = (bf16[512,384]{1,0:T(8,128)(2,1)S(1)}, bf16[512,384]{1,0:T(8,128)(2,1)S(1)}) custom-call(bf16[4,384,1024]{2,1,0:T(8,128)(2,1)} %copy-done.1, bf16[4,384,512]{2,1,0:T(8,128)(2,1)S(1)} %copy-done.3, bf16[4,768,1024]{2,1,0:T(8,128)(2,1)} %copy-done, bf16[768,384]{1,0:T(8,128)(2,1)S(1)} %get-tuple-element.47.refs_2_.near_a.outer_a, ...), custom_call_target="tpu_custom_call" | custom-call | flops 1000 | bytes 1000 | tf_op jit(solution)/shard_map/down_terms/pallas_call | solution.py:413
  181.9 2.7 %collective-permute-done.30 = bf16[512,384]{1,0:T(8,128)(2,1)S(1)} collective-permute-done((bf16[512,384]{1,0:T(8,128)(2,1)S(1)}, bf16[512,384]{1,0:T(8,128)(2,1)S(1)}, u32[]{:S(2)}, u32[]{:S(2)}) %collective-permute-start.30) | collective-permute-done | bytes 393248 | tf_op jit(solution)/shard_map/ppermute | solution.py:592
  186.7 8.7 %all-gather = f32[256,256]{1,0:T(8,128)S(1)} all-gather(f32[32,256]{1,0:T(8,128)} %sum_planes.1), channel_id=2, replica_groups=mesh['dp'=4,'expert'=8] {'expert'}, dimensions={0}, use_global_device_ids=true | all-gather | bytes 294912 | tf_op jit(solution)/shard_map/all_gather | solution.py:609
  (179 shorter events, 57.5 us)
Async XLA Ops:
  3.3 18.2 %collective-permute-start.1 = (bf16[128,2176]{1,0:T(8,128)(2,1)S(1)}, bf16[128,2176]{1,0:T(8,128)(2,1)}, u32[]{:S(2)}, u32[]{:S(2)}) collective-permute-start(bf16[128,2176]{1,0:T(8,128)(2,1)S(1)} %pad_maximum_fusion.1.refs_0_), channel_id=1, source_target_pairs={{0,2},{1,3},{2,0},{3,1},{4,6},{5,7},{6,4},{7,5},{8,10},{9,11},{10,... | collective-permute-start | bytes 1671176 | tf_op jit(solution)/shard_map/ppermute | solution.py:95
  6.3 15.2 %collective-permute-start.3 = (bf16[128,2176]{1,0:T(8,128)(2,1)S(1)}, bf16[128,2176]{1,0:T(8,128)(2,1)S(1)}, u32[]{:S(2)}, u32[]{:S(2)}) collective-permute-start(bf16[128,2176]{1,0:T(8,128)(2,1)S(1)} %pad_maximum_fusion.1.refs_0_), channel_id=1, source_target_pairs={{0,4},{1,5},{2,6},{3,7},{4,0},{5,1},{6,2},{7,3},{8,12},{9,13},{10,... | collective-permute-start | bytes 1671176 | tf_op jit(solution)/shard_map/ppermute | solution.py:95
  16.1 16.7 %collective-permute-start = (bf16[128,2176]{1,0:T(8,128)(2,1)S(1)}, bf16[128,2176]{1,0:T(8,128)(2,1)S(1)}, u32[]{:S(2)}, u32[]{:S(2)}) collective-permute-start(bf16[128,2176]{1,0:T(8,128)(2,1)S(1)} %pad_maximum_fusion.1.refs_0_), channel_id=1, source_target_pairs={{0,1},{1,0},{2,3},{3,2},{4,5},{5,4},{6,7},{7,6},{8,9},{9,8},{10,11... | collective-permute-start | bytes 1671176 | tf_op jit(solution)/shard_map/ppermute | solution.py:95
  25.4 18.9 %collective-permute-start.9 = (bf16[64,2176]{1,0:T(8,128)(2,1)S(1)}, bf16[64,2176]{1,0:T(8,128)(2,1)S(1)}, u32[]{:S(2)}, u32[]{:S(2)}) collective-permute-start(bf16[64,2176]{1,0:T(8,128)(2,1)S(1)} %get-tuple-element.33), channel_id=1, source_target_pairs={{0,2},{1,3},{2,0},{3,1},{4,6},{5,7},{6,4},{7,5},{8,10},{9,11},{10,... | collective-permute-start | bytes 835592 | tf_op jit(solution)/shard_map/ppermute | solution.py:95
  31.5 12.8 %collective-permute-start.10 = (bf16[64,2176]{1,0:T(8,128)(2,1)S(1)}, bf16[64,2176]{1,0:T(8,128)(2,1)S(1)}, u32[]{:S(2)}, u32[]{:S(2)}) collective-permute-start(bf16[64,2176]{1,0:T(8,128)(2,1)S(1)} %collective-permute-done.8.refs_3_.refs_6_), channel_id=1, source_target_pairs={{0,1},{1,0},{2,3},{3,2},{4,5},{5,4},{6,7},{7,6},{8,9},{9,8},{10,11... | collective-permute-start | bytes 835592 | tf_op jit(solution)/shard_map/ppermute | solution.py:95
  31.5 16.5 %collective-permute-start.2 = (bf16[128,2176]{1,0:T(8,128)(2,1)}, bf16[128,2176]{1,0:T(8,128)(2,1)}, u32[]{:S(2)}, u32[]{:S(2)}) collective-permute-start(bf16[128,2176]{1,0:T(8,128)(2,1)} %collective-permute-done.1.refs_0_.refs_2_), channel_id=1, source_target_pairs={{0,1},{1,0},{2,3},{3,2},{4,5},{5,4},{6,7},{7,6},{8,9},{9,8},{10,11... | collective-permute-start | bytes 1671176 | tf_op jit(solution)/shard_map/ppermute | solution.py:95
  32.1 39.3 %collective-permute-start.17 = (bf16[2,384,768]{2,1,0:T(8,128)(2,1)S(1)}, bf16[2,384,768]{2,1,0:T(8,128)(2,1)S(1)}, u32[]{:S(2)}, u32[]{:S(2)}) collective-permute-start(bf16[2,384,768]{2,1,0:T(8,128)(2,1)S(1)} %get-tuple-element.37.near_a), channel_id=1, source_target_pairs={{8,16},{16,8},{9,17},{17,9},{10,18},{18,10},{11,19},{19,11},{12,20... | collective-permute-start | bytes 3538952 | tf_op jit(solution)/shard_map/ppermute | solution.py:537
  33.6 37.8 %collective-permute-start.18 = (bf16[2,384,768]{2,1,0:T(8,128)(2,1)S(1)}, bf16[2,384,768]{2,1,0:T(8,128)(2,1)S(1)}, u32[]{:S(2)}, u32[]{:S(2)}) collective-permute-start(bf16[2,384,768]{2,1,0:T(8,128)(2,1)S(1)} %get-tuple-element.37.near_a), channel_id=1, source_target_pairs={{0,8},{24,16},{1,9},{25,17},{2,10},{26,18},{3,11},{27,19},{4,12},{... | collective-permute-start | bytes 3538952 | tf_op jit(solution)/shard_map/ppermute | solution.py:538
  47.5 22.5 %collective-permute-start.13 = (bf16[128,2944]{1,0:T(8,128)(2,1)}, bf16[128,2944]{1,0:T(8,128)(2,1)}, u32[]{:S(2)}, u32[]{:S(2)}) collective-permute-start(bf16[128,2944]{1,0:T(8,128)(2,1)} %side_by_side.1.refs_12_.refs_0_), channel_id=1, source_target_pairs={{0,2},{1,3},{2,0},{3,1},{4,6},{5,7},{6,4},{7,5},{8,10},{9,11},{10,... | collective-permute-start | bytes 2261000 | tf_op jit(solution)/shard_map/ppermute | solution.py:95
  48.0 23.3 %collective-permute-start.15 = (bf16[128,2944]{1,0:T(8,128)(2,1)}, bf16[128,2944]{1,0:T(8,128)(2,1)}, u32[]{:S(2)}, u32[]{:S(2)}) collective-permute-start(bf16[128,2944]{1,0:T(8,128)(2,1)} %side_by_side.1.refs_12_.refs_0_), channel_id=1, source_target_pairs={{0,4},{1,5},{2,6},{3,7},{4,0},{5,1},{6,2},{7,3},{8,12},{9,13},{10,... | collective-permute-start | bytes 2261000 | tf_op jit(solution)/shard_map/ppermute | solution.py:95
  48.6 27.2 %collective-permute-start.12 = (bf16[128,2944]{1,0:T(8,128)(2,1)}, bf16[128,2944]{1,0:T(8,128)(2,1)S(1)}, u32[]{:S(2)}, u32[]{:S(2)}) collective-permute-start(bf16[128,2944]{1,0:T(8,128)(2,1)} %side_by_side.1.refs_12_.refs_0_), channel_id=1, source_target_pairs={{0,1},{1,0},{2,3},{3,2},{4,5},{5,4},{6,7},{7,6},{8,9},{9,8},{10,11... | collective-permute-start | bytes 2261000 | tf_op jit(solution)/shard_map/ppermute | solution.py:95
  70.0 38.6 %collective-permute-start.24 = (bf16[2,384,768]{2,1,0:T(8,128)(2,1)}, bf16[2,384,768]{2,1,0:T(8,128)(2,1)S(1)}, u32[]{:S(2)}, u32[]{:S(2)}) collective-permute-start(bf16[2,384,768]{2,1,0:T(8,128)(2,1)} %get-tuple-element.44.refs_0_), channel_id=1, source_target_pairs={{0,8},{24,16},{1,9},{25,17},{2,10},{26,18},{3,11},{27,19},{4,12},{... | collective-permute-start | bytes 3538952 | tf_op jit(solution)/shard_map/ppermute | solution.py:556
  73.2 35.4 %collective-permute-start.23 = (bf16[2,384,768]{2,1,0:T(8,128)(2,1)S(1)}, bf16[2,384,768]{2,1,0:T(8,128)(2,1)S(1)}, u32[]{:S(2)}, u32[]{:S(2)}) collective-permute-start(bf16[2,384,768]{2,1,0:T(8,128)(2,1)S(1)} %get-tuple-element.43.outer_a), channel_id=1, source_target_pairs={{8,16},{16,8},{9,17},{17,9},{10,18},{18,10},{11,19},{19,11},{12,20... | collective-permute-start | bytes 3538952 | tf_op jit(solution)/shard_map/ppermute | solution.py:561
  110.0 30.7 %collective-permute-start.27 = (bf16[768,768]{1,0:T(8,128)(2,1)}, bf16[768,768]{1,0:T(8,128)(2,1)}, u32[]{:S(2)}, u32[]{:S(2)}) collective-permute-start(bf16[768,768]{1,0:T(8,128)(2,1)} %get-tuple-element.45.refs_0_.near_a.outer_a), channel_id=1, source_target_pairs={{8,16},{16,8},{9,17},{17,9},{10,18},{18,10},{11,19},{19,11},{12,20... | collective-permute-start | bytes 3538952 | tf_op jit(solution)/shard_map/ppermute | solution.py:588
  118.0 22.8 %collective-permute-start.25 = (bf16[512,768]{1,0:T(8,128)(2,1)}, bf16[512,768]{1,0:T(8,128)(2,1)}, u32[]{:S(2)}, u32[]{:S(2)}) collective-permute-start(bf16[512,768]{1,0:T(8,128)(2,1)} %get-tuple-element.49), channel_id=1, source_target_pairs={{8,0},{16,24},{9,1},{17,25},{10,2},{18,26},{11,3},{19,27},{12,4},{... | collective-permute-start | bytes 2359304 | tf_op jit(solution)/shard_map/ppermute | solution.py:592
  126.8 30.8 %collective-permute-start.26 = (bf16[512,768]{1,0:T(8,128)(2,1)}, bf16[512,768]{1,0:T(8,128)(2,1)}, u32[]{:S(2)}, u32[]{:S(2)}) collective-permute-start(bf16[512,768]{1,0:T(8,128)(2,1)} %get-tuple-element.51), channel_id=1, source_target_pairs={{8,0},{16,24},{9,1},{17,25},{10,2},{18,26},{11,3},{19,27},{12,4},{... | collective-permute-start | bytes 2359304 | tf_op jit(solution)/shard_map/ppermute | solution.py:592
  128.1 28.9 %collective-permute-start.29 = (bf16[768,384]{1,0:T(8,128)(2,1)S(1)}, bf16[768,384]{1,0:T(8,128)(2,1)}, u32[]{:S(2)}, u32[]{:S(2)}) collective-permute-start(bf16[768,384]{1,0:T(8,128)(2,1)S(1)} %get-tuple-element.46.refs_1_.near_a.outer_a), channel_id=1, source_target_pairs={{8,16},{16,8},{9,17},{17,9},{10,18},{18,10},{11,19},{19,11},{12,20... | collective-permute-start | bytes 1769480 | tf_op jit(solution)/shard_map/ppermute | solution.py:588
  146.5 29.2 %collective-permute-start.28 = (bf16[512,768]{1,0:T(8,128)(2,1)S(1)}, bf16[512,768]{1,0:T(8,128)(2,1)S(1)}, u32[]{:S(2)}, u32[]{:S(2)}) collective-permute-start(bf16[512,768]{1,0:T(8,128)(2,1)S(1)} %get-tuple-element.54), channel_id=1, source_target_pairs={{8,0},{16,24},{9,1},{17,25},{10,2},{18,26},{11,3},{19,27},{12,4},{... | collective-permute-start | bytes 2359304 | tf_op jit(solution)/shard_map/ppermute | solution.py:592
  147.8 19.5 %collective-permute-start.31 = (bf16[768,384]{1,0:T(8,128)(2,1)S(1)}, bf16[768,384]{1,0:T(8,128)(2,1)S(1)}, u32[]{:S(2)}, u32[]{:S(2)}) collective-permute-start(bf16[768,384]{1,0:T(8,128)(2,1)S(1)} %get-tuple-element.47.refs_2_.near_a.outer_a), channel_id=1, source_target_pairs={{8,16},{16,8},{9,17},{17,9},{10,18},{18,10},{11,19},{19,11},{12,20... | collective-permute-start | bytes 1769480 | tf_op jit(solution)/shard_map/ppermute | solution.py:588
  148.6 36.1 %collective-permute-start.33 = (f32[32,256]{1,0:T(8,128)S(1)}, f32[32,256]{1,0:T(8,128)S(1)}, u32[]{:S(2)}, u32[]{:S(2)}) collective-permute-start(f32[32,256]{1,0:T(8,128)S(1)} %reduce_sum.29.refs_2_.refs_0_), channel_id=1, source_target_pairs={{0,8},{8,0},{16,24},{24,16},{1,9},{9,1},{17,25},{25,17},{2,10},{10... | collective-permute-start | bytes 98312 | tf_op jit(solution)/shard_map/ppermute | solution.py:476
  156.9 27.7 %collective-permute-start.34 = (f32[32,256]{1,0:T(8,128)S(1)}, f32[32,256]{1,0:T(8,128)S(1)}, u32[]{:S(2)}, u32[]{:S(2)}) collective-permute-start(f32[32,256]{1,0:T(8,128)S(1)} %reduce_sum.29.refs_2_.refs_0_), channel_id=1, source_target_pairs={{0,16},{8,24},{16,0},{24,8},{1,17},{9,25},{17,1},{25,9},{2,18},{10... | collective-permute-start | bytes 98312 | tf_op jit(solution)/shard_map/ppermute | solution.py:476
  161.5 23.1 %collective-permute-start.30 = (bf16[512,384]{1,0:T(8,128)(2,1)S(1)}, bf16[512,384]{1,0:T(8,128)(2,1)S(1)}, u32[]{:S(2)}, u32[]{:S(2)}) collective-permute-start(bf16[512,384]{1,0:T(8,128)(2,1)S(1)} %get-tuple-element.56), channel_id=1, source_target_pairs={{8,0},{16,24},{9,1},{17,25},{10,2},{18,26},{11,3},{19,27},{12,4},{... | collective-permute-start | bytes 1179656 | tf_op jit(solution)/shard_map/ppermute | solution.py:592
  167.3 17.4 %collective-permute-start.35 = (f32[32,256]{1,0:T(8,128)S(1)}, f32[32,256]{1,0:T(8,128)S(1)}, u32[]{:S(2)}, u32[]{:S(2)}) collective-permute-start(f32[32,256]{1,0:T(8,128)S(1)} %reduce_sum.29.refs_2_.refs_0_), channel_id=1, source_target_pairs={{0,24},{8,16},{16,8},{24,0},{1,25},{9,17},{17,9},{25,1},{2,26},{10... | collective-permute-start | bytes 98312 | tf_op jit(solution)/shard_map/ppermute | solution.py:476
  180.5 15.9 %collective-permute-start.32 = (bf16[512,384]{1,0:T(8,128)(2,1)S(1)}, bf16[512,384]{1,0:T(8,128)(2,1)S(1)}, u32[]{:S(2)}, u32[]{:S(2)}) collective-permute-start(bf16[512,384]{1,0:T(8,128)(2,1)S(1)} %get-tuple-element.58), channel_id=1, source_target_pairs={{8,0},{16,24},{9,1},{17,25},{10,2},{18,26},{11,3},{19,27},{12,4},{... | collective-permute-start | bytes 1179656 | tf_op jit(solution)/shard_map/ppermute | solution.py:592
  (60 other events, 479.0 us)

commit v3 on v2

--- a/solution.py
+++ b/solution.py
@@ -11,7 +11,8 @@
 BF16 = jnp.bfloat16
 LANES = 128
 KINDS = 4
-VMEM_LIMIT = 48 * 1024 * 1024
+MIB = 1024 * 1024
+VMEM_LIMIT = 51 * MIB
 ANYWHERE = pl.BlockSpec(memory_space=pl.ANY)
 SMALL = pl.CostEstimate(flops=1000, bytes_accessed=1000, transcendentals=0)
 
@@ -95,16 +96,18 @@
     return lax.ppermute(x, "expert", [(i, i ^ bits) for i in range(8)])
 
 
-def plane_blocks(x, across, along, diagonal):
+def plane_blocks(x, across, along, stacked, diagonal):
+    swapped = plane_swap(stacked, 1)
+    corner = [plane_swap(piece, 1) for piece in diagonal]
     return [
-        x,
-        plane_swap(x, 1),
-        across,
-        plane_swap(across, 1),
-        along,
-        plane_swap(along, 1),
-        diagonal,
-        tuple(plane_swap(piece, 1) for piece in diagonal),
+        [(x, None)],
+        [(swapped, 0)],
+        [(across, None)],
+        [(swapped, 1)],
+        [(along, None)],
+        [(swapped, 2)],
+        [(piece, None) for piece in diagonal],
+        [(piece, None) for piece in corner],
     ]
 
 
@@ -168,35 +171,35 @@
 
 
 def read_block(block, start, stop):
-    if isinstance(block, tuple):
-        return jnp.concatenate([half[:, start:stop] for half in block], axis=0)
-    return block[:, start:stop]
-
-
-def split_blocks(blocks):
-    flat = []
+    pieces = []
+    for ref, index in block:
+        pieces.append(ref[:, start:stop] if index is None else ref[index, :, start:stop])
+    return jnp.concatenate(pieces, axis=0) if len(pieces) > 1 else pieces[0]
+
+
+def arrays_of(blocks):
+    arrays = []
+    layout = []
     for block in blocks:
-        flat.extend(block if isinstance(block, tuple) else (block,))
-    return flat
-
-
-def join_blocks(refs, shapes):
-    refs = list(refs)
-    blocks = []
-    for count in shapes:
-        blocks.append(refs.pop(0) if count == 1 else (refs.pop(0), refs.pop(0)))
-    return blocks
-
-
-def counts_of(blocks):
-    return tuple(2 if isinstance(block, tuple) else 1 for block in blocks)
+        pieces = []
+        for array, index in block:
+            found = [i for i, known in enumerate(arrays) if known is array]
+            if not found:
+                arrays.append(array)
+                found = [len(arrays) - 1]
+            pieces.append((found[0], index))
+        layout.append(pieces)
+    return arrays, layout
+
+
+def blocks_of(refs, layout):
+    return [[(refs[place], index) for place, index in pieces] for pieces in layout]
 
 
 def hidden_kernel(
-    local_experts, total_experts, capacity, width, part, counts, n_after, place, *refs
+    local_experts, total_experts, capacity, width, part, n_blocks, layout, n_after, place, *refs
 ):
-    n_blocks = sum(counts)
-    blocks = join_blocks(refs[:n_blocks], counts)
+    blocks = blocks_of(refs[:n_blocks], layout)
     weight_ref, acts_ref = refs[n_blocks : n_blocks + 2]
     hidden_ref, products_ref, near_ref = refs[n_blocks + 2 + n_after :][:3]
     rows = refs[-1]
@@ -226,9 +229,14 @@
     near_ref[0, :, part:] = rows[expert, :, pl.ds(other, part)]
 
 
+def whole_block(shape):
+    return pl.BlockSpec(shape, lambda *_: (0,) * len(shape))
+
+
 def hidden_call(place, blocks, weight, acts, total_experts, capacity, part, after, through):
     local_experts, width, hidden_width = weight.shape
     slots = acts.shape[1]
+    flat, layout = arrays_of(blocks)
     kernel = functools.partial(
         hidden_kernel,
         local_experts,
@@ -236,10 +244,10 @@
         capacity,
         width,
         part,
-        counts_of(blocks),
+        len(flat),
+        layout,
         len(after) + len(through),
     )
-    flat = split_blocks(blocks)
     tokens = flat[0]
     n_before = 1 + len(flat) + 2 + len(after)
     return pl.pallas_call(
@@ -247,7 +255,7 @@
         grid_spec=pltpu.PrefetchScalarGridSpec(
             num_scalar_prefetch=1,
             grid=(local_experts,),
-            in_specs=[pl.BlockSpec(b.shape, lambda e, p: (0, 0)) for b in flat]
+            in_specs=[whole_block(b.shape) for b in flat]
             + [
                 pl.BlockSpec((1, width, hidden_width), lambda e, p: (e, 0, 0)),
                 pl.BlockSpec((1, slots, hidden_width), lambda e, p: (e, 0, 0)),
@@ -264,11 +272,11 @@
         out_shape=[
             jax.ShapeDtypeStruct((local_experts, slots, hidden_width), BF16),
             jax.ShapeDtypeStruct((local_experts, 8, LANES), F32),
-            pltpu.VMEM((local_experts, slots, 2 * part), BF16),
+            jax.ShapeDtypeStruct((local_experts, slots, 2 * part), BF16),
         ]
         + [jax.ShapeDtypeStruct(array.shape, array.dtype) for array in through],
         input_output_aliases={n_before + i: 3 + i for i in range(len(through))},
-        compiler_params=pltpu.CompilerParams(vmem_limit_bytes=VMEM_LIMIT),
+        compiler_params=pltpu.CompilerParams(vmem_limit_bytes=56 * MIB),
         cost_estimate=pl.CostEstimate(
             flops=2 * local_experts * slots * width * (hidden_width + 256),
             bytes_accessed=2 * (weight.size + 2 * acts.size + 10 * tokens.size),
@@ -279,51 +287,66 @@
 
 
 def rows_kernel(
-    local_experts, total_experts, capacity, widths, counts, n_after, place, *refs
+    local_experts, total_experts, capacity, widths, n_blocks, layout, n_after, place, *refs
 ):
-    n_blocks = sum(counts)
-    blocks = join_blocks(refs[:n_blocks], counts)
-    beyond, outer = refs[n_blocks + n_after :]
-    targets = ((beyond, 0), (beyond, 8 * capacity), (outer, 0))
+    blocks = blocks_of(refs[:n_blocks], layout)
+    outs = refs[n_blocks + n_after : n_blocks + n_after + local_experts]
+    rows, stored = refs[n_blocks + n_after + local_experts :]
+    slots = 8 * capacity
     me = place[0]
     picker = pick_rows(me, local_experts, total_experts)
-    for k in range(8):
-        start = 0
-        for (out, first), width in zip(targets, widths):
-            base = pl.multiple_of(first + (me ^ k) * capacity, 16)
-
-            def store(e, column, step, value, base=base, out=out):
-                out[e, pl.ds(base, capacity), column : column + step] = value
+    start = 0
+    stores = []
+    for index, width in enumerate(widths):
+        for k in range(8):
+            base = pl.multiple_of(index * slots + (me ^ k) * capacity, 16)
+
+            def store(e, column, step, value, base=base):
+                rows[e, pl.ds(base, capacity), column : column + step] = value
 
             place_rows(blocks[k], start, width, picker, local_experts, capacity, 512, store)
-            start += width + LANES
+        start += width + LANES
+        group = pl.ds(index * slots, slots)
+        for expert in range(local_experts):
+            held = rows.at[expert, group]
+            target = outs[expert].at[group]
+            stores.append(pltpu.make_async_copy(held, target, stored.at[index, expert]))
+            stores[-1].start()
+    for copy in stores:
+        copy.wait()
 
 
 def rows_call(place, blocks, widths, local_experts, total_experts, capacity, after):
+    flat, layout = arrays_of(blocks)
+    shape = (len(widths) * 8 * capacity, widths[0])
     kernel = functools.partial(
         rows_kernel,
         local_experts,
         total_experts,
         capacity,
         widths,
-        counts_of(blocks),
+        len(flat),
+        layout,
         len(after),
     )
-    flat = split_blocks(blocks)
-    slots = 8 * capacity
-    vmem = pl.BlockSpec(memory_space=pltpu.VMEM)
     return pl.pallas_call(
         kernel,
         in_specs=[pl.BlockSpec(memory_space=pltpu.SMEM)]
-        + [vmem] * len(flat)
+        + [pl.BlockSpec(memory_space=pltpu.VMEM)] * len(flat)
         + [ANYWHERE] * len(after),
-        out_specs=[vmem] * 2,
-        out_shape=[
-            pltpu.VMEM((local_experts, 2 * slots, widths[0]), BF16),
-            pltpu.VMEM((local_experts, slots, widths[2]), BF16),
+        out_specs=[pl.BlockSpec(memory_space=pltpu.VMEM)] + [ANYWHERE] * (local_experts - 1),
+        out_shape=[pltpu.VMEM(shape, BF16)]
+        + [jax.ShapeDtypeStruct(shape, BF16)] * (local_experts - 1),
+        scratch_shapes=[
+            pltpu.VMEM((local_experts, *shape), BF16),
+            pltpu.SemaphoreType.DMA((len(widths), local_experts)),
         ],
-        compiler_params=pltpu.CompilerParams(vmem_limit_bytes=VMEM_LIMIT),
-        cost_estimate=SMALL,
+        compiler_params=pltpu.CompilerParams(vmem_limit_bytes=56 * MIB),
+        cost_estimate=pl.CostEstimate(
+            flops=2 * local_experts * 8 * capacity * 256 * sum(widths),
+            bytes_accessed=2 * local_experts * shape[0] * shape[1],
+            transcendentals=0,
+        ),
         name="far_rows",
     )(place, *flat, *after)
 
@@ -335,20 +358,38 @@
             target[target_index] = refs[source][source_index]
 
 
-def copies(name, sources, results, moves, after, through=()):
+def copies(name, sources, results, moves, after, vmem_limit):
     vmem = pl.BlockSpec(memory_space=pltpu.VMEM)
-    n_before = len(sources) + len(after)
     return pl.pallas_call(
-        functools.partial(copy_kernel, moves, n_before + len(through)),
-        in_specs=[vmem] * len(sources) + [ANYWHERE] * (len(after) + len(through)),
-        out_specs=[vmem] * len(results) + [ANYWHERE] * len(through),
-        out_shape=[jax.ShapeDtypeStruct(shape, BF16) for shape in results]
-        + [jax.ShapeDtypeStruct(array.shape, array.dtype) for array in through],
-        input_output_aliases={n_before + i: len(results) + i for i in range(len(through))},
-        compiler_params=pltpu.CompilerParams(vmem_limit_bytes=VMEM_LIMIT),
+        functools.partial(copy_kernel, moves, len(sources) + len(after)),
+        in_specs=[vmem] * len(sources) + [ANYWHERE] * len(after),
+        out_specs=[vmem] * len(results),
+        out_shape=[jax.ShapeDtypeStruct(shape, BF16) for shape in results],
+        compiler_params=pltpu.CompilerParams(vmem_limit_bytes=vmem_limit),
+        cost_estimate=pl.CostEstimate(
+            flops=0,
+            bytes_accessed=4 * sum(array.size for array in sources),
+            transcendentals=0,
+        ),
+        name=name,
+    )(*sources, *after)
+
+
+def nothing_kernel(*_):
+    pass
+
+
+def held_until(arrays, after):
+    return pl.pallas_call(
+        nothing_kernel,
+        in_specs=[ANYWHERE] * (len(arrays) + len(after)),
+        out_specs=[ANYWHERE] * len(arrays),
+        out_shape=[jax.ShapeDtypeStruct(array.shape, array.dtype) for array in arrays],
+        input_output_aliases={i: i for i in range(len(arrays))},
+        compiler_params=pltpu.CompilerParams(has_side_effects=True),
         cost_estimate=SMALL,
-        name=name,
-    )(*sources, *after, *through)
+        name="held_until",
+    )(*arrays, *after)
 
 
 def rows_of(start, stop):
@@ -359,73 +400,64 @@
     return (slice(None), slice(start, stop))
 
 
-def halves_of(across, along, after, through):
-    tokens, width = across.shape
-    half = tokens // 2
-    return copies(
-        "token_halves",
-        [across, along],
-        [(half, width)] * 2,
-        [
-            [(0, rows_of(0, half), Ellipsis)],
-            [(1, rows_of(half, tokens), Ellipsis)],
-        ],
-        after,
-        through,
-    )
-
-
 def outer_product(rows, acts):
     return lax.dot_general(rows, acts, (((0,), (0,)), ((), ())), preferred_element_type=F32)
 
 
-def down_kernel(near, outer, beyond, near_a, outer_a, inner_a, far_a, *refs):
-    own_ref, other_ref = refs[-2:]
-    slots = near.shape[1]
-
-    def acts_of(ref):
-        return ref[0] if len(ref.shape) == 3 else ref[...]
-
-    total = outer_product(near[0], acts_of(near_a))
-    total += outer_product(beyond[0, :slots], acts_of(inner_a))
-    total += outer_product(beyond[0, slots:], acts_of(far_a))
-
-    @pl.when(pl.program_id(0) == 0)
-    def _():
-        other_ref[...] = total.astype(BF16)
-
-    @pl.when(pl.program_id(0) == 1)
-    def _():
-        own_ref[...] = (total + outer_product(outer[0], acts_of(outer_a))).astype(BF16)
-
-
-def down_call(expert, near, outer, beyond, acts, after):
-    slots = near.shape[1]
-    hidden_width = acts[0][0].shape[-1]
-    part = outer.shape[2]
-    result = pl.BlockSpec((part, hidden_width), lambda i: (0, 0))
-
-    def block_of(array, index):
-        if array.ndim == 3:
-            return pl.BlockSpec((1, slots, hidden_width), lambda i: (index, 0, 0))
-        return pl.BlockSpec((slots, hidden_width), lambda i: (index, 0))
-
+def down_kernel(places, n_after, rows, *refs):
+    sources = refs[:5]
+    own_ref, other_ref, near, acts, results, loaded, stored = refs[5 + n_after :]
+    slots, width = near.shape
+    part = width // 2
+    targets = [near] + [acts.at[pl.ds(i * slots, slots)] for i in range(4)]
+    loads = [
+        pltpu.make_async_copy(source.at[place], target, loaded.at[i])
+        for i, (source, place, target) in enumerate(zip(sources, places, targets))
+    ]
+    for load in loads:
+        load.start()
+    stores = [
+        pltpu.make_async_copy(results.at[i], target, stored.at[i])
+        for i, target in enumerate((other_ref, own_ref))
+    ]
+    for load in loads[:4]:
+        load.wait()
+    total = outer_product(near[:, part:], acts[:slots])
+    total += outer_product(rows[: 2 * slots, part:], acts[slots : 3 * slots])
+    results[0] = total.astype(BF16)
+    stores[0].start()
+    loads[4].wait()
+    total = outer_product(near[:, :part], acts[:slots])
+    total += outer_product(rows[:, :part], acts[slots:])
+    results[1] = total.astype(BF16)
+    stores[1].start()
+    for store in stores:
+        store.wait()
+
+
+def down_call(rows, near, acts, after):
+    sources = [near, *acts]
+    arrays = [array for array, _ in sources]
+    places = [place for _, place in sources]
+    slots, hidden_width = arrays[1].shape[1:]
+    width = rows.shape[1]
     return pl.pallas_call(
-        down_kernel,
-        grid=(2,),
-        in_specs=[
-            pl.BlockSpec((1, slots, part), lambda i: (expert, 0, 1 - i)),
-            pl.BlockSpec((1, slots, part), lambda i: (expert, 0, 0)),
-            pl.BlockSpec((1, 2 * slots, part), lambda i: (expert, 0, 1 - i)),
-        ]
-        + [block_of(array, index) for array, index in acts]
-        + [ANYWHERE] * len(after),
-        out_specs=[result, result],
-        out_shape=[jax.ShapeDtypeStruct((part, hidden_width), BF16)] * 2,
-        compiler_params=pltpu.CompilerParams(vmem_limit_bytes=VMEM_LIMIT),
+        functools.partial(down_kernel, places, len(after)),
+        in_specs=[pl.BlockSpec(memory_space=pltpu.VMEM)]
+        + [ANYWHERE] * (len(arrays) + len(after)),
+        out_specs=[ANYWHERE] * 2,
+        out_shape=[jax.ShapeDtypeStruct((width // 2, hidden_width), BF16)] * 2,
+        scratch_shapes=[
+            pltpu.VMEM((slots, width), BF16),
+            pltpu.VMEM((4 * slots, hidden_width), BF16),
+            pltpu.VMEM((2, width // 2, hidden_width), BF16),
+            pltpu.SemaphoreType.DMA((5,)),
+            pltpu.SemaphoreType.DMA((2,)),
+        ],
+        compiler_params=pltpu.CompilerParams(vmem_limit_bytes=50 * MIB),
         cost_estimate=SMALL,
         name="down_terms",
-    )(near, outer, beyond, *[array for array, _ in acts], *after)
+    )(pltpu.with_memory_space_constraint(rows, pltpu.VMEM), *arrays, *after)
 
 
 def router_kernel(total_experts, n_after, products, places, weights, gate, inputs, *refs):
@@ -461,7 +493,7 @@
             jax.ShapeDtypeStruct(inputs.shape, BF16),
             jax.ShapeDtypeStruct((8, gate.shape[0], gate.shape[1] // 8), F32),
         ],
-        compiler_params=pltpu.CompilerParams(vmem_limit_bytes=VMEM_LIMIT),
+        compiler_params=pltpu.CompilerParams(vmem_limit_bytes=24 * MIB),
         cost_estimate=SMALL,
         name="router_terms",
     )(products, places, weights, gate, inputs, *after)
@@ -472,8 +504,7 @@
     refs[-1][...] = (own[...] + first[...]) + (second[...] + third[...])
 
 
-def sum_planes(x, after):
-    others = [lax.ppermute(x, "dp", [(i, i ^ k) for i in range(4)]) for k in (1, 2, 3)]
+def sum_planes(x, others, after):
     vmem = pl.BlockSpec(memory_space=pltpu.VMEM)
     return pl.pallas_call(
         sum_kernel,
@@ -516,26 +547,31 @@
     tokens = jnp.concatenate([out_grad, notes], axis=1)
     across = plane_swap(tokens, 2)
     along = plane_swap(tokens, 4)
-    n_tokens, wide = tokens.shape
+    n_tokens = tokens.shape[0]
     half = n_tokens // 2
-    early = local_experts // 2
-    *halves, acts_early, acts_late = copies(
+
+    groups = [(0, 2), (2, local_experts)]
+    acts_early, *acts_late = copies(
+        "acts_pieces",
+        [acts],
+        [(stop - start, slots, hidden_width) for start, stop in groups],
+        [[(0, slice(start, stop), Ellipsis)] for start, stop in groups],
+        [across],
+        60 * MIB,
+    )
+    *halves, stacked = copies(
         "first_pieces",
-        [across, along, acts],
-        [(half, wide)] * 2
-        + [(early, slots, hidden_width), (local_experts - early, slots, hidden_width)],
-        [
-            [(0, rows_of(0, half), Ellipsis)],
-            [(1, rows_of(half, n_tokens), Ellipsis)],
-            [(2, slice(0, early), Ellipsis)],
-            [(2, slice(early, local_experts), Ellipsis)],
-        ],
-        [from_inner, from_far, from_outer],
+        [across, along, tokens],
+        [(half, tokens.shape[1])] * 2 + [(3, *tokens.shape)],
+        [[(0, rows_of(0, half), Ellipsis)], [(1, rows_of(half, n_tokens), Ellipsis)]]
+        + [[(source, Ellipsis, index) for index, source in enumerate((2, 0, 1))]],
+        [from_inner, from_far, from_outer, acts_early],
+        60 * MIB,
     )
     diagonal = plane_diagonal(halves)
-    own_blocks = plane_blocks(tokens, across, along, diagonal)
-    inner_early = lax.ppermute(acts_early, "dp", INNER)
-    outer_early = lax.ppermute(acts_early, "dp", OUTER)
+    own_blocks = plane_blocks(tokens, across, along, stacked, diagonal)
+    inners = [lax.ppermute(acts_early, "dp", INNER)]
+    outers = [lax.ppermute(acts_early, "dp", OUTER)]
 
     widths = [block.shape[1] for block in (from_inner, from_far, from_outer)]
     starts = [sum(widths[:i]) for i in range(3)]
@@ -545,72 +581,73 @@
         [(n_tokens, sum(widths))],
         [[(i, Ellipsis, columns_of(starts[i], starts[i] + widths[i])) for i in range(3)]],
         diagonal,
+        60 * MIB,
     )
     columns_across = plane_swap(columns, 2)
     columns_along = plane_swap(columns, 4)
 
-    hidden, products, near, acts_late = hidden_call(
-        place, own_blocks, down_weight, acts, total_experts, capacity, part, [columns],
-        [acts_late],
-    )
-    outer_late = lax.ppermute(acts_late, "dp", OUTER)
-
-    *column_halves, outer_early = halves_of(
-        columns_across, columns_along, [hidden, inner_early], [outer_early]
-    )
-    far_early = lax.ppermute(outer_early, "dp", INNER)
+    hidden, products, near, *late = hidden_call(
+        place, own_blocks, down_weight, acts, total_experts, capacity, part,
+        [columns], acts_late,
+    )
+    inners += [lax.ppermute(a, "dp", INNER) for a in late]
+    outers += [lax.ppermute(a, "dp", OUTER) for a in late]
+    fars = [lax.ppermute(outers[0], "dp", INNER)]
+    fars += [
+        lax.ppermute(outers[1][i : i + 1], "dp", INNER) for i in range(local_experts - 2)
+    ]
+
+    *column_halves, stacked = copies(
+        "second_pieces",
+        [columns_across, columns_along, columns],
+        [(half, sum(widths))] * 2 + [(3, *columns.shape)],
+        [[(0, rows_of(0, half), Ellipsis)], [(1, rows_of(half, n_tokens), Ellipsis)]]
+        + [[(source, Ellipsis, index) for index, source in enumerate((2, 0, 1))]],
+        [hidden, outers[0], inners[0]],
+        56 * MIB,
+    )
     other_blocks = plane_blocks(
-        columns, columns_across, columns_along, plane_diagonal(column_halves)
-    )
+        columns, columns_across, columns_along, stacked, plane_diagonal(column_halves)
+    )
+    rows = rows_call(
+        place, other_blocks, (2 * part, 2 * part, part), local_experts, total_experts, capacity, []
+    )
+
+    def down(expert, after, hold=()):
+        group, place = divmod(expert, 2)
+        far = (fars[0], expert) if expert < 2 else (fars[expert - 1], 0)
+        pieces = [(acts, expert), (inners[group], place), far, (outers[group], place)]
+        own, other = down_call(rows[expert], (near, expert), pieces, after)
+        if hold:
+            (other,) = held_until([other], hold)
+        return own, lax.ppermute(other, "dp", OUTWARD)
+
+    def finish(own, came):
+        return (own.astype(F32) + came.astype(F32)).astype(BF16)
+
+    downs = [down(0, [])]
+    downs.append(down(1, [downs[0][0]]))
     returned = lax.all_to_all(
         products.transpose(1, 0, 2), "expert", split_axis=0, concat_axis=0
     ).reshape(total_experts, LANES)
-    beyond, outer = rows_call(
-        place, other_blocks, (2 * part, 2 * part, part), local_experts, total_experts, capacity,
-        [returned],
-    )
-
-    cut = hidden_width // 2
-    chunks = [(2, 0, hidden_width), (3, 0, cut), (3, cut, hidden_width)]
-    homes = copies(
-        "home_acts",
-        [acts_late, outer_late],
-        [(2 * slots, stop - start) for _, start, stop in chunks],
-        [
-            [
-                (source, (expert - early, slice(None), slice(start, stop)), rows_of(source * slots, (source + 1) * slots))
-                for source in range(2)
-            ]
-            for expert, start, stop in chunks
-        ],
-        [outer, far_early],
-    )
-    beyonds = [lax.ppermute(home, "dp", INNER) for home in homes]
-
-    def down(expert, pieces, after):
-        own, other = down_call(expert, near, outer, beyond, pieces, after)
-        return own, lax.ppermute(other, "dp", OUTWARD)
-
-    downs = []
-    for expert in range(early):
-        pieces = [(a, expert) for a in (acts_early, outer_early, inner_early, far_early)]
-        downs.append(down(expert, pieces, list(homes) + [own for own, _ in downs]))
     input_grad, router_part = router_call(
-        returned, positions.T, weights.T, router_weight, inputs, [downs[-1][0]]
-    )
+        returned, positions.T, weights.T, router_weight, inputs, [downs[1][0]]
+    )
+    downs.append(down(2, [downs[1][0], inners[1], downs[0][1]]))
+    (router_part,) = held_until([router_part], [downs[2][0]])
     reduced = jnp.sum(
         lax.all_to_all(router_part, "expert", split_axis=0, concat_axis=0), axis=0
     )
-    for index, (expert, start, stop) in enumerate(chunks):
-        pieces = [(homes[index], 0), (homes[index], 1), (beyonds[index], 0), (beyonds[index], 1)]
-        downs.append(down(expert, pieces, [downs[-1][0], downs[-2][1], reduced]))
-    summed = sum_planes(reduced, [downs[-1][0]])
+    others = [lax.ppermute(reduced, "dp", [(i, i ^ k) for i in range(4)]) for k in (1, 2, 3)]
+    finished = [finish(*downs[0])]
+    downs.append(down(3, [reduced, *finished], others))
+    finished += [finish(*downs[expert]) for expert in range(1, 4)]
+    summed = sum_planes(reduced, others, [downs[-1][0]])
     router_grad = (
         lax.all_gather(summed, "expert").transpose(1, 0, 2).reshape(total_experts, width)
     )
 
-    finished = [(own.astype(F32) + came.astype(F32)).astype(BF16) for own, came in downs]
-    down_grad = jnp.stack(finished[:3] + [jnp.concatenate(finished[3:], axis=1)])
+    down_grad = jnp.stack(finished)
 
     hidden_grad = hidden.reshape(saved_hidden.shape)
     return (hidden_grad, down_grad, input_grad, router_grad)

time: 201 us -> 193 us (0.960)
  local copies, waits for them, and re-layouts: 20.8 us -> 11.4 us
  blocking collectives: 25.8 us -> 17.5 us
  Pallas kernels: 57.5 us -> 61.7 us
  waiting for transfers between devices: 30.8 us -> 34.3 us
  starting transfers between devices: 53.8 us -> 56.3 us
    unnamed x96 -> x82, local copies, waits for them, and re-layouts: 20.1 us -> 9.73 us
    all_to_all x1 -> x0, blocking collectives: 9.33 us -> none  [local_line(): lax.all_to_all(router_part, 'expert', split_axis=0, concat_axis=0)]
    all_to_all x0 -> x1, waiting for transfers between devices: none -> 5.57 us  [local_line(): lax.all_to_all(router_part, 'expert', split_axis=0, concat_axis=0)]
    ppermute x1, waiting for transfers between devices: 5.34 us -> 0.01 us  [local_line(): from_far = lax.ppermute(pair, 'dp', FAR)]
    ppermute x5 -> x4, waiting for transfers between devices: 10 us -> 5.86 us  [down(): return (own, lax.ppermute(other, 'dp', OUTWARD))]
    all_to_all x0 -> x1, starting transfers between devices: none -> 3.68 us  [local_line(): lax.all_to_all(router_part, 'expert', split_axis=0, concat_axis=0)]
    ppermute x10, waiting for transfers between devices: 0.03 us -> 3.6 us  [the longest x3 3.58 us: local_line(): lax.ppermute(reduced, 'dp', [(i, i ^ k) for i in range(4)])]
    ppermute x18 -> x14, waiting for transfers between devices: 15.4 us -> 18.4 us  [plane_swap(): return lax.ppermute(x, 'expert', [(i, i ^ bits) for i in range(8)])]
  transfers between devices with their start and end apart: 36 -> 32, of which waited for: 8 -> 13; matrix products, arithmetic and copies ran while one was open for 3% -> 4% of each run, Pallas kernels for 28% -> 29%
where the time goes in v3:
time: 193 us; the launch traced here: 192 us
  Pallas kernels  61.7 us (32%)
  starting transfers between devices  56.3 us (29%)
  waiting for transfers between devices  34.3 us (18%)
  blocking collectives  17.5 us (9%)
  local copies, waits for them, and re-layouts  11.4 us (6%)
  other arithmetic  9.57 us (5%)
    pallas_call x4, Pallas kernels, down_call(): pl.pallas_call(functools.partial(down_kernel, places, len(after)), in_spe...  22.2 us
    ppermute x14, waiting for transfers between devices, plane_swap(): return lax.ppermute(x, 'expert', [(i, i ^ bits) for i in range(8)])  18.4 us
    pallas_call x1, Pallas kernels, hidden_call(): pl.pallas_call(kernel, grid_spec=pltpu.PrefetchScalarGridSpec(num_scalar_...  15 us
    ppermute x3, starting transfers between devices, local_line(): lax.ppermute(reduced, 'dp', [(i, i ^ k) for i in range(4)])  12.3 us
    ppermute x14, starting transfers between devices, plane_swap(): return lax.ppermute(x, 'expert', [(i, i ^ bits) for i in range(8)])  11.6 us
    pallas_call x4, Pallas kernels, copies(): pl.pallas_call(functools.partial(copy_kernel, moves, len(sources) + len(a...  11.2 us
    pallas_call x1, Pallas kernels, rows_call(): pl.pallas_call(kernel, in_specs=[pl.BlockSpec(memory_space=pltpu.SMEM)] +...  10.1 us
    all_gather x1, blocking collectives, local_line(): lax.all_gather(summed, 'expert').transpose(1, 0, 2)  9.79 us
  transfers between devices with their start and end apart: 32, of which 13 were waited for; matrix products, arithmetic and copies ran while one was open for 4% of the time, Pallas kernels for 29%

profile of v3, /device:TPU:0, one launch (start us, length us, event | category | flops | bytes accessed | tf_op | source)
XLA Modules:
  0.0 192.1 jit_solution(10330877860443326340)
XLA Ops:
  2.7 3.0 %collective-permute-start = (bf16[128,2176]{1,0:T(8,128)(2,1)S(1)}, bf16[128,2176]{1,0:T(8,128)(2,1)S(1)}, u32[]{:S(2)}, u32[]{:S(2)}) collective-permute-start(bf16[128,2176]{1,0:T(8,128)(2,1)S(1)} %pad_maximum_fusion.1.refs_2_.refs_0_), channel_id=1, source_target_pairs={{0,2},{1,3},{2,0},{3,1},{4,6},{5,7},{6,4},{7,5},{8,10},{9,11},{10,... | collective-permute-start | bytes 1671176 | tf_op jit(solution)/shard_map/ppermute | solution.py:96
  8.0 6.2 %collective-permute-start.3 = (bf16[128,1152]{1,0:T(8,128)(2,1)S(1)}, bf16[128,1152]{1,0:T(8,128)(2,1)S(1)}, u32[]{:S(2)}, u32[]{:S(2)}) collective-permute-start(bf16[128,1152]{1,0:T(8,128)(2,1)S(1)} %pad_maximum_fusion.2), channel_id=1, source_target_pairs={{0,16},{24,8},{1,17},{25,9},{2,18},{26,10},{3,19},{27,11},{4,20},{... | collective-permute-start | bytes 884744 | tf_op jit(solution)/shard_map/ppermute | solution.py:541
  15.6 2.7 %collective-permute-done.refs_1_.refs_0_.refs_2_ = bf16[128,2176]{1,0:T(8,128)(2,1)S(1)} collective-permute-done((bf16[128,2176]{1,0:T(8,128)(2,1)S(1)}, bf16[128,2176]{1,0:T(8,128)(2,1)S(1)}, u32[]{:S(2)}, u32[]{:S(2)}) %collective-permute-start) | collective-permute-done | bytes 557088 | tf_op jit(solution)/shard_map/ppermute | solution.py:96
  19.2 3.2 %acts_pieces.1 = (bf16[2,384,768]{2,1,0:T(8,128)(2,1)}, bf16[2,384,768]{2,1,0:T(8,128)(2,1)}) custom-call(bf16[4,384,768]{2,1,0:T(8,128)(2,1)} %bitcast.26, bf16[128,2176]{1,0:T(8,128)(2,1)} %copy-done.23), custom_call_target="tpu_custom_call" | custom-call | bytes 4718592 | tf_op jit(solution)/shard_map/acts_pieces/pallas_call | solution.py:363
  24.2 2.8 %first_pieces.1 = (bf16[64,2176]{1,0:T(8,128)(2,1)}, bf16[64,2176]{1,0:T(8,128)(2,1)}, bf16[3,128,2176]{2,1,0:T(8,128)(2,1)}) custom-call(bf16[128,2176]{1,0:T(8,128)(2,1)} %copy-done.23, bf16[128,2176]{1,0:T(8,128)(2,1)} %copy-done.29, bf16[128,2176]{1,0:T(8,128)(2,1)} %copy-done.22, bf16[128,1152]{1,0:T(8,128)(2,1)} %copy-done.25, ...), custom_call_target="tpu_custom_call" | custom-call | bytes 3342336 | tf_op jit(solution)/shard_map/first_pieces/pallas_call | solution.py:363
  29.5 3.5 %collective-permute-start.12 = (bf16[2,384,768]{2,1,0:T(8,128)(2,1)}, bf16[2,384,768]{2,1,0:T(8,128)(2,1)S(1)}, u32[]{:S(2)}, u32[]{:S(2)}) collective-permute-start(bf16[2,384,768]{2,1,0:T(8,128)(2,1)} %get-tuple-element.30.refs_6_), channel_id=1, source_target_pairs={{0,8},{24,16},{1,9},{25,17},{2,10},{26,18},{3,11},{27,19},{4,12},{... | collective-permute-start | bytes 3538952 | tf_op jit(solution)/shard_map/ppermute | solution.py:574
  33.8 2.5 %collective-permute-done.6.refs_3_.refs_4_ = bf16[64,2176]{1,0:T(8,128)(2,1)S(1)} collective-permute-done((bf16[64,2176]{1,0:T(8,128)(2,1)}, bf16[64,2176]{1,0:T(8,128)(2,1)S(1)}, u32[]{:S(2)}, u32[]{:S(2)}) %collective-permute-start.6) | collective-permute-done | bytes 278560 | tf_op jit(solution)/shard_map/ppermute | solution.py:96
  42.4 15.0 %hidden_and_products.1 = (bf16[4,384,768]{2,1,0:T(8,128)(2,1)}, f32[4,8,128]{2,1,0:T(8,128)}, bf16[4,384,1024]{2,1,0:T(8,128)(2,1)}, bf16[2,384,768]{2,1,0:T(8,128)(2,1)}) custom-call(s32[3]{0:T(128)} %pad_add_fusion.place, bf16[128,2176]{1,0:T(8,128)(2,1)} %copy-done.22, ...), custom_call_target="tpu_custom_call", output_to_operand_aliasing={{3}: (12, {})} | custom-call | flops 6442450944 | bytes 22872064 | tf_op jit(solution)/shard_map/hidden_and_products/pallas_call | solution.py:253
  61.2 3.2 %second_pieces.1 = (bf16[64,2944]{1,0:T(8,128)(2,1)}, bf16[64,2944]{1,0:T(8,128)(2,1)}, bf16[3,128,2944]{2,1,0:T(8,128)(2,1)}) custom-call(bf16[128,2944]{1,0:T(8,128)(2,1)} %copy-done.27, bf16[128,2944]{1,0:T(8,128)(2,1)} %collective-permute-done.11.refs_1_.refs_3_, bf16[128,2944]{1,0:T(8,128)(2,1)} %side_by_side.1.refs_10_.refs_2_.refs_0_, ...), custom_call_target="tpu_custom_call" | custom-call | bytes 4521984 | tf_op jit(solution)/shard_map/second_pieces/pallas_call | solution.py:363
  65.2 6.8 %collective-permute-start.23 = (bf16[2,384,768]{2,1,0:T(8,128)(2,1)}, bf16[2,384,768]{2,1,0:T(8,128)(2,1)S(1)}, u32[]{:S(2)}, u32[]{:S(2)}) collective-permute-start(bf16[2,384,768]{2,1,0:T(8,128)(2,1)} %get-tuple-element.47), channel_id=1, source_target_pairs={{0,8},{24,16},{1,9},{25,17},{2,10},{26,18},{3,11},{27,19},{4,12},{... | collective-permute-start | bytes 3538952 | tf_op jit(solution)/shard_map/ppermute | solution.py:594
  74.5 8.3 %collective-permute-done.15.refs_4_ = bf16[64,2944]{1,0:T(8,128)(2,1)S(1)} collective-permute-done((bf16[64,2944]{1,0:T(8,128)(2,1)}, bf16[64,2944]{1,0:T(8,128)(2,1)S(1)}, u32[]{:S(2)}, u32[]{:S(2)}) %collective-permute-start.15) | collective-permute-done | bytes 376864 | tf_op jit(solution)/shard_map/ppermute | solution.py:96
  86.2 10.1 %far_rows.1 = (bf16[1152,1024]{1,0:T(8,128)(2,1)S(1)}, bf16[1152,1024]{1,0:T(8,128)(2,1)}, bf16[1152,1024]{1,0:T(8,128)(2,1)}, bf16[1152,1024]{1,0:T(8,128)(2,1)}) custom-call(s32[3]{0:T(128)} %pad_add_fusion.place, bf16[128,2944]{1,0:T(8,128)(2,1)} %side_by_side.1.refs_10_.refs_2_.refs_0_, bf16[3,128,2944]{2,1,0:T(8,128)(2,1)} %collective-permute-done.14.refs_1_, ...), custom_call_target="tpu_custom_call" | custom-call | flops 2013265920 | bytes 9437184 | tf_op jit(solution)/shard_map/far_rows/pallas_call | solution.py:332
  97.3 5.6 %down_terms.4 = (bf16[512,768]{1,0:T(8,128)(2,1)S(1)}, bf16[512,768]{1,0:T(8,128)(2,1)S(1)}) custom-call(bf16[1152,1024]{1,0:T(8,128)(2,1)S(1)} %get-tuple-element.39.rows, bf16[4,384,1024]{2,1,0:T(8,128)(2,1)} %get-tuple-element.40.refs_0_, bf16[4,384,768]{2,1,0:T(8,128)(2,1)} %bitcast.28, bf16[2,384,768]{2,1,0:T(8,128)(2,1)} %copy-done.18, ...), custom_call_target="tpu_custom_call" | custom-call | flops 1000 | bytes 1000 | tf_op jit(solution)/shard_map/down_terms/pallas_call | solution.py:444
  107.8 5.7 %down_terms.5 = (bf16[512,768]{1,0:T(8,128)(2,1)S(1)}, bf16[512,768]{1,0:T(8,128)(2,1)}) custom-call(bf16[1152,1024]{1,0:T(8,128)(2,1)S(1)} %copy-done.10, bf16[4,384,1024]{2,1,0:T(8,128)(2,1)} %get-tuple-element.40.refs_0_, bf16[4,384,768]{2,1,0:T(8,128)(2,1)} %bitcast.29, bf16[2,384,768]{2,1,0:T(8,128)(2,1)} %copy-done.18, ...), custom_call_target="tpu_custom_call" | custom-call | flops 1000 | bytes 1000 | tf_op jit(solution)/shard_map/down_terms/pallas_call | solution.py:444
  114.8 7.7 %all_to_all.10 = f32[8,4,128]{2,1,0:T(4,128)S(1)} all-to-all(f32[8,4,128]{2,1,0:T(4,128)S(1)} %copy.22), channel_id=1, replica_groups=mesh['dp'=4,'expert'=8] {'expert'}, dimensions={0} | all-to-all | bytes 32768 | tf_op jit(solution)/shard_map/all_to_all | solution.py:630
  126.4 5.4 %down_terms.6 = (bf16[512,768]{1,0:T(8,128)(2,1)S(1)}, bf16[512,768]{1,0:T(8,128)(2,1)}) custom-call(bf16[1152,1024]{1,0:T(8,128)(2,1)S(1)} %copy-done.8, bf16[4,384,1024]{2,1,0:T(8,128)(2,1)} %get-tuple-element.40.refs_0_, bf16[4,384,768]{2,1,0:T(8,128)(2,1)} %bitcast.30, bf16[2,384,768]{2,1,0:T(8,128)(2,1)} %copy-done.15, ...), custom_call_target="tpu_custom_call" | custom-call | flops 1000 | bytes 1000 | tf_op jit(solution)/shard_map/down_terms/pallas_call | solution.py:444
  132.7 3.7 %all-to-all-start.1 = ((f32[8,32,256]{2,1,0:T(8,128)}), f32[8,32,256]{2,1,0:T(8,128)S(1)}, u32[]{:S(2)}, u32[]{:S(2)}) async-start(f32[8,32,256]{2,1,0:T(8,128)} %held_until.2), calls=%async_computation.1 | async-start | bytes 524288 | tf_op jit(solution)/shard_map/all_to_all | solution.py:639
  137.7 5.6 %all-to-all-done.1 = f32[8,32,256]{2,1,0:T(8,128)S(1)} async-done(((f32[8,32,256]{2,1,0:T(8,128)}), f32[8,32,256]{2,1,0:T(8,128)S(1)}, u32[]{:S(2)}, u32[]{:S(2)}) %all-to-all-start.1) | async-done | bytes 262176 | tf_op jit(solution)/shard_map/all_to_all | solution.py:639
  143.3 9.8 %collective-permute-start.27 = (f32[32,256]{1,0:T(8,128)S(1)}, f32[32,256]{1,0:T(8,128)S(1)}, u32[]{:S(2)}, u32[]{:S(2)}) collective-permute-start(f32[32,256]{1,0:T(8,128)S(1)} %reduce_sum.29.refs_5_.refs_0_), channel_id=1, source_target_pairs={{0,8},{8,0},{16,24},{24,16},{1,9},{9,1},{17,25},{25,17},{2,10},{10... | collective-permute-start | bytes 98312 | tf_op jit(solution)/shard_map/ppermute | solution.py:641
  155.6 2.2 %add_convert_fusion.3.refs_6_ = bf16[512,768]{1,0:T(8,128)(2,1)} fusion(bf16[512,768]{1,0:T(8,128)(2,1)} %copy-done.21, bf16[512,768]{1,0:T(8,128)(2,1)S(1)} %copy-done.3), kind=kLoop, calls=%fused_computation.4 | loop fusion | flops 1572864 | bytes 2359296 | tf_op jit(solution)/shard_map/convert_element_type | solution.py:626
  157.8 5.5 %down_terms.7 = (bf16[512,768]{1,0:T(8,128)(2,1)S(1)}, bf16[512,768]{1,0:T(8,128)(2,1)}) custom-call(bf16[1152,1024]{1,0:T(8,128)(2,1)S(1)} %copy-done.9, bf16[4,384,1024]{2,1,0:T(8,128)(2,1)} %get-tuple-element.40.refs_0_, bf16[4,384,768]{2,1,0:T(8,128)(2,1)} %bitcast.31, bf16[2,384,768]{2,1,0:T(8,128)(2,1)} %copy-done.15, ...), custom_call_target="tpu_custom_call" | custom-call | flops 1000 | bytes 1000 | tf_op jit(solution)/shard_map/down_terms/pallas_call | solution.py:444
  164.3 3.6 %collective-permute-done.27.__1_.refs_1_ = f32[32,256]{1,0:T(8,128)S(1)} collective-permute-done((f32[32,256]{1,0:T(8,128)S(1)}, f32[32,256]{1,0:T(8,128)S(1)}, u32[]{:S(2)}, u32[]{:S(2)}) %collective-permute-start.27) | collective-permute-done | bytes 32800 | tf_op jit(solution)/shard_map/ppermute | solution.py:641
  172.7 9.8 %all-gather = f32[256,256]{1,0:T(8,128)S(1)} all-gather(f32[32,256]{1,0:T(8,128)} %sum_planes.1), channel_id=2, replica_groups=mesh['dp'=4,'expert'=8] {'expert'}, dimensions={0}, use_global_device_ids=true | all-gather | bytes 294912 | tf_op jit(solution)/shard_map/all_gather | solution.py:647
  184.6 5.4 %collective-permute-done.30 = bf16[512,768]{1,0:T(8,128)(2,1)S(1)} collective-permute-done((bf16[512,768]{1,0:T(8,128)(2,1)}, bf16[512,768]{1,0:T(8,128)(2,1)S(1)}, u32[]{:S(2)}, u32[]{:S(2)}) %collective-permute-start.30) | collective-permute-done | bytes 786464 | tf_op jit(solution)/shard_map/ppermute | solution.py:623
  (156 shorter events, 53.5 us)
Async XLA Ops:
  2.7 15.6 %collective-permute-start = (bf16[128,2176]{1,0:T(8,128)(2,1)S(1)}, bf16[128,2176]{1,0:T(8,128)(2,1)S(1)}, u32[]{:S(2)}, u32[]{:S(2)}) collective-permute-start(bf16[128,2176]{1,0:T(8,128)(2,1)S(1)} %pad_maximum_fusion.1.refs_2_.refs_0_), channel_id=1, source_target_pairs={{0,2},{1,3},{2,0},{3,1},{4,6},{5,7},{6,4},{7,5},{8,10},{9,11},{10,... | collective-permute-start | bytes 1671176 | tf_op jit(solution)/shard_map/ppermute | solution.py:96
  5.7 17.5 %collective-permute-start.1 = (bf16[128,2176]{1,0:T(8,128)(2,1)S(1)}, bf16[128,2176]{1,0:T(8,128)(2,1)S(1)}, u32[]{:S(2)}, u32[]{:S(2)}) collective-permute-start(bf16[128,2176]{1,0:T(8,128)(2,1)S(1)} %pad_maximum_fusion.1.refs_2_.refs_0_), channel_id=1, source_target_pairs={{0,4},{1,5},{2,6},{3,7},{4,0},{5,1},{6,2},{7,3},{8,12},{9,13},{10,... | collective-permute-start | bytes 1671176 | tf_op jit(solution)/shard_map/ppermute | solution.py:96
  7.3 15.8 %collective-permute-start.2 = (bf16[128,1152]{1,0:T(8,128)(2,1)S(1)}, bf16[128,1152]{1,0:T(8,128)(2,1)S(1)}, u32[]{:S(2)}, u32[]{:S(2)}) collective-permute-start(bf16[128,1152]{1,0:T(8,128)(2,1)S(1)} %pad_maximum_fusion.2), channel_id=1, source_target_pairs={{8,16},{16,8},{9,17},{17,9},{10,18},{18,10},{11,19},{19,11},{12,20... | collective-permute-start | bytes 884744 | tf_op jit(solution)/shard_map/ppermute | solution.py:540
  8.0 15.2 %collective-permute-start.3 = (bf16[128,1152]{1,0:T(8,128)(2,1)S(1)}, bf16[128,1152]{1,0:T(8,128)(2,1)S(1)}, u32[]{:S(2)}, u32[]{:S(2)}) collective-permute-start(bf16[128,1152]{1,0:T(8,128)(2,1)S(1)} %pad_maximum_fusion.2), channel_id=1, source_target_pairs={{0,16},{24,8},{1,17},{25,9},{2,18},{26,10},{3,19},{27,11},{4,20},{... | collective-permute-start | bytes 884744 | tf_op jit(solution)/shard_map/ppermute | solution.py:541
  27.0 15.4 %collective-permute-start.5 = (bf16[3,128,2176]{2,1,0:T(8,128)(2,1)}, bf16[3,128,2176]{2,1,0:T(8,128)(2,1)}, u32[]{:S(2)}, u32[]{:S(2)}) collective-permute-start(bf16[3,128,2176]{2,1,0:T(8,128)(2,1)} %get-tuple-element.31), channel_id=1, source_target_pairs={{0,1},{1,0},{2,3},{3,2},{4,5},{5,4},{6,7},{7,6},{8,9},{9,8},{10,11... | collective-permute-start | bytes 5013512 | tf_op jit(solution)/shard_map/ppermute | solution.py:96
  29.5 30.3 %collective-permute-start.12 = (bf16[2,384,768]{2,1,0:T(8,128)(2,1)}, bf16[2,384,768]{2,1,0:T(8,128)(2,1)S(1)}, u32[]{:S(2)}, u32[]{:S(2)}) collective-permute-start(bf16[2,384,768]{2,1,0:T(8,128)(2,1)} %get-tuple-element.30.refs_6_), channel_id=1, source_target_pairs={{0,8},{24,16},{1,9},{25,17},{2,10},{26,18},{3,11},{27,19},{4,12},{... | collective-permute-start | bytes 3538952 | tf_op jit(solution)/shard_map/ppermute | solution.py:574
  33.0 26.8 %collective-permute-start.13 = (bf16[2,384,768]{2,1,0:T(8,128)(2,1)}, bf16[2,384,768]{2,1,0:T(8,128)(2,1)S(1)}, u32[]{:S(2)}, u32[]{:S(2)}) collective-permute-start(bf16[2,384,768]{2,1,0:T(8,128)(2,1)} %get-tuple-element.30.refs_6_), channel_id=1, source_target_pairs={{8,16},{16,8},{9,17},{17,9},{10,18},{18,10},{11,19},{19,11},{12,20... | collective-permute-start | bytes 3538952 | tf_op jit(solution)/shard_map/ppermute | solution.py:573
  39.7 18.8 %collective-permute-start.10 = (bf16[128,2944]{1,0:T(8,128)(2,1)}, bf16[128,2944]{1,0:T(8,128)(2,1)S(1)}, u32[]{:S(2)}, u32[]{:S(2)}) collective-permute-start(bf16[128,2944]{1,0:T(8,128)(2,1)} %side_by_side.1.refs_10_.refs_2_.refs_0_), channel_id=1, source_target_pairs={{0,2},{1,3},{2,0},{3,1},{4,6},{5,7},{6,4},{7,5},{8,10},{9,11},{10,... | collective-permute-start | bytes 2261000 | tf_op jit(solution)/shard_map/ppermute | solution.py:96
  41.2 18.6 %collective-permute-start.11 = (bf16[128,2944]{1,0:T(8,128)(2,1)}, bf16[128,2944]{1,0:T(8,128)(2,1)}, u32[]{:S(2)}, u32[]{:S(2)}) collective-permute-start(bf16[128,2944]{1,0:T(8,128)(2,1)} %side_by_side.1.refs_10_.refs_2_.refs_0_), channel_id=1, source_target_pairs={{0,4},{1,5},{2,6},{3,7},{4,0},{5,1},{6,2},{7,3},{8,12},{9,13},{10,... | collective-permute-start | bytes 2261000 | tf_op jit(solution)/shard_map/ppermute | solution.py:96
  64.4 21.1 %collective-permute-start.14 = (bf16[3,128,2944]{2,1,0:T(8,128)(2,1)}, bf16[3,128,2944]{2,1,0:T(8,128)(2,1)}, u32[]{:S(2)}, u32[]{:S(2)}) collective-permute-start(bf16[3,128,2944]{2,1,0:T(8,128)(2,1)} %get-tuple-element.36), channel_id=1, source_target_pairs={{0,1},{1,0},{2,3},{3,2},{4,5},{5,4},{6,7},{7,6},{8,9},{9,8},{10,11... | collective-permute-start | bytes 6782984 | tf_op jit(solution)/shard_map/ppermute | solution.py:96
  64.4 31.9 %collective-permute-start.19 = (bf16[2,384,768]{2,1,0:T(8,128)(2,1)}, bf16[2,384,768]{2,1,0:T(8,128)(2,1)S(1)}, u32[]{:S(2)}, u32[]{:S(2)}) collective-permute-start(bf16[2,384,768]{2,1,0:T(8,128)(2,1)} %copy-done.17), channel_id=1, source_target_pairs={{8,16},{16,8},{9,17},{17,9},{10,18},{18,10},{11,19},{19,11},{12,20... | collective-permute-start | bytes 3538952 | tf_op jit(solution)/shard_map/ppermute | solution.py:595
  65.2 39.4 %collective-permute-start.23 = (bf16[2,384,768]{2,1,0:T(8,128)(2,1)}, bf16[2,384,768]{2,1,0:T(8,128)(2,1)S(1)}, u32[]{:S(2)}, u32[]{:S(2)}) collective-permute-start(bf16[2,384,768]{2,1,0:T(8,128)(2,1)} %get-tuple-element.47), channel_id=1, source_target_pairs={{0,8},{24,16},{1,9},{25,17},{2,10},{26,18},{3,11},{27,19},{4,12},{... | collective-permute-start | bytes 3538952 | tf_op jit(solution)/shard_map/ppermute | solution.py:594
  72.0 10.9 %collective-permute-start.15 = (bf16[64,2944]{1,0:T(8,128)(2,1)}, bf16[64,2944]{1,0:T(8,128)(2,1)S(1)}, u32[]{:S(2)}, u32[]{:S(2)}) collective-permute-start(bf16[64,2944]{1,0:T(8,128)(2,1)} %get-tuple-element.37), channel_id=1, source_target_pairs={{0,4},{1,5},{2,6},{3,7},{4,0},{5,1},{6,2},{7,3},{8,12},{9,13},{10,... | collective-permute-start | bytes 1130504 | tf_op jit(solution)/shard_map/ppermute | solution.py:96
  84.6 40.5 %collective-permute-start.22 = (bf16[2,384,768]{2,1,0:T(8,128)(2,1)}, bf16[2,384,768]{2,1,0:T(8,128)(2,1)S(1)}, u32[]{:S(2)}, u32[]{:S(2)}) collective-permute-start(bf16[2,384,768]{2,1,0:T(8,128)(2,1)} %get-tuple-element.47), channel_id=1, source_target_pairs={{8,16},{16,8},{9,17},{17,9},{10,18},{18,10},{11,19},{19,11},{12,20... | collective-permute-start | bytes 3538952 | tf_op jit(solution)/shard_map/ppermute | solution.py:593
  103.0 22.5 %collective-permute-start.20 = (bf16[512,768]{1,0:T(8,128)(2,1)S(1)}, bf16[512,768]{1,0:T(8,128)(2,1)S(1)}, u32[]{:S(2)}, u32[]{:S(2)}) collective-permute-start(bf16[512,768]{1,0:T(8,128)(2,1)S(1)} %get-tuple-element.42), channel_id=1, source_target_pairs={{8,0},{16,24},{9,1},{17,25},{10,2},{18,26},{11,3},{19,27},{12,4},{... | collective-permute-start | bytes 2359304 | tf_op jit(solution)/shard_map/ppermute | solution.py:623
  105.5 19.5 %collective-permute-start.24 = (bf16[1,384,768]{2,1,0:T(8,128)(2,1)S(1)}, bf16[1,384,768]{2,1,0:T(8,128)(2,1)S(1)}, u32[]{:S(2)}, u32[]{:S(2)}) collective-permute-start(bf16[1,384,768]{2,1,0:T(8,128)(2,1)S(1)} %get-tuple-element.58), channel_id=1, source_target_pairs={{8,16},{16,8},{9,17},{17,9},{10,18},{18,10},{11,19},{19,11},{12,20... | collective-permute-start | bytes 1769480 | tf_op jit(solution)/shard_map/ppermute | solution.py:597
  106.2 48.0 %collective-permute-start.26 = (bf16[1,384,768]{2,1,0:T(8,128)(2,1)}, bf16[1,384,768]{2,1,0:T(8,128)(2,1)}, u32[]{:S(2)}, u32[]{:S(2)}) collective-permute-start(bf16[1,384,768]{2,1,0:T(8,128)(2,1)} %get-tuple-element.59), channel_id=1, source_target_pairs={{8,16},{16,8},{9,17},{17,9},{10,18},{18,10},{11,19},{19,11},{12,20... | collective-permute-start | bytes 1769480 | tf_op jit(solution)/shard_map/ppermute | solution.py:597
  113.5 56.4 %collective-permute-start.21 = (bf16[512,768]{1,0:T(8,128)(2,1)}, bf16[512,768]{1,0:T(8,128)(2,1)}, u32[]{:S(2)}, u32[]{:S(2)}) collective-permute-start(bf16[512,768]{1,0:T(8,128)(2,1)} %get-tuple-element.45), channel_id=1, source_target_pairs={{8,0},{16,24},{9,1},{17,25},{10,2},{18,26},{11,3},{19,27},{12,4},{... | collective-permute-start | bytes 2359304 | tf_op jit(solution)/shard_map/ppermute | solution.py:623
  132.7 10.6 %all-to-all-start.1 = ((f32[8,32,256]{2,1,0:T(8,128)}), f32[8,32,256]{2,1,0:T(8,128)S(1)}, u32[]{:S(2)}, u32[]{:S(2)}) async-start(f32[8,32,256]{2,1,0:T(8,128)} %held_until.2), calls=%async_computation.1 | async-start | bytes 524288 | tf_op jit(solution)/shard_map/all_to_all | solution.py:639
  136.4 46.9 %collective-permute-start.25 = (bf16[512,768]{1,0:T(8,128)(2,1)}, bf16[512,768]{1,0:T(8,128)(2,1)}, u32[]{:S(2)}, u32[]{:S(2)}) collective-permute-start(bf16[512,768]{1,0:T(8,128)(2,1)} %get-tuple-element.49), channel_id=1, source_target_pairs={{8,0},{16,24},{9,1},{17,25},{10,2},{18,26},{11,3},{19,27},{12,4},{... | collective-permute-start | bytes 2359304 | tf_op jit(solution)/shard_map/ppermute | solution.py:623
  143.3 24.6 %collective-permute-start.27 = (f32[32,256]{1,0:T(8,128)S(1)}, f32[32,256]{1,0:T(8,128)S(1)}, u32[]{:S(2)}, u32[]{:S(2)}) collective-permute-start(f32[32,256]{1,0:T(8,128)S(1)} %reduce_sum.29.refs_5_.refs_0_), channel_id=1, source_target_pairs={{0,8},{8,0},{16,24},{24,16},{1,9},{9,1},{17,25},{25,17},{2,10},{10... | collective-permute-start | bytes 98312 | tf_op jit(solution)/shard_map/ppermute | solution.py:641
  153.1 14.7 %collective-permute-start.28 = (f32[32,256]{1,0:T(8,128)S(1)}, f32[32,256]{1,0:T(8,128)S(1)}, u32[]{:S(2)}, u32[]{:S(2)}) collective-permute-start(f32[32,256]{1,0:T(8,128)S(1)} %reduce_sum.29.refs_5_.refs_0_), channel_id=1, source_target_pairs={{0,16},{8,24},{16,0},{24,8},{1,17},{9,25},{17,1},{25,9},{2,18},{10... | collective-permute-start | bytes 98312 | tf_op jit(solution)/shard_map/ppermute | solution.py:641
  154.2 13.6 %collective-permute-start.29 = (f32[32,256]{1,0:T(8,128)S(1)}, f32[32,256]{1,0:T(8,128)S(1)}, u32[]{:S(2)}, u32[]{:S(2)}) collective-permute-start(f32[32,256]{1,0:T(8,128)S(1)} %reduce_sum.29.refs_5_.refs_0_), channel_id=1, source_target_pairs={{0,24},{8,16},{16,8},{24,0},{1,25},{9,17},{17,9},{25,1},{2,26},{10... | collective-permute-start | bytes 98312 | tf_op jit(solution)/shard_map/ppermute | solution.py:641
  168.5 21.5 %collective-permute-start.30 = (bf16[512,768]{1,0:T(8,128)(2,1)}, bf16[512,768]{1,0:T(8,128)(2,1)S(1)}, u32[]{:S(2)}, u32[]{:S(2)}) collective-permute-start(bf16[512,768]{1,0:T(8,128)(2,1)} %held_until.3), channel_id=1, source_target_pairs={{8,0},{16,24},{9,1},{17,25},{10,2},{18,26},{11,3},{19,27},{12,4},{... | collective-permute-start | bytes 2359304 | tf_op jit(solution)/shard_map/ppermute | solution.py:623
  (49 other events, 298.2 us)

commit v4 on v3

--- a/solution.py
+++ b/solution.py
@@ -606,9 +606,15 @@
         [hidden, outers[0], inners[0]],
         56 * MIB,
     )
-    other_blocks = plane_blocks(
-        columns, columns_across, columns_along, stacked, plane_diagonal(column_halves)
-    )
+    (products,) = held_until([products], column_halves)
+    returned = lax.all_to_all(
+        products.transpose(1, 0, 2), "expert", split_axis=0, concat_axis=0
+    ).reshape(total_experts, LANES)
+    input_grad, router_part = router_call(
+        returned, positions.T, weights.T, router_weight, inputs, []
+    )
+    corner = held_until(plane_diagonal(column_halves), [router_part])
+    other_blocks = plane_blocks(columns, columns_across, columns_along, stacked, corner)
     rows = rows_call(
         place, other_blocks, (2 * part, 2 * part, part), local_experts, total_experts, capacity, []
     )
@@ -627,20 +633,13 @@
 
     downs = [down(0, [])]
     downs.append(down(1, [downs[0][0]]))
-    returned = lax.all_to_all(
-        products.transpose(1, 0, 2), "expert", split_axis=0, concat_axis=0
-    ).reshape(total_experts, LANES)
-    input_grad, router_part = router_call(
-        returned, positions.T, weights.T, router_weight, inputs, [downs[1][0]]
-    )
-    downs.append(down(2, [downs[1][0], inners[1], downs[0][1]]))
-    (router_part,) = held_until([router_part], [downs[2][0]])
     reduced = jnp.sum(
         lax.all_to_all(router_part, "expert", split_axis=0, concat_axis=0), axis=0
     )
+    downs.append(down(2, [downs[1][0], inners[1], downs[0][1]]))
     others = [lax.ppermute(reduced, "dp", [(i, i ^ k) for i in range(4)]) for k in (1, 2, 3)]
     finished = [finish(*downs[0])]
-    downs.append(down(3, [reduced, *finished], others))
+    downs.append(down(3, [downs[2][0], *finished, *others]))
     finished += [finish(*downs[expert]) for expert in range(1, 4)]
     summed = sum_planes(reduced, others, [downs[-1][0]])
     router_grad = (

time: 193 us -> 191 us (0.990)
  blocking collectives: 17.5 us -> 28.3 us
  waiting for transfers between devices: 34.3 us -> 24.3 us
  starting transfers between devices: 56.3 us -> 51.6 us
    all_to_all x0 -> x1, blocking collectives: none -> 10 us  [local_line(): lax.all_to_all(router_part, 'expert', split_axis=0, concat_axis=0)]
    ppermute x14, waiting for transfers between devices: 18.4 us -> 9.85 us  [plane_swap(): return lax.ppermute(x, 'expert', [(i, i ^ bits) for i in range(8)])]
    ppermute x4, waiting for transfers between devices: 5.86 us -> 13.2 us  [down(): return (own, lax.ppermute(other, 'dp', OUTWARD))]
    all_to_all x1 -> x0, waiting for transfers between devices: 5.57 us -> none  [local_line(): lax.all_to_all(router_part, 'expert', split_axis=0, concat_axis=0)]
    all_to_all x1 -> x0, starting transfers between devices: 3.68 us -> none  [local_line(): lax.all_to_all(router_part, 'expert', split_axis=0, concat_axis=0)]
    ppermute x3, waiting for transfers between devices: 3.58 us -> 0.41 us  [local_line(): lax.ppermute(reduced, 'dp', [(i, i ^ k) for i in range(4)])]
    unnamed x82 -> x74, local copies, waits for them, and re-layouts: 9.73 us -> 9.88 us
  transfers between devices with their start and end apart: 32 -> 31, of which waited for: 13 -> 9; matrix products, arithmetic and copies ran while one was open for 4% -> 5% of each run, Pallas kernels for 29% -> 29%
where the time goes in v4:
time: 191 us; the launch traced here: 190 us
  Pallas kernels  61.6 us (32%)
  starting transfers between devices  51.6 us (27%)
  blocking collectives  28.3 us (15%)
  waiting for transfers between devices  24.3 us (13%)
  local copies, waits for them, and re-layouts  12.5 us (7%)
  other arithmetic  9.92 us (5%)
    pallas_call x4, Pallas kernels, down_call(): pl.pallas_call(functools.partial(down_kernel, places, len(after)), in_spe...  22.1 us
    pallas_call x1, Pallas kernels, hidden_call(): pl.pallas_call(kernel, grid_spec=pltpu.PrefetchScalarGridSpec(num_scalar_...  15 us
    ppermute x4, waiting for transfers between devices, down(): return (own, lax.ppermute(other, 'dp', OUTWARD))  13.2 us
    ppermute x14, starting transfers between devices, plane_swap(): return lax.ppermute(x, 'expert', [(i, i ^ bits) for i in range(8)])  11.6 us
    ppermute x3, starting transfers between devices, local_line(): lax.ppermute(reduced, 'dp', [(i, i ^ k) for i in range(4)])  11.3 us
    pallas_call x4, Pallas kernels, copies(): pl.pallas_call(functools.partial(copy_kernel, moves, len(sources) + len(a...  11.2 us
    pallas_call x1, Pallas kernels, rows_call(): pl.pallas_call(kernel, in_specs=[pl.BlockSpec(memory_space=pltpu.SMEM)] +...  10.1 us
    all_to_all x1, blocking collectives, local_line(): lax.all_to_all(router_part, 'expert', split_axis=0, concat_axis=0)  10 us
  transfers between devices with their start and end apart: 31, of which 9 were waited for; matrix products, arithmetic and copies ran while one was open for 5% of the time, Pallas kernels for 29%

profile of v4, /device:TPU:0, one launch (start us, length us, event | category | flops | bytes accessed | tf_op | source)
XLA Modules:
  0.0 189.6 jit_solution(14569057611846031365)
XLA Ops:
  2.7 3.0 %collective-permute-start = (bf16[128,2176]{1,0:T(8,128)(2,1)S(1)}, bf16[128,2176]{1,0:T(8,128)(2,1)S(1)}, u32[]{:S(2)}, u32[]{:S(2)}) collective-permute-start(bf16[128,2176]{1,0:T(8,128)(2,1)S(1)} %pad_maximum_fusion.1.refs_2_.refs_0_), channel_id=1, source_target_pairs={{0,2},{1,3},{2,0},{3,1},{4,6},{5,7},{6,4},{7,5},{8,10},{9,11},{10,... | collective-permute-start | bytes 1671176 | tf_op jit(solution)/shard_map/ppermute | solution.py:96
  8.0 6.2 %collective-permute-start.3 = (bf16[128,1152]{1,0:T(8,128)(2,1)S(1)}, bf16[128,1152]{1,0:T(8,128)(2,1)S(1)}, u32[]{:S(2)}, u32[]{:S(2)}) collective-permute-start(bf16[128,1152]{1,0:T(8,128)(2,1)S(1)} %pad_maximum_fusion.2), channel_id=1, source_target_pairs={{0,16},{24,8},{1,17},{25,9},{2,18},{26,10},{3,19},{27,11},{4,20},{... | collective-permute-start | bytes 884744 | tf_op jit(solution)/shard_map/ppermute | solution.py:541
  15.6 2.7 %collective-permute-done.refs_1_.refs_0_.refs_2_ = bf16[128,2176]{1,0:T(8,128)(2,1)S(1)} collective-permute-done((bf16[128,2176]{1,0:T(8,128)(2,1)S(1)}, bf16[128,2176]{1,0:T(8,128)(2,1)S(1)}, u32[]{:S(2)}, u32[]{:S(2)}) %collective-permute-start) | collective-permute-done | bytes 557088 | tf_op jit(solution)/shard_map/ppermute | solution.py:96
  19.2 3.2 %acts_pieces.1 = (bf16[2,384,768]{2,1,0:T(8,128)(2,1)}, bf16[2,384,768]{2,1,0:T(8,128)(2,1)}) custom-call(bf16[4,384,768]{2,1,0:T(8,128)(2,1)} %bitcast.26, bf16[128,2176]{1,0:T(8,128)(2,1)} %copy-done.24), custom_call_target="tpu_custom_call" | custom-call | bytes 4718592 | tf_op jit(solution)/shard_map/acts_pieces/pallas_call | solution.py:363
  24.2 2.8 %first_pieces.1 = (bf16[64,2176]{1,0:T(8,128)(2,1)}, bf16[64,2176]{1,0:T(8,128)(2,1)}, bf16[3,128,2176]{2,1,0:T(8,128)(2,1)}) custom-call(bf16[128,2176]{1,0:T(8,128)(2,1)} %copy-done.24, bf16[128,2176]{1,0:T(8,128)(2,1)} %copy-done.29, bf16[128,2176]{1,0:T(8,128)(2,1)} %copy-done.23, bf16[128,1152]{1,0:T(8,128)(2,1)} %copy-done.26, ...), custom_call_target="tpu_custom_call" | custom-call | bytes 3342336 | tf_op jit(solution)/shard_map/first_pieces/pallas_call | solution.py:363
  29.4 3.5 %collective-permute-start.12 = (bf16[2,384,768]{2,1,0:T(8,128)(2,1)}, bf16[2,384,768]{2,1,0:T(8,128)(2,1)S(1)}, u32[]{:S(2)}, u32[]{:S(2)}) collective-permute-start(bf16[2,384,768]{2,1,0:T(8,128)(2,1)} %get-tuple-element.32.refs_6_), channel_id=1, source_target_pairs={{0,8},{24,16},{1,9},{25,17},{2,10},{26,18},{3,11},{27,19},{4,12},{... | collective-permute-start | bytes 3538952 | tf_op jit(solution)/shard_map/ppermute | solution.py:574
  33.7 2.5 %collective-permute-done.6.refs_3_.refs_4_ = bf16[64,2176]{1,0:T(8,128)(2,1)S(1)} collective-permute-done((bf16[64,2176]{1,0:T(8,128)(2,1)}, bf16[64,2176]{1,0:T(8,128)(2,1)S(1)}, u32[]{:S(2)}, u32[]{:S(2)}) %collective-permute-start.6) | collective-permute-done | bytes 278560 | tf_op jit(solution)/shard_map/ppermute | solution.py:96
  37.7 2.0 %side_by_side.1.refs_10_.refs_2_.refs_0_ = bf16[128,2944]{1,0:T(8,128)(2,1)} custom-call(bf16[128,1152]{1,0:T(8,128)(2,1)} %copy-done.26, bf16[128,1152]{1,0:T(8,128)(2,1)} %copy-done.27, bf16[128,640]{1,0:T(8,128)(2,1)} %copy-done.28, bf16[64,2176]{1,0:T(8,128)(2,1)} %copy-done.31, bf16[64,2176]{1,0:T(8,128)(2,1)} %copy-done.32), custom_call_target="tpu_custom_call" | custom-call | bytes 1507328 | tf_op jit(solution)/shard_map/side_by_side/pallas_call | solution.py:363
  43.0 15.0 %hidden_and_products.1 = (bf16[4,384,768]{2,1,0:T(8,128)(2,1)}, f32[4,8,128]{2,1,0:T(8,128)}, bf16[4,384,1024]{2,1,0:T(8,128)(2,1)}, bf16[2,384,768]{2,1,0:T(8,128)(2,1)}) custom-call(s32[3]{0:T(128)} %pad_add_fusion.place, bf16[128,2176]{1,0:T(8,128)(2,1)} %copy-done.23, ...), custom_call_target="tpu_custom_call", output_to_operand_aliasing={{3}: (12, {})} | custom-call | flops 6442450944 | bytes 22872064 | tf_op jit(solution)/shard_map/hidden_and_products/pallas_call | solution.py:253
  58.6 1.9 collective-permute-done.11.refs_1_.refs_3_
  62.0 3.3 %second_pieces.1 = (bf16[64,2944]{1,0:T(8,128)(2,1)}, bf16[64,2944]{1,0:T(8,128)(2,1)}, bf16[3,128,2944]{2,1,0:T(8,128)(2,1)}) custom-call(bf16[128,2944]{1,0:T(8,128)(2,1)} %collective-permute-done.10.refs_0_.refs_2_, bf16[128,2944]{1,0:T(8,128)(2,1)} %collective-permute-done.11.refs_1_.refs_3_, bf16[128,2944]{1,0:T(8,128)(2,1)} %side_by_side.1.refs_10_.refs_2_.refs_0_, ...), custom_call_target="tpu_custom_call" | custom-call | bytes 4521984 | tf_op jit(solution)/shard_map/second_pieces/pallas_call | solution.py:363
  66.0 6.7 %collective-permute-start.23 = (bf16[2,384,768]{2,1,0:T(8,128)(2,1)}, bf16[2,384,768]{2,1,0:T(8,128)(2,1)S(1)}, u32[]{:S(2)}, u32[]{:S(2)}) collective-permute-start(bf16[2,384,768]{2,1,0:T(8,128)(2,1)} %get-tuple-element.53), channel_id=1, source_target_pairs={{0,8},{24,16},{1,9},{25,17},{2,10},{26,18},{3,11},{27,19},{4,12},{... | collective-permute-start | bytes 3538952 | tf_op jit(solution)/shard_map/ppermute | solution.py:594
  75.7 9.4 %all_to_all.10 = f32[8,4,128]{2,1,0:T(4,128)S(1)} all-to-all(f32[8,4,128]{2,1,0:T(4,128)S(1)} %copy.23), channel_id=1, replica_groups=mesh['dp'=4,'expert'=8] {'expert'}, dimensions={0} | all-to-all | bytes 32768 | tf_op jit(solution)/shard_map/all_to_all | solution.py:610
  92.7 10.1 %far_rows.1 = (bf16[1152,1024]{1,0:T(8,128)(2,1)S(1)}, bf16[1152,1024]{1,0:T(8,128)(2,1)}, bf16[1152,1024]{1,0:T(8,128)(2,1)}, bf16[1152,1024]{1,0:T(8,128)(2,1)}) custom-call(s32[3]{0:T(128)} %pad_add_fusion.place, bf16[128,2944]{1,0:T(8,128)(2,1)} %side_by_side.1.refs_10_.refs_2_.refs_0_, bf16[3,128,2944]{2,1,0:T(8,128)(2,1)} %collective-permute-done.14.refs_1_, ...), custom_call_target="tpu_custom_call" | custom-call | flops 2013265920 | bytes 9437184 | tf_op jit(solution)/shard_map/far_rows/pallas_call | solution.py:332
  103.8 5.6 %down_terms.4 = (bf16[512,768]{1,0:T(8,128)(2,1)S(1)}, bf16[512,768]{1,0:T(8,128)(2,1)}) custom-call(bf16[1152,1024]{1,0:T(8,128)(2,1)S(1)} %get-tuple-element.45.rows, bf16[4,384,1024]{2,1,0:T(8,128)(2,1)} %get-tuple-element.46.refs_0_, bf16[4,384,768]{2,1,0:T(8,128)(2,1)} %bitcast.28, bf16[2,384,768]{2,1,0:T(8,128)(2,1)} %copy-done.20, ...), custom_call_target="tpu_custom_call" | custom-call | flops 1000 | bytes 1000 | tf_op jit(solution)/shard_map/down_terms/pallas_call | solution.py:444
  113.6 5.7 %down_terms.5 = (bf16[512,768]{1,0:T(8,128)(2,1)S(1)}, bf16[512,768]{1,0:T(8,128)(2,1)}) custom-call(bf16[1152,1024]{1,0:T(8,128)(2,1)S(1)} %copy-done.10, bf16[4,384,1024]{2,1,0:T(8,128)(2,1)} %get-tuple-element.46.refs_0_, bf16[4,384,768]{2,1,0:T(8,128)(2,1)} %bitcast.29, bf16[2,384,768]{2,1,0:T(8,128)(2,1)} %copy-done.20, ...), custom_call_target="tpu_custom_call" | custom-call | flops 1000 | bytes 1000 | tf_op jit(solution)/shard_map/down_terms/pallas_call | solution.py:444
  121.5 10.0 %all_to_all.11 = f32[8,32,256]{2,1,0:T(8,128)} all-to-all(f32[8,32,256]{2,1,0:T(8,128)S(1)} %copy-done.12), channel_id=1, replica_groups=mesh['dp'=4,'expert'=8] {'expert'}, dimensions={0} | all-to-all | bytes 524288 | tf_op jit(solution)/shard_map/all_to_all | solution.py:637
  133.1 8.8 %collective-permute-start.27 = (f32[32,256]{1,0:T(8,128)}, f32[32,256]{1,0:T(8,128)S(1)}, u32[]{:S(2)}, u32[]{:S(2)}) collective-permute-start(f32[32,256]{1,0:T(8,128)} %reduce_sum.29.refs_0_), channel_id=1, source_target_pairs={{0,8},{8,0},{16,24},{24,16},{1,9},{9,1},{17,25},{25,17},{2,10},{10... | collective-permute-start | bytes 98312 | tf_op jit(solution)/shard_map/ppermute | solution.py:640
  142.0 2.4 %collective-permute-start.29 = (f32[32,256]{1,0:T(8,128)}, f32[32,256]{1,0:T(8,128)S(1)}, u32[]{:S(2)}, u32[]{:S(2)}) collective-permute-start(f32[32,256]{1,0:T(8,128)} %reduce_sum.29.refs_0_), channel_id=1, source_target_pairs={{0,24},{8,16},{16,8},{24,0},{1,25},{9,17},{17,9},{25,1},{2,26},{10... | collective-permute-start | bytes 98312 | tf_op jit(solution)/shard_map/ppermute | solution.py:640
  144.4 5.4 %down_terms.6 = (bf16[512,768]{1,0:T(8,128)(2,1)S(1)}, bf16[512,768]{1,0:T(8,128)(2,1)}) custom-call(bf16[1152,1024]{1,0:T(8,128)(2,1)S(1)} %copy-done.8, bf16[4,384,1024]{2,1,0:T(8,128)(2,1)} %get-tuple-element.46.refs_0_, bf16[4,384,768]{2,1,0:T(8,128)(2,1)} %bitcast.30, bf16[2,384,768]{2,1,0:T(8,128)(2,1)} %collective-permute-done.22.refs_2_.refs_6_, ...), custom_call_target="tpu_custom_call" | custom-call | flops 1000 | bytes 1000 | tf_op jit(solution)/shard_map/down_terms/pallas_call | solution.py:444
  151.7 2.2 %add_convert_fusion.3.refs_6_ = bf16[512,768]{1,0:T(8,128)(2,1)} fusion(bf16[512,768]{1,0:T(8,128)(2,1)} %collective-permute-done.20.refs_7_, bf16[512,768]{1,0:T(8,128)(2,1)S(1)} %copy-done.3), kind=kLoop, calls=%fused_computation.4 | loop fusion | flops 1572864 | bytes 2359296 | tf_op jit(solution)/shard_map/convert_element_type | solution.py:632
  154.0 5.4 %down_terms.7 = (bf16[512,768]{1,0:T(8,128)(2,1)S(1)}, bf16[512,768]{1,0:T(8,128)(2,1)}) custom-call(bf16[1152,1024]{1,0:T(8,128)(2,1)S(1)} %copy-done.9, bf16[4,384,1024]{2,1,0:T(8,128)(2,1)} %get-tuple-element.46.refs_0_, bf16[4,384,768]{2,1,0:T(8,128)(2,1)} %bitcast.31, bf16[2,384,768]{2,1,0:T(8,128)(2,1)} %collective-permute-done.22.refs_2_.refs_6_, ...), custom_call_target="tpu_custom_call" | custom-call | flops 1000 | bytes 1000 | tf_op jit(solution)/shard_map/down_terms/pallas_call | solution.py:444
  163.1 8.9 %all-gather = f32[256,256]{1,0:T(8,128)S(1)} all-gather(f32[32,256]{1,0:T(8,128)} %sum_planes.1), channel_id=2, replica_groups=mesh['dp'=4,'expert'=8] {'expert'}, dimensions={0}, use_global_device_ids=true | all-gather | bytes 294912 | tf_op jit(solution)/shard_map/all_gather | solution.py:646
  174.3 13.2 %collective-permute-done.30 = bf16[512,768]{1,0:T(8,128)(2,1)S(1)} collective-permute-done((bf16[512,768]{1,0:T(8,128)(2,1)}, bf16[512,768]{1,0:T(8,128)(2,1)S(1)}, u32[]{:S(2)}, u32[]{:S(2)}) %collective-permute-start.30) | collective-permute-done | bytes 786464 | tf_op jit(solution)/shard_map/ppermute | solution.py:629
  (147 shorter events, 48.5 us)
Async XLA Ops:
  2.7 15.6 %collective-permute-start = (bf16[128,2176]{1,0:T(8,128)(2,1)S(1)}, bf16[128,2176]{1,0:T(8,128)(2,1)S(1)}, u32[]{:S(2)}, u32[]{:S(2)}) collective-permute-start(bf16[128,2176]{1,0:T(8,128)(2,1)S(1)} %pad_maximum_fusion.1.refs_2_.refs_0_), channel_id=1, source_target_pairs={{0,2},{1,3},{2,0},{3,1},{4,6},{5,7},{6,4},{7,5},{8,10},{9,11},{10,... | collective-permute-start | bytes 1671176 | tf_op jit(solution)/shard_map/ppermute | solution.py:96
  5.7 17.5 %collective-permute-start.1 = (bf16[128,2176]{1,0:T(8,128)(2,1)S(1)}, bf16[128,2176]{1,0:T(8,128)(2,1)S(1)}, u32[]{:S(2)}, u32[]{:S(2)}) collective-permute-start(bf16[128,2176]{1,0:T(8,128)(2,1)S(1)} %pad_maximum_fusion.1.refs_2_.refs_0_), channel_id=1, source_target_pairs={{0,4},{1,5},{2,6},{3,7},{4,0},{5,1},{6,2},{7,3},{8,12},{9,13},{10,... | collective-permute-start | bytes 1671176 | tf_op jit(solution)/shard_map/ppermute | solution.py:96
  7.3 15.8 %collective-permute-start.2 = (bf16[128,1152]{1,0:T(8,128)(2,1)S(1)}, bf16[128,1152]{1,0:T(8,128)(2,1)S(1)}, u32[]{:S(2)}, u32[]{:S(2)}) collective-permute-start(bf16[128,1152]{1,0:T(8,128)(2,1)S(1)} %pad_maximum_fusion.2), channel_id=1, source_target_pairs={{8,16},{16,8},{9,17},{17,9},{10,18},{18,10},{11,19},{19,11},{12,20... | collective-permute-start | bytes 884744 | tf_op jit(solution)/shard_map/ppermute | solution.py:540
  8.0 15.2 %collective-permute-start.3 = (bf16[128,1152]{1,0:T(8,128)(2,1)S(1)}, bf16[128,1152]{1,0:T(8,128)(2,1)S(1)}, u32[]{:S(2)}, u32[]{:S(2)}) collective-permute-start(bf16[128,1152]{1,0:T(8,128)(2,1)S(1)} %pad_maximum_fusion.2), channel_id=1, source_target_pairs={{0,16},{24,8},{1,17},{25,9},{2,18},{26,10},{3,19},{27,11},{4,20},{... | collective-permute-start | bytes 884744 | tf_op jit(solution)/shard_map/ppermute | solution.py:541
  27.0 16.0 %collective-permute-start.5 = (bf16[3,128,2176]{2,1,0:T(8,128)(2,1)}, bf16[3,128,2176]{2,1,0:T(8,128)(2,1)}, u32[]{:S(2)}, u32[]{:S(2)}) collective-permute-start(bf16[3,128,2176]{2,1,0:T(8,128)(2,1)} %get-tuple-element.33), channel_id=1, source_target_pairs={{0,1},{1,0},{2,3},{3,2},{4,5},{5,4},{6,7},{7,6},{8,9},{9,8},{10,11... | collective-permute-start | bytes 5013512 | tf_op jit(solution)/shard_map/ppermute | solution.py:96
  29.4 31.1 %collective-permute-start.12 = (bf16[2,384,768]{2,1,0:T(8,128)(2,1)}, bf16[2,384,768]{2,1,0:T(8,128)(2,1)S(1)}, u32[]{:S(2)}, u32[]{:S(2)}) collective-permute-start(bf16[2,384,768]{2,1,0:T(8,128)(2,1)} %get-tuple-element.32.refs_6_), channel_id=1, source_target_pairs={{0,8},{24,16},{1,9},{25,17},{2,10},{26,18},{3,11},{27,19},{4,12},{... | collective-permute-start | bytes 3538952 | tf_op jit(solution)/shard_map/ppermute | solution.py:574
  33.0 27.5 %collective-permute-start.13 = (bf16[2,384,768]{2,1,0:T(8,128)(2,1)}, bf16[2,384,768]{2,1,0:T(8,128)(2,1)S(1)}, u32[]{:S(2)}, u32[]{:S(2)}) collective-permute-start(bf16[2,384,768]{2,1,0:T(8,128)(2,1)} %get-tuple-element.32.refs_6_), channel_id=1, source_target_pairs={{8,16},{16,8},{9,17},{17,9},{10,18},{18,10},{11,19},{19,11},{12,20... | collective-permute-start | bytes 3538952 | tf_op jit(solution)/shard_map/ppermute | solution.py:573
  39.7 18.9 %collective-permute-start.10 = (bf16[128,2944]{1,0:T(8,128)(2,1)}, bf16[128,2944]{1,0:T(8,128)(2,1)}, u32[]{:S(2)}, u32[]{:S(2)}) collective-permute-start(bf16[128,2944]{1,0:T(8,128)(2,1)} %side_by_side.1.refs_10_.refs_2_.refs_0_), channel_id=1, source_target_pairs={{0,2},{1,3},{2,0},{3,1},{4,6},{5,7},{6,4},{7,5},{8,10},{9,11},{10,... | collective-permute-start | bytes 2261000 | tf_op jit(solution)/shard_map/ppermute | solution.py:96
  41.9 18.6 %collective-permute-start.11 = (bf16[128,2944]{1,0:T(8,128)(2,1)}, bf16[128,2944]{1,0:T(8,128)(2,1)}, u32[]{:S(2)}, u32[]{:S(2)}) collective-permute-start(bf16[128,2944]{1,0:T(8,128)(2,1)} %side_by_side.1.refs_10_.refs_2_.refs_0_), channel_id=1, source_target_pairs={{0,4},{1,5},{2,6},{3,7},{4,0},{5,1},{6,2},{7,3},{8,12},{9,13},{10,... | collective-permute-start | bytes 2261000 | tf_op jit(solution)/shard_map/ppermute | solution.py:96
  65.3 26.6 %collective-permute-start.14 = (bf16[3,128,2944]{2,1,0:T(8,128)(2,1)}, bf16[3,128,2944]{2,1,0:T(8,128)(2,1)}, u32[]{:S(2)}, u32[]{:S(2)}) collective-permute-start(bf16[3,128,2944]{2,1,0:T(8,128)(2,1)} %get-tuple-element.38), channel_id=1, source_target_pairs={{0,1},{1,0},{2,3},{3,2},{4,5},{5,4},{6,7},{7,6},{8,9},{9,8},{10,11... | collective-permute-start | bytes 6782984 | tf_op jit(solution)/shard_map/ppermute | solution.py:96
  65.3 37.4 %collective-permute-start.19 = (bf16[2,384,768]{2,1,0:T(8,128)(2,1)}, bf16[2,384,768]{2,1,0:T(8,128)(2,1)S(1)}, u32[]{:S(2)}, u32[]{:S(2)}) collective-permute-start(bf16[2,384,768]{2,1,0:T(8,128)(2,1)} %copy-done.19), channel_id=1, source_target_pairs={{8,16},{16,8},{9,17},{17,9},{10,18},{18,10},{11,19},{19,11},{12,20... | collective-permute-start | bytes 3538952 | tf_op jit(solution)/shard_map/ppermute | solution.py:595
  66.0 44.9 %collective-permute-start.23 = (bf16[2,384,768]{2,1,0:T(8,128)(2,1)}, bf16[2,384,768]{2,1,0:T(8,128)(2,1)S(1)}, u32[]{:S(2)}, u32[]{:S(2)}) collective-permute-start(bf16[2,384,768]{2,1,0:T(8,128)(2,1)} %get-tuple-element.53), channel_id=1, source_target_pairs={{0,8},{24,16},{1,9},{25,17},{2,10},{26,18},{3,11},{27,19},{4,12},{... | collective-permute-start | bytes 3538952 | tf_op jit(solution)/shard_map/ppermute | solution.py:594
  72.8 14.8 %collective-permute-start.15 = (bf16[64,2944]{1,0:T(8,128)(2,1)}, bf16[64,2944]{1,0:T(8,128)(2,1)S(1)}, u32[]{:S(2)}, u32[]{:S(2)}) collective-permute-start(bf16[64,2944]{1,0:T(8,128)(2,1)} %get-tuple-element.39.__1_), channel_id=1, source_target_pairs={{0,4},{1,5},{2,6},{3,7},{4,0},{5,1},{6,2},{7,3},{8,12},{9,13},{10,... | collective-permute-start | bytes 1130504 | tf_op jit(solution)/shard_map/ppermute | solution.py:96
  73.9 13.7 %collective-permute-start.16 = (bf16[64,2944]{1,0:T(8,128)(2,1)}, bf16[64,2944]{1,0:T(8,128)(2,1)}, u32[]{:S(2)}, u32[]{:S(2)}) collective-permute-start(bf16[64,2944]{1,0:T(8,128)(2,1)} %get-tuple-element.40.__2_), channel_id=1, source_target_pairs={{0,2},{1,3},{2,0},{3,1},{4,6},{5,7},{6,4},{7,5},{8,10},{9,11},{10,... | collective-permute-start | bytes 1130504 | tf_op jit(solution)/shard_map/ppermute | solution.py:96
  90.2 42.9 %collective-permute-start.22 = (bf16[2,384,768]{2,1,0:T(8,128)(2,1)}, bf16[2,384,768]{2,1,0:T(8,128)(2,1)}, u32[]{:S(2)}, u32[]{:S(2)}) collective-permute-start(bf16[2,384,768]{2,1,0:T(8,128)(2,1)} %get-tuple-element.53), channel_id=1, source_target_pairs={{8,16},{16,8},{9,17},{17,9},{10,18},{18,10},{11,19},{19,11},{12,20... | collective-permute-start | bytes 3538952 | tf_op jit(solution)/shard_map/ppermute | solution.py:593
  109.4 32.6 %collective-permute-start.20 = (bf16[512,768]{1,0:T(8,128)(2,1)}, bf16[512,768]{1,0:T(8,128)(2,1)}, u32[]{:S(2)}, u32[]{:S(2)}) collective-permute-start(bf16[512,768]{1,0:T(8,128)(2,1)} %get-tuple-element.48), channel_id=1, source_target_pairs={{8,0},{16,24},{9,1},{17,25},{10,2},{18,26},{11,3},{19,27},{12,4},{... | collective-permute-start | bytes 2359304 | tf_op jit(solution)/shard_map/ppermute | solution.py:629
  112.2 29.8 %collective-permute-start.24 = (bf16[1,384,768]{2,1,0:T(8,128)(2,1)}, bf16[1,384,768]{2,1,0:T(8,128)(2,1)S(1)}, u32[]{:S(2)}, u32[]{:S(2)}) collective-permute-start(bf16[1,384,768]{2,1,0:T(8,128)(2,1)} %get-tuple-element.62), channel_id=1, source_target_pairs={{8,16},{16,8},{9,17},{17,9},{10,18},{18,10},{11,19},{19,11},{12,20... | collective-permute-start | bytes 1769480 | tf_op jit(solution)/shard_map/ppermute | solution.py:597
  112.9 41.1 %collective-permute-start.26 = (bf16[1,384,768]{2,1,0:T(8,128)(2,1)}, bf16[1,384,768]{2,1,0:T(8,128)(2,1)S(1)}, u32[]{:S(2)}, u32[]{:S(2)}) collective-permute-start(bf16[1,384,768]{2,1,0:T(8,128)(2,1)} %get-tuple-element.63), channel_id=1, source_target_pairs={{8,16},{16,8},{9,17},{17,9},{10,18},{18,10},{11,19},{19,11},{12,20... | collective-permute-start | bytes 1769480 | tf_op jit(solution)/shard_map/ppermute | solution.py:597
  120.2 52.5 %collective-permute-start.21 = (bf16[512,768]{1,0:T(8,128)(2,1)}, bf16[512,768]{1,0:T(8,128)(2,1)}, u32[]{:S(2)}, u32[]{:S(2)}) collective-permute-start(bf16[512,768]{1,0:T(8,128)(2,1)} %get-tuple-element.51), channel_id=1, source_target_pairs={{8,0},{16,24},{9,1},{17,25},{10,2},{18,26},{11,3},{19,27},{12,4},{... | collective-permute-start | bytes 2359304 | tf_op jit(solution)/shard_map/ppermute | solution.py:629
  133.1 17.2 %collective-permute-start.27 = (f32[32,256]{1,0:T(8,128)}, f32[32,256]{1,0:T(8,128)S(1)}, u32[]{:S(2)}, u32[]{:S(2)}) collective-permute-start(f32[32,256]{1,0:T(8,128)} %reduce_sum.29.refs_0_), channel_id=1, source_target_pairs={{0,8},{8,0},{16,24},{24,16},{1,9},{9,1},{17,25},{25,17},{2,10},{10... | collective-permute-start | bytes 98312 | tf_op jit(solution)/shard_map/ppermute | solution.py:640
  142.0 11.9 %collective-permute-start.28 = (f32[32,256]{1,0:T(8,128)}, f32[32,256]{1,0:T(8,128)S(1)}, u32[]{:S(2)}, u32[]{:S(2)}) collective-permute-start(f32[32,256]{1,0:T(8,128)} %reduce_sum.29.refs_0_), channel_id=1, source_target_pairs={{0,16},{8,24},{16,0},{24,8},{1,17},{9,25},{17,1},{25,9},{2,18},{10... | collective-permute-start | bytes 98312 | tf_op jit(solution)/shard_map/ppermute | solution.py:640
  142.0 11.9 %collective-permute-start.29 = (f32[32,256]{1,0:T(8,128)}, f32[32,256]{1,0:T(8,128)S(1)}, u32[]{:S(2)}, u32[]{:S(2)}) collective-permute-start(f32[32,256]{1,0:T(8,128)} %reduce_sum.29.refs_0_), channel_id=1, source_target_pairs={{0,24},{8,16},{16,8},{24,0},{1,25},{9,17},{17,9},{25,1},{2,26},{10... | collective-permute-start | bytes 98312 | tf_op jit(solution)/shard_map/ppermute | solution.py:640
  150.3 23.8 %collective-permute-start.25 = (bf16[512,768]{1,0:T(8,128)(2,1)}, bf16[512,768]{1,0:T(8,128)(2,1)S(1)}, u32[]{:S(2)}, u32[]{:S(2)}) collective-permute-start(bf16[512,768]{1,0:T(8,128)(2,1)} %get-tuple-element.55), channel_id=1, source_target_pairs={{8,0},{16,24},{9,1},{17,25},{10,2},{18,26},{11,3},{19,27},{12,4},{... | collective-permute-start | bytes 2359304 | tf_op jit(solution)/shard_map/ppermute | solution.py:629
  160.3 27.3 %collective-permute-start.30 = (bf16[512,768]{1,0:T(8,128)(2,1)}, bf16[512,768]{1,0:T(8,128)(2,1)S(1)}, u32[]{:S(2)}, u32[]{:S(2)}) collective-permute-start(bf16[512,768]{1,0:T(8,128)(2,1)} %get-tuple-element.58), channel_id=1, source_target_pairs={{8,0},{16,24},{9,1},{17,25},{10,2},{18,26},{11,3},{19,27},{12,4},{... | collective-permute-start | bytes 2359304 | tf_op jit(solution)/shard_map/ppermute | solution.py:629
  (44 other events, 265.3 us)

commit v5 on v4

--- a/solution.py
+++ b/solution.py
@@ -334,9 +334,9 @@
         in_specs=[pl.BlockSpec(memory_space=pltpu.SMEM)]
         + [pl.BlockSpec(memory_space=pltpu.VMEM)] * len(flat)
         + [ANYWHERE] * len(after),
-        out_specs=[pl.BlockSpec(memory_space=pltpu.VMEM)] + [ANYWHERE] * (local_experts - 1),
-        out_shape=[pltpu.VMEM(shape, BF16)]
-        + [jax.ShapeDtypeStruct(shape, BF16)] * (local_experts - 1),
+        out_specs=[pl.BlockSpec(memory_space=pltpu.VMEM)] * 2 + [ANYWHERE] * (local_experts - 2),
+        out_shape=[pltpu.VMEM(shape, BF16)] * 2
+        + [jax.ShapeDtypeStruct(shape, BF16)] * (local_experts - 2),
         scratch_shapes=[
             pltpu.VMEM((local_experts, *shape), BF16),
             pltpu.SemaphoreType.DMA((len(widths), local_experts)),

time: 191 us -> 190 us (level)
    unnamed x74 -> x72, local copies, waits for them, and re-layouts: 9.88 us -> 9.81 us
where the time goes in v5:
time: 190 us; the launch traced here: 189 us
  Pallas kernels  61.6 us (32%)
  starting transfers between devices  51.5 us (27%)
  blocking collectives  28.2 us (15%)
  waiting for transfers between devices  24.2 us (13%)
  local copies, waits for them, and re-layouts  12.5 us (7%)
  other arithmetic  10 us (5%)
    pallas_call x4, Pallas kernels, down_call(): pl.pallas_call(functools.partial(down_kernel, places, len(after)), in_spe...  22 us
    pallas_call x1, Pallas kernels, hidden_call(): pl.pallas_call(kernel, grid_spec=pltpu.PrefetchScalarGridSpec(num_scalar_...  15 us
    ppermute x4, waiting for transfers between devices, down(): return (own, lax.ppermute(other, 'dp', OUTWARD))  13.4 us
    ppermute x14, starting transfers between devices, plane_swap(): return lax.ppermute(x, 'expert', [(i, i ^ bits) for i in range(8)])  11.6 us
    pallas_call x4, Pallas kernels, copies(): pl.pallas_call(functools.partial(copy_kernel, moves, len(sources) + len(a...  11.3 us
    ppermute x3, starting transfers between devices, local_line(): lax.ppermute(reduced, 'dp', [(i, i ^ k) for i in range(4)])  11.2 us
    all_to_all x1, blocking collectives, local_line(): lax.all_to_all(router_part, 'expert', split_axis=0, concat_axis=0)  10 us
    pallas_call x1, Pallas kernels, rows_call(): pl.pallas_call(kernel, in_specs=[pl.BlockSpec(memory_space=pltpu.SMEM)] +...  10 us
  transfers between devices with their start and end apart: 31, of which 9 were waited for; matrix products, arithmetic and copies ran while one was open for 5% of the time, Pallas kernels for 29%

profile of v5, /device:TPU:0, one launch (start us, length us, event | category | flops | bytes accessed | tf_op | source)
XLA Modules:
  0.0 189.3 jit_solution(13888513657856679164)
XLA Ops:
  2.7 3.0 %collective-permute-start = (bf16[128,2176]{1,0:T(8,128)(2,1)S(1)}, bf16[128,2176]{1,0:T(8,128)(2,1)S(1)}, u32[]{:S(2)}, u32[]{:S(2)}) collective-permute-start(bf16[128,2176]{1,0:T(8,128)(2,1)S(1)} %pad_maximum_fusion.1.refs_2_.refs_0_), channel_id=1, source_target_pairs={{0,2},{1,3},{2,0},{3,1},{4,6},{5,7},{6,4},{7,5},{8,10},{9,11},{10,... | collective-permute-start | bytes 1671176 | tf_op jit(solution)/shard_map/ppermute | solution.py:96
  8.0 6.2 %collective-permute-start.3 = (bf16[128,1152]{1,0:T(8,128)(2,1)S(1)}, bf16[128,1152]{1,0:T(8,128)(2,1)S(1)}, u32[]{:S(2)}, u32[]{:S(2)}) collective-permute-start(bf16[128,1152]{1,0:T(8,128)(2,1)S(1)} %pad_maximum_fusion.2), channel_id=1, source_target_pairs={{0,16},{24,8},{1,17},{25,9},{2,18},{26,10},{3,19},{27,11},{4,20},{... | collective-permute-start | bytes 884744 | tf_op jit(solution)/shard_map/ppermute | solution.py:541
  15.6 2.7 %collective-permute-done.refs_1_.refs_0_.refs_2_ = bf16[128,2176]{1,0:T(8,128)(2,1)S(1)} collective-permute-done((bf16[128,2176]{1,0:T(8,128)(2,1)S(1)}, bf16[128,2176]{1,0:T(8,128)(2,1)S(1)}, u32[]{:S(2)}, u32[]{:S(2)}) %collective-permute-start) | collective-permute-done | bytes 557088 | tf_op jit(solution)/shard_map/ppermute | solution.py:96
  19.2 3.2 %acts_pieces.1 = (bf16[2,384,768]{2,1,0:T(8,128)(2,1)}, bf16[2,384,768]{2,1,0:T(8,128)(2,1)}) custom-call(bf16[4,384,768]{2,1,0:T(8,128)(2,1)} %bitcast.26, bf16[128,2176]{1,0:T(8,128)(2,1)} %copy-done.23), custom_call_target="tpu_custom_call" | custom-call | bytes 4718592 | tf_op jit(solution)/shard_map/acts_pieces/pallas_call | solution.py:363
  24.2 2.8 %first_pieces.1 = (bf16[64,2176]{1,0:T(8,128)(2,1)}, bf16[64,2176]{1,0:T(8,128)(2,1)}, bf16[3,128,2176]{2,1,0:T(8,128)(2,1)}) custom-call(bf16[128,2176]{1,0:T(8,128)(2,1)} %copy-done.23, bf16[128,2176]{1,0:T(8,128)(2,1)} %copy-done.28, bf16[128,2176]{1,0:T(8,128)(2,1)} %copy-done.22, bf16[128,1152]{1,0:T(8,128)(2,1)} %copy-done.25, ...), custom_call_target="tpu_custom_call" | custom-call | bytes 3342336 | tf_op jit(solution)/shard_map/first_pieces/pallas_call | solution.py:363
  29.5 3.5 %collective-permute-start.12 = (bf16[2,384,768]{2,1,0:T(8,128)(2,1)}, bf16[2,384,768]{2,1,0:T(8,128)(2,1)S(1)}, u32[]{:S(2)}, u32[]{:S(2)}) collective-permute-start(bf16[2,384,768]{2,1,0:T(8,128)(2,1)} %get-tuple-element.32.refs_6_), channel_id=1, source_target_pairs={{0,8},{24,16},{1,9},{25,17},{2,10},{26,18},{3,11},{27,19},{4,12},{... | collective-permute-start | bytes 3538952 | tf_op jit(solution)/shard_map/ppermute | solution.py:574
  33.7 2.5 %collective-permute-done.6.refs_3_.refs_4_ = bf16[64,2176]{1,0:T(8,128)(2,1)S(1)} collective-permute-done((bf16[64,2176]{1,0:T(8,128)(2,1)}, bf16[64,2176]{1,0:T(8,128)(2,1)S(1)}, u32[]{:S(2)}, u32[]{:S(2)}) %collective-permute-start.6) | collective-permute-done | bytes 278560 | tf_op jit(solution)/shard_map/ppermute | solution.py:96
  37.7 2.1 %side_by_side.1.refs_10_.refs_2_.refs_0_ = bf16[128,2944]{1,0:T(8,128)(2,1)} custom-call(bf16[128,1152]{1,0:T(8,128)(2,1)} %copy-done.25, bf16[128,1152]{1,0:T(8,128)(2,1)} %copy-done.26, bf16[128,640]{1,0:T(8,128)(2,1)} %copy-done.27, bf16[64,2176]{1,0:T(8,128)(2,1)} %copy-done.30, bf16[64,2176]{1,0:T(8,128)(2,1)} %copy-done.31), custom_call_target="tpu_custom_call" | custom-call | bytes 1507328 | tf_op jit(solution)/shard_map/side_by_side/pallas_call | solution.py:363
  43.2 15.0 %hidden_and_products.1 = (bf16[4,384,768]{2,1,0:T(8,128)(2,1)}, f32[4,8,128]{2,1,0:T(8,128)}, bf16[4,384,1024]{2,1,0:T(8,128)(2,1)}, bf16[2,384,768]{2,1,0:T(8,128)(2,1)}) custom-call(s32[3]{0:T(128)} %pad_add_fusion.place, bf16[128,2176]{1,0:T(8,128)(2,1)} %copy-done.22, ...), custom_call_target="tpu_custom_call", output_to_operand_aliasing={{3}: (12, {})} | custom-call | flops 6442450944 | bytes 22872064 | tf_op jit(solution)/shard_map/hidden_and_products/pallas_call | solution.py:253
  58.7 1.9 collective-permute-done.11.refs_1_.refs_3_
  62.0 3.3 %second_pieces.1 = (bf16[64,2944]{1,0:T(8,128)(2,1)}, bf16[64,2944]{1,0:T(8,128)(2,1)}, bf16[3,128,2944]{2,1,0:T(8,128)(2,1)}) custom-call(bf16[128,2944]{1,0:T(8,128)(2,1)} %collective-permute-done.10.refs_0_.refs_2_, bf16[128,2944]{1,0:T(8,128)(2,1)} %collective-permute-done.11.refs_1_.refs_3_, bf16[128,2944]{1,0:T(8,128)(2,1)} %side_by_side.1.refs_10_.refs_2_.refs_0_, ...), custom_call_target="tpu_custom_call" | custom-call | bytes 4521984 | tf_op jit(solution)/shard_map/second_pieces/pallas_call | solution.py:363
  66.0 6.7 %collective-permute-start.23 = (bf16[2,384,768]{2,1,0:T(8,128)(2,1)}, bf16[2,384,768]{2,1,0:T(8,128)(2,1)S(1)}, u32[]{:S(2)}, u32[]{:S(2)}) collective-permute-start(bf16[2,384,768]{2,1,0:T(8,128)(2,1)} %get-tuple-element.53), channel_id=1, source_target_pairs={{0,8},{24,16},{1,9},{25,17},{2,10},{26,18},{3,11},{27,19},{4,12},{... | collective-permute-start | bytes 3538952 | tf_op jit(solution)/shard_map/ppermute | solution.py:594
  75.7 9.4 %all_to_all.10 = f32[8,4,128]{2,1,0:T(4,128)S(1)} all-to-all(f32[8,4,128]{2,1,0:T(4,128)S(1)} %copy.23), channel_id=1, replica_groups=mesh['dp'=4,'expert'=8] {'expert'}, dimensions={0} | all-to-all | bytes 32768 | tf_op jit(solution)/shard_map/all_to_all | solution.py:610
  92.7 10.0 %far_rows.1 = (bf16[1152,1024]{1,0:T(8,128)(2,1)S(1)}, bf16[1152,1024]{1,0:T(8,128)(2,1)S(1)}, bf16[1152,1024]{1,0:T(8,128)(2,1)}, bf16[1152,1024]{1,0:T(8,128)(2,1)}) custom-call(s32[3]{0:T(128)} %pad_add_fusion.place, bf16[128,2944]{1,0:T(8,128)(2,1)} %side_by_side.1.refs_10_.refs_2_.refs_0_, bf16[3,128,2944]{2,1,0:T(8,128)(2,1)} %collective-permute-done.14.refs_1_, ...), custom_call_target="tpu_custom_call" | custom-call | flops 2013265920 | bytes 9437184 | tf_op jit(solution)/shard_map/far_rows/pallas_call | solution.py:332
  103.8 5.5 %down_terms.4 = (bf16[512,768]{1,0:T(8,128)(2,1)S(1)}, bf16[512,768]{1,0:T(8,128)(2,1)}) custom-call(bf16[1152,1024]{1,0:T(8,128)(2,1)S(1)} %get-tuple-element.45.rows, bf16[4,384,1024]{2,1,0:T(8,128)(2,1)} %get-tuple-element.46.refs_0_, bf16[4,384,768]{2,1,0:T(8,128)(2,1)} %bitcast.28, bf16[2,384,768]{2,1,0:T(8,128)(2,1)} %copy-done.19, ...), custom_call_target="tpu_custom_call" | custom-call | flops 1000 | bytes 1000 | tf_op jit(solution)/shard_map/down_terms/pallas_call | solution.py:444
  113.3 5.7 %down_terms.5 = (bf16[512,768]{1,0:T(8,128)(2,1)S(1)}, bf16[512,768]{1,0:T(8,128)(2,1)}) custom-call(bf16[1152,1024]{1,0:T(8,128)(2,1)S(1)} %get-tuple-element.49.rows, bf16[4,384,1024]{2,1,0:T(8,128)(2,1)} %get-tuple-element.46.refs_0_, bf16[4,384,768]{2,1,0:T(8,128)(2,1)} %bitcast.29, bf16[2,384,768]{2,1,0:T(8,128)(2,1)} %copy-done.19, ...), custom_call_target="tpu_custom_call" | custom-call | flops 1000 | bytes 1000 | tf_op jit(solution)/shard_map/down_terms/pallas_call | solution.py:444
  121.2 10.0 %all_to_all.11 = f32[8,32,256]{2,1,0:T(8,128)} all-to-all(f32[8,32,256]{2,1,0:T(8,128)S(1)} %copy-done.11), channel_id=1, replica_groups=mesh['dp'=4,'expert'=8] {'expert'}, dimensions={0} | all-to-all | bytes 524288 | tf_op jit(solution)/shard_map/all_to_all | solution.py:637
  132.8 8.8 %collective-permute-start.27 = (f32[32,256]{1,0:T(8,128)}, f32[32,256]{1,0:T(8,128)S(1)}, u32[]{:S(2)}, u32[]{:S(2)}) collective-permute-start(f32[32,256]{1,0:T(8,128)} %reduce_sum.29.refs_0_), channel_id=1, source_target_pairs={{0,8},{8,0},{16,24},{24,16},{1,9},{9,1},{17,25},{25,17},{2,10},{10... | collective-permute-start | bytes 98312 | tf_op jit(solution)/shard_map/ppermute | solution.py:640
  141.7 2.4 %collective-permute-start.29 = (f32[32,256]{1,0:T(8,128)}, f32[32,256]{1,0:T(8,128)S(1)}, u32[]{:S(2)}, u32[]{:S(2)}) collective-permute-start(f32[32,256]{1,0:T(8,128)} %reduce_sum.29.refs_0_), channel_id=1, source_target_pairs={{0,24},{8,16},{16,8},{24,0},{1,25},{9,17},{17,9},{25,1},{2,26},{10... | collective-permute-start | bytes 98312 | tf_op jit(solution)/shard_map/ppermute | solution.py:640
  144.1 5.4 %down_terms.6 = (bf16[512,768]{1,0:T(8,128)(2,1)S(1)}, bf16[512,768]{1,0:T(8,128)(2,1)}) custom-call(bf16[1152,1024]{1,0:T(8,128)(2,1)S(1)} %copy-done.8, bf16[4,384,1024]{2,1,0:T(8,128)(2,1)} %get-tuple-element.46.refs_0_, bf16[4,384,768]{2,1,0:T(8,128)(2,1)} %bitcast.30, bf16[2,384,768]{2,1,0:T(8,128)(2,1)} %collective-permute-done.22.refs_2_.refs_6_, ...), custom_call_target="tpu_custom_call" | custom-call | flops 1000 | bytes 1000 | tf_op jit(solution)/shard_map/down_terms/pallas_call | solution.py:444
  151.3 2.2 %add_convert_fusion.3.refs_6_ = bf16[512,768]{1,0:T(8,128)(2,1)} fusion(bf16[512,768]{1,0:T(8,128)(2,1)} %collective-permute-done.20.refs_7_, bf16[512,768]{1,0:T(8,128)(2,1)S(1)} %copy-done.3), kind=kLoop, calls=%fused_computation.4 | loop fusion | flops 1572864 | bytes 2359296 | tf_op jit(solution)/shard_map/convert_element_type | solution.py:632
  153.6 5.4 %down_terms.7 = (bf16[512,768]{1,0:T(8,128)(2,1)S(1)}, bf16[512,768]{1,0:T(8,128)(2,1)}) custom-call(bf16[1152,1024]{1,0:T(8,128)(2,1)S(1)} %copy-done.9, bf16[4,384,1024]{2,1,0:T(8,128)(2,1)} %get-tuple-element.46.refs_0_, bf16[4,384,768]{2,1,0:T(8,128)(2,1)} %bitcast.31, bf16[2,384,768]{2,1,0:T(8,128)(2,1)} %collective-permute-done.22.refs_2_.refs_6_, ...), custom_call_target="tpu_custom_call" | custom-call | flops 1000 | bytes 1000 | tf_op jit(solution)/shard_map/down_terms/pallas_call | solution.py:444
  162.8 8.8 %all-gather = f32[256,256]{1,0:T(8,128)S(1)} all-gather(f32[32,256]{1,0:T(8,128)} %sum_planes.1), channel_id=2, replica_groups=mesh['dp'=4,'expert'=8] {'expert'}, dimensions={0}, use_global_device_ids=true | all-gather | bytes 294912 | tf_op jit(solution)/shard_map/all_gather | solution.py:646
  173.8 13.4 %collective-permute-done.30 = bf16[512,768]{1,0:T(8,128)(2,1)S(1)} collective-permute-done((bf16[512,768]{1,0:T(8,128)(2,1)}, bf16[512,768]{1,0:T(8,128)(2,1)S(1)}, u32[]{:S(2)}, u32[]{:S(2)}) %collective-permute-start.30) | collective-permute-done | bytes 786464 | tf_op jit(solution)/shard_map/ppermute | solution.py:629
  (145 shorter events, 48.1 us)
Async XLA Ops:
  2.7 15.6 %collective-permute-start = (bf16[128,2176]{1,0:T(8,128)(2,1)S(1)}, bf16[128,2176]{1,0:T(8,128)(2,1)S(1)}, u32[]{:S(2)}, u32[]{:S(2)}) collective-permute-start(bf16[128,2176]{1,0:T(8,128)(2,1)S(1)} %pad_maximum_fusion.1.refs_2_.refs_0_), channel_id=1, source_target_pairs={{0,2},{1,3},{2,0},{3,1},{4,6},{5,7},{6,4},{7,5},{8,10},{9,11},{10,... | collective-permute-start | bytes 1671176 | tf_op jit(solution)/shard_map/ppermute | solution.py:96
  5.7 17.5 %collective-permute-start.1 = (bf16[128,2176]{1,0:T(8,128)(2,1)S(1)}, bf16[128,2176]{1,0:T(8,128)(2,1)S(1)}, u32[]{:S(2)}, u32[]{:S(2)}) collective-permute-start(bf16[128,2176]{1,0:T(8,128)(2,1)S(1)} %pad_maximum_fusion.1.refs_2_.refs_0_), channel_id=1, source_target_pairs={{0,4},{1,5},{2,6},{3,7},{4,0},{5,1},{6,2},{7,3},{8,12},{9,13},{10,... | collective-permute-start | bytes 1671176 | tf_op jit(solution)/shard_map/ppermute | solution.py:96
  7.3 15.8 %collective-permute-start.2 = (bf16[128,1152]{1,0:T(8,128)(2,1)S(1)}, bf16[128,1152]{1,0:T(8,128)(2,1)S(1)}, u32[]{:S(2)}, u32[]{:S(2)}) collective-permute-start(bf16[128,1152]{1,0:T(8,128)(2,1)S(1)} %pad_maximum_fusion.2), channel_id=1, source_target_pairs={{8,16},{16,8},{9,17},{17,9},{10,18},{18,10},{11,19},{19,11},{12,20... | collective-permute-start | bytes 884744 | tf_op jit(solution)/shard_map/ppermute | solution.py:540
  8.0 15.2 %collective-permute-start.3 = (bf16[128,1152]{1,0:T(8,128)(2,1)S(1)}, bf16[128,1152]{1,0:T(8,128)(2,1)S(1)}, u32[]{:S(2)}, u32[]{:S(2)}) collective-permute-start(bf16[128,1152]{1,0:T(8,128)(2,1)S(1)} %pad_maximum_fusion.2), channel_id=1, source_target_pairs={{0,16},{24,8},{1,17},{25,9},{2,18},{26,10},{3,19},{27,11},{4,20},{... | collective-permute-start | bytes 884744 | tf_op jit(solution)/shard_map/ppermute | solution.py:541
  27.0 16.2 %collective-permute-start.5 = (bf16[3,128,2176]{2,1,0:T(8,128)(2,1)}, bf16[3,128,2176]{2,1,0:T(8,128)(2,1)}, u32[]{:S(2)}, u32[]{:S(2)}) collective-permute-start(bf16[3,128,2176]{2,1,0:T(8,128)(2,1)} %get-tuple-element.33), channel_id=1, source_target_pairs={{0,1},{1,0},{2,3},{3,2},{4,5},{5,4},{6,7},{7,6},{8,9},{9,8},{10,11... | collective-permute-start | bytes 5013512 | tf_op jit(solution)/shard_map/ppermute | solution.py:96
  29.5 31.1 %collective-permute-start.12 = (bf16[2,384,768]{2,1,0:T(8,128)(2,1)}, bf16[2,384,768]{2,1,0:T(8,128)(2,1)S(1)}, u32[]{:S(2)}, u32[]{:S(2)}) collective-permute-start(bf16[2,384,768]{2,1,0:T(8,128)(2,1)} %get-tuple-element.32.refs_6_), channel_id=1, source_target_pairs={{0,8},{24,16},{1,9},{25,17},{2,10},{26,18},{3,11},{27,19},{4,12},{... | collective-permute-start | bytes 3538952 | tf_op jit(solution)/shard_map/ppermute | solution.py:574
  33.0 27.6 %collective-permute-start.13 = (bf16[2,384,768]{2,1,0:T(8,128)(2,1)}, bf16[2,384,768]{2,1,0:T(8,128)(2,1)S(1)}, u32[]{:S(2)}, u32[]{:S(2)}) collective-permute-start(bf16[2,384,768]{2,1,0:T(8,128)(2,1)} %get-tuple-element.32.refs_6_), channel_id=1, source_target_pairs={{8,16},{16,8},{9,17},{17,9},{10,18},{18,10},{11,19},{19,11},{12,20... | collective-permute-start | bytes 3538952 | tf_op jit(solution)/shard_map/ppermute | solution.py:573
  39.8 18.9 %collective-permute-start.10 = (bf16[128,2944]{1,0:T(8,128)(2,1)}, bf16[128,2944]{1,0:T(8,128)(2,1)}, u32[]{:S(2)}, u32[]{:S(2)}) collective-permute-start(bf16[128,2944]{1,0:T(8,128)(2,1)} %side_by_side.1.refs_10_.refs_2_.refs_0_), channel_id=1, source_target_pairs={{0,2},{1,3},{2,0},{3,1},{4,6},{5,7},{6,4},{7,5},{8,10},{9,11},{10,... | collective-permute-start | bytes 2261000 | tf_op jit(solution)/shard_map/ppermute | solution.py:96
  42.0 18.6 %collective-permute-start.11 = (bf16[128,2944]{1,0:T(8,128)(2,1)}, bf16[128,2944]{1,0:T(8,128)(2,1)}, u32[]{:S(2)}, u32[]{:S(2)}) collective-permute-start(bf16[128,2944]{1,0:T(8,128)(2,1)} %side_by_side.1.refs_10_.refs_2_.refs_0_), channel_id=1, source_target_pairs={{0,4},{1,5},{2,6},{3,7},{4,0},{5,1},{6,2},{7,3},{8,12},{9,13},{10,... | collective-permute-start | bytes 2261000 | tf_op jit(solution)/shard_map/ppermute | solution.py:96
  65.3 26.7 %collective-permute-start.14 = (bf16[3,128,2944]{2,1,0:T(8,128)(2,1)}, bf16[3,128,2944]{2,1,0:T(8,128)(2,1)}, u32[]{:S(2)}, u32[]{:S(2)}) collective-permute-start(bf16[3,128,2944]{2,1,0:T(8,128)(2,1)} %get-tuple-element.38), channel_id=1, source_target_pairs={{0,1},{1,0},{2,3},{3,2},{4,5},{5,4},{6,7},{7,6},{8,9},{9,8},{10,11... | collective-permute-start | bytes 6782984 | tf_op jit(solution)/shard_map/ppermute | solution.py:96
  65.3 37.4 %collective-permute-start.19 = (bf16[2,384,768]{2,1,0:T(8,128)(2,1)}, bf16[2,384,768]{2,1,0:T(8,128)(2,1)S(1)}, u32[]{:S(2)}, u32[]{:S(2)}) collective-permute-start(bf16[2,384,768]{2,1,0:T(8,128)(2,1)} %copy-done.18), channel_id=1, source_target_pairs={{8,16},{16,8},{9,17},{17,9},{10,18},{18,10},{11,19},{19,11},{12,20... | collective-permute-start | bytes 3538952 | tf_op jit(solution)/shard_map/ppermute | solution.py:595
  66.0 44.6 %collective-permute-start.23 = (bf16[2,384,768]{2,1,0:T(8,128)(2,1)}, bf16[2,384,768]{2,1,0:T(8,128)(2,1)S(1)}, u32[]{:S(2)}, u32[]{:S(2)}) collective-permute-start(bf16[2,384,768]{2,1,0:T(8,128)(2,1)} %get-tuple-element.53), channel_id=1, source_target_pairs={{0,8},{24,16},{1,9},{25,17},{2,10},{26,18},{3,11},{27,19},{4,12},{... | collective-permute-start | bytes 3538952 | tf_op jit(solution)/shard_map/ppermute | solution.py:594
  72.8 14.8 %collective-permute-start.15 = (bf16[64,2944]{1,0:T(8,128)(2,1)}, bf16[64,2944]{1,0:T(8,128)(2,1)S(1)}, u32[]{:S(2)}, u32[]{:S(2)}) collective-permute-start(bf16[64,2944]{1,0:T(8,128)(2,1)} %get-tuple-element.39.__1_), channel_id=1, source_target_pairs={{0,4},{1,5},{2,6},{3,7},{4,0},{5,1},{6,2},{7,3},{8,12},{9,13},{10,... | collective-permute-start | bytes 1130504 | tf_op jit(solution)/shard_map/ppermute | solution.py:96
  73.9 13.7 %collective-permute-start.16 = (bf16[64,2944]{1,0:T(8,128)(2,1)}, bf16[64,2944]{1,0:T(8,128)(2,1)}, u32[]{:S(2)}, u32[]{:S(2)}) collective-permute-start(bf16[64,2944]{1,0:T(8,128)(2,1)} %get-tuple-element.40.__2_), channel_id=1, source_target_pairs={{0,2},{1,3},{2,0},{3,1},{4,6},{5,7},{6,4},{7,5},{8,10},{9,11},{10,... | collective-permute-start | bytes 1130504 | tf_op jit(solution)/shard_map/ppermute | solution.py:96
  90.2 42.6 %collective-permute-start.22 = (bf16[2,384,768]{2,1,0:T(8,128)(2,1)}, bf16[2,384,768]{2,1,0:T(8,128)(2,1)}, u32[]{:S(2)}, u32[]{:S(2)}) collective-permute-start(bf16[2,384,768]{2,1,0:T(8,128)(2,1)} %get-tuple-element.53), channel_id=1, source_target_pairs={{8,16},{16,8},{9,17},{17,9},{10,18},{18,10},{11,19},{19,11},{12,20... | collective-permute-start | bytes 3538952 | tf_op jit(solution)/shard_map/ppermute | solution.py:593
  109.4 32.3 %collective-permute-start.20 = (bf16[512,768]{1,0:T(8,128)(2,1)}, bf16[512,768]{1,0:T(8,128)(2,1)}, u32[]{:S(2)}, u32[]{:S(2)}) collective-permute-start(bf16[512,768]{1,0:T(8,128)(2,1)} %get-tuple-element.48), channel_id=1, source_target_pairs={{8,0},{16,24},{9,1},{17,25},{10,2},{18,26},{11,3},{19,27},{12,4},{... | collective-permute-start | bytes 2359304 | tf_op jit(solution)/shard_map/ppermute | solution.py:629
  111.9 29.8 %collective-permute-start.24 = (bf16[1,384,768]{2,1,0:T(8,128)(2,1)}, bf16[1,384,768]{2,1,0:T(8,128)(2,1)S(1)}, u32[]{:S(2)}, u32[]{:S(2)}) collective-permute-start(bf16[1,384,768]{2,1,0:T(8,128)(2,1)} %get-tuple-element.62), channel_id=1, source_target_pairs={{8,16},{16,8},{9,17},{17,9},{10,18},{18,10},{11,19},{19,11},{12,20... | collective-permute-start | bytes 1769480 | tf_op jit(solution)/shard_map/ppermute | solution.py:597
  112.6 41.0 %collective-permute-start.26 = (bf16[1,384,768]{2,1,0:T(8,128)(2,1)}, bf16[1,384,768]{2,1,0:T(8,128)(2,1)S(1)}, u32[]{:S(2)}, u32[]{:S(2)}) collective-permute-start(bf16[1,384,768]{2,1,0:T(8,128)(2,1)} %get-tuple-element.63), channel_id=1, source_target_pairs={{8,16},{16,8},{9,17},{17,9},{10,18},{18,10},{11,19},{19,11},{12,20... | collective-permute-start | bytes 1769480 | tf_op jit(solution)/shard_map/ppermute | solution.py:597
  119.9 52.3 %collective-permute-start.21 = (bf16[512,768]{1,0:T(8,128)(2,1)}, bf16[512,768]{1,0:T(8,128)(2,1)}, u32[]{:S(2)}, u32[]{:S(2)}) collective-permute-start(bf16[512,768]{1,0:T(8,128)(2,1)} %get-tuple-element.51), channel_id=1, source_target_pairs={{8,0},{16,24},{9,1},{17,25},{10,2},{18,26},{11,3},{19,27},{12,4},{... | collective-permute-start | bytes 2359304 | tf_op jit(solution)/shard_map/ppermute | solution.py:629
  132.8 16.9 %collective-permute-start.27 = (f32[32,256]{1,0:T(8,128)}, f32[32,256]{1,0:T(8,128)S(1)}, u32[]{:S(2)}, u32[]{:S(2)}) collective-permute-start(f32[32,256]{1,0:T(8,128)} %reduce_sum.29.refs_0_), channel_id=1, source_target_pairs={{0,8},{8,0},{16,24},{24,16},{1,9},{9,1},{17,25},{25,17},{2,10},{10... | collective-permute-start | bytes 98312 | tf_op jit(solution)/shard_map/ppermute | solution.py:640
  141.7 11.9 %collective-permute-start.28 = (f32[32,256]{1,0:T(8,128)}, f32[32,256]{1,0:T(8,128)S(1)}, u32[]{:S(2)}, u32[]{:S(2)}) collective-permute-start(f32[32,256]{1,0:T(8,128)} %reduce_sum.29.refs_0_), channel_id=1, source_target_pairs={{0,16},{8,24},{16,0},{24,8},{1,17},{9,25},{17,1},{25,9},{2,18},{10... | collective-permute-start | bytes 98312 | tf_op jit(solution)/shard_map/ppermute | solution.py:640
  141.7 11.9 %collective-permute-start.29 = (f32[32,256]{1,0:T(8,128)}, f32[32,256]{1,0:T(8,128)S(1)}, u32[]{:S(2)}, u32[]{:S(2)}) collective-permute-start(f32[32,256]{1,0:T(8,128)} %reduce_sum.29.refs_0_), channel_id=1, source_target_pairs={{0,24},{8,16},{16,8},{24,0},{1,25},{9,17},{17,9},{25,1},{2,26},{10... | collective-permute-start | bytes 98312 | tf_op jit(solution)/shard_map/ppermute | solution.py:640
  149.8 23.9 %collective-permute-start.25 = (bf16[512,768]{1,0:T(8,128)(2,1)}, bf16[512,768]{1,0:T(8,128)(2,1)S(1)}, u32[]{:S(2)}, u32[]{:S(2)}) collective-permute-start(bf16[512,768]{1,0:T(8,128)(2,1)} %get-tuple-element.55), channel_id=1, source_target_pairs={{8,0},{16,24},{9,1},{17,25},{10,2},{18,26},{11,3},{19,27},{12,4},{... | collective-permute-start | bytes 2359304 | tf_op jit(solution)/shard_map/ppermute | solution.py:629
  159.9 27.4 %collective-permute-start.30 = (bf16[512,768]{1,0:T(8,128)(2,1)}, bf16[512,768]{1,0:T(8,128)(2,1)S(1)}, u32[]{:S(2)}, u32[]{:S(2)}) collective-permute-start(bf16[512,768]{1,0:T(8,128)(2,1)} %get-tuple-element.58), channel_id=1, source_target_pairs={{8,0},{16,24},{9,1},{17,25},{10,2},{18,26},{11,3},{19,27},{12,4},{... | collective-permute-start | bytes 2359304 | tf_op jit(solution)/shard_map/ppermute | solution.py:629
  (43 other events, 261.2 us)

commit v6 on v5

--- a/solution.py
+++ b/solution.py
@@ -334,14 +334,14 @@
         in_specs=[pl.BlockSpec(memory_space=pltpu.SMEM)]
         + [pl.BlockSpec(memory_space=pltpu.VMEM)] * len(flat)
         + [ANYWHERE] * len(after),
-        out_specs=[pl.BlockSpec(memory_space=pltpu.VMEM)] * 2 + [ANYWHERE] * (local_experts - 2),
-        out_shape=[pltpu.VMEM(shape, BF16)] * 2
-        + [jax.ShapeDtypeStruct(shape, BF16)] * (local_experts - 2),
+        out_specs=[pl.BlockSpec(memory_space=pltpu.VMEM)] * 3 + [ANYWHERE] * (local_experts - 3),
+        out_shape=[pltpu.VMEM(shape, BF16)] * 3
+        + [jax.ShapeDtypeStruct(shape, BF16)] * (local_experts - 3),
         scratch_shapes=[
             pltpu.VMEM((local_experts, *shape), BF16),
             pltpu.SemaphoreType.DMA((len(widths), local_experts)),
         ],
-        compiler_params=pltpu.CompilerParams(vmem_limit_bytes=56 * MIB),
+        compiler_params=pltpu.CompilerParams(vmem_limit_bytes=44 * MIB),
         cost_estimate=pl.CostEstimate(
             flops=2 * local_experts * 8 * capacity * 256 * sum(widths),
             bytes_accessed=2 * local_experts * shape[0] * shape[1],

time: 190 us -> 191 us (level)
  starting transfers between devices: 51.5 us -> 53.6 us
    unnamed x72 -> x78, local copies, waits for them, and re-layouts: 9.81 us -> 10.3 us
  transfers between devices with their start and end apart: 31 -> 31, of which waited for: 9 -> 9; matrix products, arithmetic and copies ran while one was open for 5% -> 4% of each run, Pallas kernels for 29% -> 29%
where the time goes in v6:
time: 191 us; the launch traced here: 190 us
  Pallas kernels  60.7 us (32%)
  starting transfers between devices  53.6 us (28%)
  blocking collectives  27.9 us (15%)
  waiting for transfers between devices  23.6 us (12%)
  local copies, waits for them, and re-layouts  14 us (7%)
  other arithmetic  8.38 us (4%)
    pallas_call x4, Pallas kernels, down_call(): pl.pallas_call(functools.partial(down_kernel, places, len(after)), in_spe...  22.1 us
    pallas_call x1, Pallas kernels, hidden_call(): pl.pallas_call(kernel, grid_spec=pltpu.PrefetchScalarGridSpec(num_scalar_...  15 us
    ppermute x4, waiting for transfers between devices, down(): return (own, lax.ppermute(other, 'dp', OUTWARD))  13.3 us
    ppermute x14, starting transfers between devices, plane_swap(): return lax.ppermute(x, 'expert', [(i, i ^ bits) for i in range(8)])  12 us
    pallas_call x4, Pallas kernels, copies(): pl.pallas_call(functools.partial(copy_kernel, moves, len(sources) + len(a...  11.4 us
    ppermute x3, starting transfers between devices, local_line(): lax.ppermute(reduced, 'dp', [(i, i ^ k) for i in range(4)])  10.6 us
    unnamed x78, local copies, waits for them, and re-layouts  10.3 us
    all_to_all x1, blocking collectives, local_line(): lax.all_to_all(router_part, 'expert', split_axis=0, concat_axis=0)  9.89 us
  transfers between devices with their start and end apart: 31, of which 9 were waited for; matrix products, arithmetic and copies ran while one was open for 4% of the time, Pallas kernels for 29%

profile of v6, /device:TPU:0, one launch (start us, length us, event | category | flops | bytes accessed | tf_op | source)
XLA Modules:
  0.0 189.6 jit_solution(11393812419261849517)
XLA Ops:
  2.7 3.0 %collective-permute-start = (bf16[128,2176]{1,0:T(8,128)(2,1)S(1)}, bf16[128,2176]{1,0:T(8,128)(2,1)S(1)}, u32[]{:S(2)}, u32[]{:S(2)}) collective-permute-start(bf16[128,2176]{1,0:T(8,128)(2,1)S(1)} %pad_maximum_fusion.1.refs_2_.refs_0_), channel_id=1, source_target_pairs={{0,2},{1,3},{2,0},{3,1},{4,6},{5,7},{6,4},{7,5},{8,10},{9,11},{10,... | collective-permute-start | bytes 1671176 | tf_op jit(solution)/shard_map/ppermute | solution.py:96
  8.0 6.2 %collective-permute-start.3 = (bf16[128,1152]{1,0:T(8,128)(2,1)S(1)}, bf16[128,1152]{1,0:T(8,128)(2,1)S(1)}, u32[]{:S(2)}, u32[]{:S(2)}) collective-permute-start(bf16[128,1152]{1,0:T(8,128)(2,1)S(1)} %pad_maximum_fusion.2), channel_id=1, source_target_pairs={{0,16},{24,8},{1,17},{25,9},{2,18},{26,10},{3,19},{27,11},{4,20},{... | collective-permute-start | bytes 884744 | tf_op jit(solution)/shard_map/ppermute | solution.py:541
  15.6 2.7 %collective-permute-done.refs_1_.refs_0_.refs_2_ = bf16[128,2176]{1,0:T(8,128)(2,1)S(1)} collective-permute-done((bf16[128,2176]{1,0:T(8,128)(2,1)S(1)}, bf16[128,2176]{1,0:T(8,128)(2,1)S(1)}, u32[]{:S(2)}, u32[]{:S(2)}) %collective-permute-start) | collective-permute-done | bytes 557088 | tf_op jit(solution)/shard_map/ppermute | solution.py:96
  19.2 3.2 %acts_pieces.1 = (bf16[2,384,768]{2,1,0:T(8,128)(2,1)}, bf16[2,384,768]{2,1,0:T(8,128)(2,1)}) custom-call(bf16[4,384,768]{2,1,0:T(8,128)(2,1)} %bitcast.26, bf16[128,2176]{1,0:T(8,128)(2,1)} %copy-done.27), custom_call_target="tpu_custom_call" | custom-call | bytes 4718592 | tf_op jit(solution)/shard_map/acts_pieces/pallas_call | solution.py:363
  24.2 2.8 %first_pieces.1 = (bf16[64,2176]{1,0:T(8,128)(2,1)}, bf16[64,2176]{1,0:T(8,128)(2,1)}, bf16[3,128,2176]{2,1,0:T(8,128)(2,1)}) custom-call(bf16[128,2176]{1,0:T(8,128)(2,1)} %copy-done.27, bf16[128,2176]{1,0:T(8,128)(2,1)} %copy-done.33, bf16[128,2176]{1,0:T(8,128)(2,1)} %copy-done.26, bf16[128,1152]{1,0:T(8,128)(2,1)} %copy-done.29, ...), custom_call_target="tpu_custom_call" | custom-call | bytes 3342336 | tf_op jit(solution)/shard_map/first_pieces/pallas_call | solution.py:363
  29.5 3.5 %collective-permute-start.12 = (bf16[2,384,768]{2,1,0:T(8,128)(2,1)}, bf16[2,384,768]{2,1,0:T(8,128)(2,1)S(1)}, u32[]{:S(2)}, u32[]{:S(2)}) collective-permute-start(bf16[2,384,768]{2,1,0:T(8,128)(2,1)} %get-tuple-element.32.refs_6_), channel_id=1, source_target_pairs={{0,8},{24,16},{1,9},{25,17},{2,10},{26,18},{3,11},{27,19},{4,12},{... | collective-permute-start | bytes 3538952 | tf_op jit(solution)/shard_map/ppermute | solution.py:574
  37.7 2.1 %side_by_side.1.refs_10_.refs_2_.refs_0_ = bf16[128,2944]{1,0:T(8,128)(2,1)} custom-call(bf16[128,1152]{1,0:T(8,128)(2,1)} %copy-done.29, bf16[128,1152]{1,0:T(8,128)(2,1)} %copy-done.30, bf16[128,640]{1,0:T(8,128)(2,1)} %copy-done.32, bf16[64,2176]{1,0:T(8,128)(2,1)} %copy-done.34, bf16[64,2176]{1,0:T(8,128)(2,1)} %copy-done.35), custom_call_target="tpu_custom_call" | custom-call | bytes 1507328 | tf_op jit(solution)/shard_map/side_by_side/pallas_call | solution.py:363
  42.4 15.0 %hidden_and_products.1 = (bf16[4,384,768]{2,1,0:T(8,128)(2,1)}, f32[4,8,128]{2,1,0:T(8,128)}, bf16[4,384,1024]{2,1,0:T(8,128)(2,1)}, bf16[2,384,768]{2,1,0:T(8,128)(2,1)}) custom-call(s32[3]{0:T(128)} %pad_add_fusion.place, bf16[128,2176]{1,0:T(8,128)(2,1)} %copy-done.26, ...), custom_call_target="tpu_custom_call", output_to_operand_aliasing={{3}: (12, {})} | custom-call | flops 6442450944 | bytes 22872064 | tf_op jit(solution)/shard_map/hidden_and_products/pallas_call | solution.py:253
  61.0 3.4 %second_pieces.1 = (bf16[64,2944]{1,0:T(8,128)(2,1)}, bf16[64,2944]{1,0:T(8,128)(2,1)}, bf16[3,128,2944]{2,1,0:T(8,128)(2,1)}) custom-call(bf16[128,2944]{1,0:T(8,128)(2,1)} %copy-done.12, bf16[128,2944]{1,0:T(8,128)(2,1)} %copy-done.31, bf16[128,2944]{1,0:T(8,128)(2,1)} %side_by_side.1.refs_10_.refs_2_.refs_0_, ...), custom_call_target="tpu_custom_call" | custom-call | bytes 4521984 | tf_op jit(solution)/shard_map/second_pieces/pallas_call | solution.py:363
  66.2 6.3 %collective-permute-start.23 = (bf16[2,384,768]{2,1,0:T(8,128)(2,1)}, bf16[2,384,768]{2,1,0:T(8,128)(2,1)}, u32[]{:S(2)}, u32[]{:S(2)}) collective-permute-start(bf16[2,384,768]{2,1,0:T(8,128)(2,1)} %get-tuple-element.53), channel_id=1, source_target_pairs={{0,8},{24,16},{1,9},{25,17},{2,10},{26,18},{3,11},{27,19},{4,12},{... | collective-permute-start | bytes 3538952 | tf_op jit(solution)/shard_map/ppermute | solution.py:594
  75.7 8.8 %all_to_all.10 = f32[8,4,128]{2,1,0:T(4,128)S(1)} all-to-all(f32[8,4,128]{2,1,0:T(4,128)S(1)} %copy.23), channel_id=1, replica_groups=mesh['dp'=4,'expert'=8] {'expert'}, dimensions={0} | all-to-all | bytes 32768 | tf_op jit(solution)/shard_map/all_to_all | solution.py:610
  94.7 8.9 %far_rows.1 = (bf16[1152,1024]{1,0:T(8,128)(2,1)S(1)}, bf16[1152,1024]{1,0:T(8,128)(2,1)S(1)}, bf16[1152,1024]{1,0:T(8,128)(2,1)S(1)}, bf16[1152,1024]{1,0:T(8,128)(2,1)}) custom-call(s32[3]{0:T(128)S(1)} %copy-done.23, bf16[128,2944]{1,0:T(8,128)(2,1)S(1)} %copy-done.8, bf16[3,128,2944]{2,1,0:T(8,128)(2,1)} %collective-permute-done.14.refs_1_, ...), custom_call_target="tpu_custom_call" | custom-call | flops 2013265920 | bytes 9437184 | tf_op jit(solution)/shard_map/far_rows/pallas_call | solution.py:332
  103.7 5.5 %down_terms.4 = (bf16[512,768]{1,0:T(8,128)(2,1)S(1)}, bf16[512,768]{1,0:T(8,128)(2,1)}) custom-call(bf16[1152,1024]{1,0:T(8,128)(2,1)S(1)} %get-tuple-element.45.rows, bf16[4,384,1024]{2,1,0:T(8,128)(2,1)} %get-tuple-element.46.refs_0_, bf16[4,384,768]{2,1,0:T(8,128)(2,1)} %bitcast.28, bf16[2,384,768]{2,1,0:T(8,128)(2,1)} %collective-permute-done.13.refs_5_.refs_2_, ...), custom_call_target="tpu_custom_call" | custom-call | flops 1000 | bytes 1000 | tf_op jit(solution)/shard_map/down_terms/pallas_call | solution.py:444
  110.5 2.3 %fusion.5 = (bf16[1,384,768]{2,1,0:T(8,128)(2,1)}, bf16[1,384,768]{2,1,0:T(8,128)(2,1)}) fusion(bf16[2,384,768]{2,1,0:T(8,128)(2,1)} %collective-permute-done.23.refs_4_), kind=kLoop, calls=%fused_computation.27 | loop fusion | bytes 2359296 | tf_op jit(solution)/shard_map/slice | solution.py:597
  115.1 5.6 %down_terms.5 = (bf16[512,768]{1,0:T(8,128)(2,1)S(1)}, bf16[512,768]{1,0:T(8,128)(2,1)}) custom-call(bf16[1152,1024]{1,0:T(8,128)(2,1)S(1)} %get-tuple-element.49.rows, bf16[4,384,1024]{2,1,0:T(8,128)(2,1)} %get-tuple-element.46.refs_0_, bf16[4,384,768]{2,1,0:T(8,128)(2,1)} %bitcast.29, bf16[2,384,768]{2,1,0:T(8,128)(2,1)} %collective-permute-done.13.refs_5_.refs_2_, ...), custom_call_target="tpu_custom_call" | custom-call | flops 1000 | bytes 1000 | tf_op jit(solution)/shard_map/down_terms/pallas_call | solution.py:444
  122.9 9.9 %all_to_all.11 = f32[8,32,256]{2,1,0:T(8,128)S(1)} all-to-all(f32[8,32,256]{2,1,0:T(8,128)S(1)} %copy-done.11), channel_id=1, replica_groups=mesh['dp'=4,'expert'=8] {'expert'}, dimensions={0} | all-to-all | bytes 524288 | tf_op jit(solution)/shard_map/all_to_all | solution.py:637
  132.8 8.2 %collective-permute-start.27 = (f32[32,256]{1,0:T(8,128)S(1)}, f32[32,256]{1,0:T(8,128)S(1)}, u32[]{:S(2)}, u32[]{:S(2)}) collective-permute-start(f32[32,256]{1,0:T(8,128)S(1)} %reduce_sum.29.refs_0_), channel_id=1, source_target_pairs={{0,8},{8,0},{16,24},{24,16},{1,9},{9,1},{17,25},{25,17},{2,10},{10... | collective-permute-start | bytes 98312 | tf_op jit(solution)/shard_map/ppermute | solution.py:640
  141.0 2.4 %collective-permute-start.29 = (f32[32,256]{1,0:T(8,128)S(1)}, f32[32,256]{1,0:T(8,128)S(1)}, u32[]{:S(2)}, u32[]{:S(2)}) collective-permute-start(f32[32,256]{1,0:T(8,128)S(1)} %reduce_sum.29.refs_0_), channel_id=1, source_target_pairs={{0,24},{8,16},{16,8},{24,0},{1,25},{9,17},{17,9},{25,1},{2,26},{10... | collective-permute-start | bytes 98312 | tf_op jit(solution)/shard_map/ppermute | solution.py:640
  143.5 5.6 %down_terms.6 = (bf16[512,768]{1,0:T(8,128)(2,1)S(1)}, bf16[512,768]{1,0:T(8,128)(2,1)}) custom-call(bf16[1152,1024]{1,0:T(8,128)(2,1)S(1)} %get-tuple-element.52.rows, bf16[4,384,1024]{2,1,0:T(8,128)(2,1)} %get-tuple-element.46.refs_0_, bf16[4,384,768]{2,1,0:T(8,128)(2,1)} %bitcast.30, bf16[2,384,768]{2,1,0:T(8,128)(2,1)} %collective-permute-done.22.refs_2_.refs_6_, ...), custom_call_target="tpu_custom_call" | custom-call | flops 1000 | bytes 1000 | tf_op jit(solution)/shard_map/down_terms/pallas_call | solution.py:444
  151.3 2.2 %add_convert_fusion.3.refs_6_ = bf16[512,768]{1,0:T(8,128)(2,1)} fusion(bf16[512,768]{1,0:T(8,128)(2,1)} %collective-permute-done.20.refs_7_, bf16[512,768]{1,0:T(8,128)(2,1)S(1)} %copy-done.3), kind=kLoop, calls=%fused_computation.4 | loop fusion | flops 1572864 | bytes 2359296 | tf_op jit(solution)/shard_map/convert_element_type | solution.py:632
  153.6 5.4 %down_terms.7 = (bf16[512,768]{1,0:T(8,128)(2,1)S(1)}, bf16[512,768]{1,0:T(8,128)(2,1)}) custom-call(bf16[1152,1024]{1,0:T(8,128)(2,1)S(1)} %copy-done.9, bf16[4,384,1024]{2,1,0:T(8,128)(2,1)} %get-tuple-element.46.refs_0_, bf16[4,384,768]{2,1,0:T(8,128)(2,1)} %bitcast.31, bf16[2,384,768]{2,1,0:T(8,128)(2,1)} %collective-permute-done.22.refs_2_.refs_6_, ...), custom_call_target="tpu_custom_call" | custom-call | flops 1000 | bytes 1000 | tf_op jit(solution)/shard_map/down_terms/pallas_call | solution.py:444
  162.7 9.2 %all-gather = f32[256,256]{1,0:T(8,128)S(1)} all-gather(f32[32,256]{1,0:T(8,128)} %sum_planes.1), channel_id=2, replica_groups=mesh['dp'=4,'expert'=8] {'expert'}, dimensions={0}, use_global_device_ids=true | all-gather | bytes 294912 | tf_op jit(solution)/shard_map/all_gather | solution.py:646
  174.2 13.3 %collective-permute-done.30 = bf16[512,768]{1,0:T(8,128)(2,1)S(1)} collective-permute-done((bf16[512,768]{1,0:T(8,128)(2,1)}, bf16[512,768]{1,0:T(8,128)(2,1)S(1)}, u32[]{:S(2)}, u32[]{:S(2)}) %collective-permute-start.30) | collective-permute-done | bytes 786464 | tf_op jit(solution)/shard_map/ppermute | solution.py:629
  187.7 1.9 pad_maximum_fusion
  (151 shorter events, 50.9 us)
Async XLA Ops:
  2.7 15.6 %collective-permute-start = (bf16[128,2176]{1,0:T(8,128)(2,1)S(1)}, bf16[128,2176]{1,0:T(8,128)(2,1)S(1)}, u32[]{:S(2)}, u32[]{:S(2)}) collective-permute-start(bf16[128,2176]{1,0:T(8,128)(2,1)S(1)} %pad_maximum_fusion.1.refs_2_.refs_0_), channel_id=1, source_target_pairs={{0,2},{1,3},{2,0},{3,1},{4,6},{5,7},{6,4},{7,5},{8,10},{9,11},{10,... | collective-permute-start | bytes 1671176 | tf_op jit(solution)/shard_map/ppermute | solution.py:96
  5.7 17.5 %collective-permute-start.1 = (bf16[128,2176]{1,0:T(8,128)(2,1)S(1)}, bf16[128,2176]{1,0:T(8,128)(2,1)S(1)}, u32[]{:S(2)}, u32[]{:S(2)}) collective-permute-start(bf16[128,2176]{1,0:T(8,128)(2,1)S(1)} %pad_maximum_fusion.1.refs_2_.refs_0_), channel_id=1, source_target_pairs={{0,4},{1,5},{2,6},{3,7},{4,0},{5,1},{6,2},{7,3},{8,12},{9,13},{10,... | collective-permute-start | bytes 1671176 | tf_op jit(solution)/shard_map/ppermute | solution.py:96
  7.3 15.8 %collective-permute-start.2 = (bf16[128,1152]{1,0:T(8,128)(2,1)S(1)}, bf16[128,1152]{1,0:T(8,128)(2,1)S(1)}, u32[]{:S(2)}, u32[]{:S(2)}) collective-permute-start(bf16[128,1152]{1,0:T(8,128)(2,1)S(1)} %pad_maximum_fusion.2), channel_id=1, source_target_pairs={{8,16},{16,8},{9,17},{17,9},{10,18},{18,10},{11,19},{19,11},{12,20... | collective-permute-start | bytes 884744 | tf_op jit(solution)/shard_map/ppermute | solution.py:540
  8.0 15.2 %collective-permute-start.3 = (bf16[128,1152]{1,0:T(8,128)(2,1)S(1)}, bf16[128,1152]{1,0:T(8,128)(2,1)S(1)}, u32[]{:S(2)}, u32[]{:S(2)}) collective-permute-start(bf16[128,1152]{1,0:T(8,128)(2,1)S(1)} %pad_maximum_fusion.2), channel_id=1, source_target_pairs={{0,16},{24,8},{1,17},{25,9},{2,18},{26,10},{3,19},{27,11},{4,20},{... | collective-permute-start | bytes 884744 | tf_op jit(solution)/shard_map/ppermute | solution.py:541
  27.0 15.4 %collective-permute-start.5 = (bf16[3,128,2176]{2,1,0:T(8,128)(2,1)}, bf16[3,128,2176]{2,1,0:T(8,128)(2,1)}, u32[]{:S(2)}, u32[]{:S(2)}) collective-permute-start(bf16[3,128,2176]{2,1,0:T(8,128)(2,1)} %get-tuple-element.33), channel_id=1, source_target_pairs={{0,1},{1,0},{2,3},{3,2},{4,5},{5,4},{6,7},{7,6},{8,9},{9,8},{10,11... | collective-permute-start | bytes 5013512 | tf_op jit(solution)/shard_map/ppermute | solution.py:96
  29.5 30.3 %collective-permute-start.12 = (bf16[2,384,768]{2,1,0:T(8,128)(2,1)}, bf16[2,384,768]{2,1,0:T(8,128)(2,1)S(1)}, u32[]{:S(2)}, u32[]{:S(2)}) collective-permute-start(bf16[2,384,768]{2,1,0:T(8,128)(2,1)} %get-tuple-element.32.refs_6_), channel_id=1, source_target_pairs={{0,8},{24,16},{1,9},{25,17},{2,10},{26,18},{3,11},{27,19},{4,12},{... | collective-permute-start | bytes 3538952 | tf_op jit(solution)/shard_map/ppermute | solution.py:574
  33.0 26.7 %collective-permute-start.13 = (bf16[2,384,768]{2,1,0:T(8,128)(2,1)}, bf16[2,384,768]{2,1,0:T(8,128)(2,1)}, u32[]{:S(2)}, u32[]{:S(2)}) collective-permute-start(bf16[2,384,768]{2,1,0:T(8,128)(2,1)} %get-tuple-element.32.refs_6_), channel_id=1, source_target_pairs={{8,16},{16,8},{9,17},{17,9},{10,18},{18,10},{11,19},{19,11},{12,20... | collective-permute-start | bytes 3538952 | tf_op jit(solution)/shard_map/ppermute | solution.py:573
  39.8 18.8 %collective-permute-start.10 = (bf16[128,2944]{1,0:T(8,128)(2,1)}, bf16[128,2944]{1,0:T(8,128)(2,1)S(1)}, u32[]{:S(2)}, u32[]{:S(2)}) collective-permute-start(bf16[128,2944]{1,0:T(8,128)(2,1)} %side_by_side.1.refs_10_.refs_2_.refs_0_), channel_id=1, source_target_pairs={{0,2},{1,3},{2,0},{3,1},{4,6},{5,7},{6,4},{7,5},{8,10},{9,11},{10,... | collective-permute-start | bytes 2261000 | tf_op jit(solution)/shard_map/ppermute | solution.py:96
  41.3 18.5 %collective-permute-start.11 = (bf16[128,2944]{1,0:T(8,128)(2,1)}, bf16[128,2944]{1,0:T(8,128)(2,1)S(1)}, u32[]{:S(2)}, u32[]{:S(2)}) collective-permute-start(bf16[128,2944]{1,0:T(8,128)(2,1)} %side_by_side.1.refs_10_.refs_2_.refs_0_), channel_id=1, source_target_pairs={{0,4},{1,5},{2,6},{3,7},{4,0},{5,1},{6,2},{7,3},{8,12},{9,13},{10,... | collective-permute-start | bytes 2261000 | tf_op jit(solution)/shard_map/ppermute | solution.py:96
  64.3 27.3 %collective-permute-start.14 = (bf16[3,128,2944]{2,1,0:T(8,128)(2,1)}, bf16[3,128,2944]{2,1,0:T(8,128)(2,1)}, u32[]{:S(2)}, u32[]{:S(2)}) collective-permute-start(bf16[3,128,2944]{2,1,0:T(8,128)(2,1)} %get-tuple-element.38), channel_id=1, source_target_pairs={{0,1},{1,0},{2,3},{3,2},{4,5},{5,4},{6,7},{7,6},{8,9},{9,8},{10,11... | collective-permute-start | bytes 6782984 | tf_op jit(solution)/shard_map/ppermute | solution.py:96
  64.3 39.3 %collective-permute-start.19 = (bf16[2,384,768]{2,1,0:T(8,128)(2,1)}, bf16[2,384,768]{2,1,0:T(8,128)(2,1)}, u32[]{:S(2)}, u32[]{:S(2)}) collective-permute-start(bf16[2,384,768]{2,1,0:T(8,128)(2,1)} %copy-done.24), channel_id=1, source_target_pairs={{8,16},{16,8},{9,17},{17,9},{10,18},{18,10},{11,19},{19,11},{12,20... | collective-permute-start | bytes 3538952 | tf_op jit(solution)/shard_map/ppermute | solution.py:595
  66.2 44.3 %collective-permute-start.23 = (bf16[2,384,768]{2,1,0:T(8,128)(2,1)}, bf16[2,384,768]{2,1,0:T(8,128)(2,1)}, u32[]{:S(2)}, u32[]{:S(2)}) collective-permute-start(bf16[2,384,768]{2,1,0:T(8,128)(2,1)} %get-tuple-element.53), channel_id=1, source_target_pairs={{0,8},{24,16},{1,9},{25,17},{2,10},{26,18},{3,11},{27,19},{4,12},{... | collective-permute-start | bytes 3538952 | tf_op jit(solution)/shard_map/ppermute | solution.py:594
  72.5 14.5 %collective-permute-start.15 = (bf16[64,2944]{1,0:T(8,128)(2,1)}, bf16[64,2944]{1,0:T(8,128)(2,1)S(1)}, u32[]{:S(2)}, u32[]{:S(2)}) collective-permute-start(bf16[64,2944]{1,0:T(8,128)(2,1)} %get-tuple-element.39.__1_), channel_id=1, source_target_pairs={{0,4},{1,5},{2,6},{3,7},{4,0},{5,1},{6,2},{7,3},{8,12},{9,13},{10,... | collective-permute-start | bytes 1130504 | tf_op jit(solution)/shard_map/ppermute | solution.py:96
  73.5 13.5 %collective-permute-start.16 = (bf16[64,2944]{1,0:T(8,128)(2,1)}, bf16[64,2944]{1,0:T(8,128)(2,1)S(1)}, u32[]{:S(2)}, u32[]{:S(2)}) collective-permute-start(bf16[64,2944]{1,0:T(8,128)(2,1)} %get-tuple-element.40.__2_), channel_id=1, source_target_pairs={{0,2},{1,3},{2,0},{3,1},{4,6},{5,7},{6,4},{7,5},{8,10},{9,11},{10,... | collective-permute-start | bytes 1130504 | tf_op jit(solution)/shard_map/ppermute | solution.py:96
  89.8 43.0 %collective-permute-start.22 = (bf16[2,384,768]{2,1,0:T(8,128)(2,1)}, bf16[2,384,768]{2,1,0:T(8,128)(2,1)}, u32[]{:S(2)}, u32[]{:S(2)}) collective-permute-start(bf16[2,384,768]{2,1,0:T(8,128)(2,1)} %get-tuple-element.53), channel_id=1, source_target_pairs={{8,16},{16,8},{9,17},{17,9},{10,18},{18,10},{11,19},{19,11},{12,20... | collective-permute-start | bytes 3538952 | tf_op jit(solution)/shard_map/ppermute | solution.py:593
  109.2 31.8 %collective-permute-start.20 = (bf16[512,768]{1,0:T(8,128)(2,1)}, bf16[512,768]{1,0:T(8,128)(2,1)}, u32[]{:S(2)}, u32[]{:S(2)}) collective-permute-start(bf16[512,768]{1,0:T(8,128)(2,1)} %get-tuple-element.48), channel_id=1, source_target_pairs={{8,0},{16,24},{9,1},{17,25},{10,2},{18,26},{11,3},{19,27},{12,4},{... | collective-permute-start | bytes 2359304 | tf_op jit(solution)/shard_map/ppermute | solution.py:629
  112.9 28.1 %collective-permute-start.24 = (bf16[1,384,768]{2,1,0:T(8,128)(2,1)}, bf16[1,384,768]{2,1,0:T(8,128)(2,1)}, u32[]{:S(2)}, u32[]{:S(2)}) collective-permute-start(bf16[1,384,768]{2,1,0:T(8,128)(2,1)} %get-tuple-element.62), channel_id=1, source_target_pairs={{8,16},{16,8},{9,17},{17,9},{10,18},{18,10},{11,19},{19,11},{12,20... | collective-permute-start | bytes 1769480 | tf_op jit(solution)/shard_map/ppermute | solution.py:597
  114.4 39.2 %collective-permute-start.26 = (bf16[1,384,768]{2,1,0:T(8,128)(2,1)}, bf16[1,384,768]{2,1,0:T(8,128)(2,1)S(1)}, u32[]{:S(2)}, u32[]{:S(2)}) collective-permute-start(bf16[1,384,768]{2,1,0:T(8,128)(2,1)} %get-tuple-element.63), channel_id=1, source_target_pairs={{8,16},{16,8},{9,17},{17,9},{10,18},{18,10},{11,19},{19,11},{12,20... | collective-permute-start | bytes 1769480 | tf_op jit(solution)/shard_map/ppermute | solution.py:597
  121.6 51.1 %collective-permute-start.21 = (bf16[512,768]{1,0:T(8,128)(2,1)}, bf16[512,768]{1,0:T(8,128)(2,1)}, u32[]{:S(2)}, u32[]{:S(2)}) collective-permute-start(bf16[512,768]{1,0:T(8,128)(2,1)} %get-tuple-element.51), channel_id=1, source_target_pairs={{8,0},{16,24},{9,1},{17,25},{10,2},{18,26},{11,3},{19,27},{12,4},{... | collective-permute-start | bytes 2359304 | tf_op jit(solution)/shard_map/ppermute | solution.py:629
  132.8 17.1 %collective-permute-start.27 = (f32[32,256]{1,0:T(8,128)S(1)}, f32[32,256]{1,0:T(8,128)S(1)}, u32[]{:S(2)}, u32[]{:S(2)}) collective-permute-start(f32[32,256]{1,0:T(8,128)S(1)} %reduce_sum.29.refs_0_), channel_id=1, source_target_pairs={{0,8},{8,0},{16,24},{24,16},{1,9},{9,1},{17,25},{25,17},{2,10},{10... | collective-permute-start | bytes 98312 | tf_op jit(solution)/shard_map/ppermute | solution.py:640
  141.0 12.5 %collective-permute-start.28 = (f32[32,256]{1,0:T(8,128)S(1)}, f32[32,256]{1,0:T(8,128)S(1)}, u32[]{:S(2)}, u32[]{:S(2)}) collective-permute-start(f32[32,256]{1,0:T(8,128)S(1)} %reduce_sum.29.refs_0_), channel_id=1, source_target_pairs={{0,16},{8,24},{16,0},{24,8},{1,17},{9,25},{17,1},{25,9},{2,18},{10... | collective-permute-start | bytes 98312 | tf_op jit(solution)/shard_map/ppermute | solution.py:640
  141.0 12.5 %collective-permute-start.29 = (f32[32,256]{1,0:T(8,128)S(1)}, f32[32,256]{1,0:T(8,128)S(1)}, u32[]{:S(2)}, u32[]{:S(2)}) collective-permute-start(f32[32,256]{1,0:T(8,128)S(1)} %reduce_sum.29.refs_0_), channel_id=1, source_target_pairs={{0,24},{8,16},{16,8},{24,0},{1,25},{9,17},{17,9},{25,1},{2,26},{10... | collective-permute-start | bytes 98312 | tf_op jit(solution)/shard_map/ppermute | solution.py:640
  149.9 24.1 %collective-permute-start.25 = (bf16[512,768]{1,0:T(8,128)(2,1)}, bf16[512,768]{1,0:T(8,128)(2,1)S(1)}, u32[]{:S(2)}, u32[]{:S(2)}) collective-permute-start(bf16[512,768]{1,0:T(8,128)(2,1)} %get-tuple-element.55), channel_id=1, source_target_pairs={{8,0},{16,24},{9,1},{17,25},{10,2},{18,26},{11,3},{19,27},{12,4},{... | collective-permute-start | bytes 2359304 | tf_op jit(solution)/shard_map/ppermute | solution.py:629
  159.9 27.7 %collective-permute-start.30 = (bf16[512,768]{1,0:T(8,128)(2,1)}, bf16[512,768]{1,0:T(8,128)(2,1)S(1)}, u32[]{:S(2)}, u32[]{:S(2)}) collective-permute-start(bf16[512,768]{1,0:T(8,128)(2,1)} %get-tuple-element.58), channel_id=1, source_target_pairs={{8,0},{16,24},{9,1},{17,25},{10,2},{18,26},{11,3},{19,27},{12,4},{... | collective-permute-start | bytes 2359304 | tf_op jit(solution)/shard_map/ppermute | solution.py:629
  (46 other events, 307.0 us)
